TPU v7x, 32 devices: a whole 2x2x4 slice. The times are simulated.
32 devices in a mesh: scan: 2 (over x), tile: 16 (over z, y, core).
Axes of the slice: x: 2, y: 2, z: 4, core: 2. Of those that a mesh axis runs over, the one named last changes fastest.
Arguments:
- slices: float32 [4, 2, 1024, 1024], P(None, None, ('scan', 'tile')), parts along dimension 2, may hold values from -4 to 4
- probe_modes: float32 [4, 2, 128, 128], P('scan'), parts along dimension 0, may hold values from -4 to 4
- row_offset: int32 [128], P(('scan', 'tile')), parts along dimension 0, may hold values from 0 to 31, as said below
- col_offset: int32 [128], P(('scan', 'tile')), parts along dimension 0, may hold values from 0 to 1023
- amplitude: float32 [128, 128, 128], P(('scan', 'tile')), parts along dimension 0, may hold values from 0.5 to 3
Outputs:
- slice_grad: float32 [4, 2, 1024, 1024], P(None, None, ('scan', 'tile')), parts along dimension 2
- probe_grad: float32 [4, 2, 128, 128], P('scan'), parts along dimension 0
There are 2 independent parts, one for each index of `scan`. A program takes and returns all parts, laid end to end along the dimension named above; each array names one. Nothing has to cross between parts.
Inputs may be any that keep to these rules, and one draw needn't show every extreme that they name: Window w starts 32 * (w // 4) + row_offset[w] rows down the object; the largest value is taken by some window in every draw.
All inputs are finite; a program needn't handle non-finite values.
Results may differ from a plain program's by a relative error of at most 0.0003.
Values sent between devices are 32-bit elements; how exact they have to be, the bound alone decides.
No kernel may reach another device: no remote copies, remote signals or barrier semaphores. Data moves between devices by JAX's collectives and lax.ppermute only.
A program may use at most 128 MiB of HBM per device.

v0:
```python
import math

import jax
import jax.numpy as jnp
from jax import lax
from jax.sharding import PartitionSpec as P

INTENSITY_SHIFT = 0.5
FRESNEL = 0.75


def from_behind(value, axis, steps):
    count = lax.axis_size(axis)
    pairs = [(source, (source + steps) % count) for source in range(count)]
    return lax.ppermute(value, axis, pairs)


def dft_tables(window_side):
    steps_idx = jnp.arange(window_side, dtype=jnp.int32)
    product = steps_idx[:, None] * steps_idx[None, :] % window_side
    angles = product.astype(jnp.float32) * (-2.0 * math.pi / window_side)
    scale = 1.0 / math.sqrt(window_side)
    return (jnp.cos(angles) * scale, jnp.sin(angles) * scale)


def fresnel_kernel(window_side):
    steps_idx = jnp.arange(window_side, dtype=jnp.int32)
    freqs = (steps_idx + window_side // 2) % window_side - window_side // 2
    radius = (freqs[:, None] * freqs[:, None] + freqs[None, :] * freqs[None, :]).astype(jnp.float32)
    phase = radius * (-math.pi * FRESNEL / (window_side / 2.0) ** 2)
    return (jnp.cos(phase), jnp.sin(phase))


def left_apply(mat_real, mat_imag, wave_real, wave_imag):

    def product(matrix, field):
        return jnp.einsum("jk,mkl->mjl", matrix, field, precision=lax.Precision.HIGHEST)

    return (
        product(mat_real, wave_real) - product(mat_imag, wave_imag),
        product(mat_real, wave_imag) + product(mat_imag, wave_real),
    )


def right_apply(wave_real, wave_imag, mat_real, mat_imag):

    def product(field, matrix):
        return jnp.einsum("mjk,kl->mjl", field, matrix, precision=lax.Precision.HIGHEST)

    return (
        product(wave_real, mat_real) - product(wave_imag, mat_imag),
        product(wave_imag, mat_real) + product(wave_real, mat_imag),
    )


def transform(wave_real, wave_imag, mat_real, mat_imag):
    half_real, half_imag = left_apply(mat_real, mat_imag, wave_real, wave_imag)
    return right_apply(half_real, half_imag, mat_real, mat_imag)


def propagate(wave_real, wave_imag, tables):
    cos_table, sin_table, kernel_real, kernel_imag = tables
    spec_real, spec_imag = transform(wave_real, wave_imag, cos_table, sin_table)
    moved_real = spec_real * kernel_real - spec_imag * kernel_imag
    moved_imag = spec_real * kernel_imag + spec_imag * kernel_real
    return transform(moved_real, moved_imag, cos_table, -sin_table)


def window_loss(crops, probe_modes, measured, tables):
    cos_table, sin_table = (tables[0], tables[1])
    wave_real = probe_modes[:, 0]
    wave_imag = probe_modes[:, 1]
    slice_count = crops.shape[0]
    exit_real = wave_real
    exit_imag = wave_imag
    for depth_index in range(slice_count):
        trans_real = crops[depth_index, 0]
        trans_imag = crops[depth_index, 1]
        exit_real = trans_real * wave_real - trans_imag * wave_imag
        exit_imag = trans_real * wave_imag + trans_imag * wave_real
        if depth_index + 1 < slice_count:
            wave_real, wave_imag = propagate(exit_real, exit_imag, tables)
    far_real, far_imag = transform(exit_real, exit_imag, cos_table, sin_table)
    intensity = jnp.sum(far_real * far_real + far_imag * far_imag, axis=0)
    modelled = jnp.sqrt(intensity + INTENSITY_SHIFT)
    return 0.5 * jnp.sum((modelled - measured) ** 2)


def window_grads(crops, probe_modes, measured, tables):
    return jax.grad(window_loss, argnums=(0, 1))(crops, probe_modes, measured, tables)


def on_device(slices, probe_modes, row_offset, col_offset, amplitude):
    window_side = probe_modes.shape[-1]
    slice_count = slices.shape[0]
    rows_here = slices.shape[2]
    cols_here = slices.shape[3]
    upper_count = (window_side - 2) // rows_here + 1
    cos_table, sin_table = dft_tables(window_side)
    kernel_real, kernel_imag = fresnel_kernel(window_side)
    tables = (cos_table, sin_table, kernel_real, kernel_imag)
    pieces = [slices]
    moving = slices
    for offset in range(upper_count):
        moving = from_behind(moving, "tile", -1)
        pieces.append(moving)
    extended = jnp.concatenate(pieces, axis=2)[:, :, : rows_here + window_side - 1]
    extended = jnp.concatenate([extended, extended[:, :, :, : window_side - 1]], axis=3)
    anchor = jnp.zeros((), jnp.int32)
    crop_shape = (slice_count, 2, window_side, window_side)

    def one_window(row_start, col_start, measured):
        corner = (anchor, anchor, row_start, col_start)
        crops = lax.dynamic_slice(extended, corner, crop_shape)
        return window_grads(crops, probe_modes, measured, tables)

    crop_grads, probe_terms = jax.vmap(one_window)(row_offset, col_offset, amplitude)

    def add_window(window_index, gradient_buffer):
        corner = (anchor, anchor, row_offset[window_index], col_offset[window_index])
        current = lax.dynamic_slice(gradient_buffer, corner, crop_shape)
        return lax.dynamic_update_slice(gradient_buffer, current + crop_grads[window_index], corner)

    gradient_buffer = lax.fori_loop(
        0, row_offset.shape[0], add_window, jnp.zeros(extended.shape, jnp.float32)
    )
    folded = (
        gradient_buffer[:, :, :, :cols_here]
        .at[:, :, :, : window_side - 1]
        .add(gradient_buffer[:, :, :, cols_here:])
    )
    pad_rows = (upper_count + 1) * rows_here - folded.shape[2]
    padded = jnp.pad(folded, ((0, 0), (0, 0), (0, pad_rows), (0, 0)))
    shares = [
        padded[:, :, offset * rows_here : (offset + 1) * rows_here]
        for offset in range(upper_count + 1)
    ]
    own_grad = shares[0]
    for offset in range(1, upper_count + 1):
        own_grad = own_grad + from_behind(shares[offset], "tile", offset)
    probe_grad = lax.psum(jnp.sum(probe_terms, axis=0), "tile")
    return (own_grad, probe_grad)


def solution(mesh):
    placed = (
        P(None, None, ("scan", "tile"), None),
        P("scan", None, None, None),
        P(("scan", "tile")),
        P(("scan", "tile")),
        P(("scan", "tile"), None, None),
    )
    return jax.shard_map(
        on_device,
        mesh=mesh,
        in_specs=placed,
        out_specs=(P(None, None, ("scan", "tile"), None), P("scan", None, None, None)),
        check_vma=False,
    )
```

profile of v0, /device:TPU:1, one launch (start us, length us, event | category | flops | bytes accessed | tf_op | source)
XLA Modules:
  0.0 444.0 jit_solution(3375297501975912838)
XLA Ops:
  7.3 15.3 %collective-permute-done = f32[4,2,32,1024]{3,2,1,0:T(8,128)S(1)} collective-permute-done((f32[4,2,32,1024]{3,2,1,0:T(8,128)}, f32[4,2,32,1024]{3,2,1,0:T(8,128)S(1)}, u32[]{:S(2)}, u32[]{:S(2)}) %collective-permute-start) | collective-permute-done | bytes 1048608 | tf_op jit(solution)/shard_map/ppermute | solution.py:15
  22.6 2.8 collective-permute-start.1
  25.4 11.4 %collective-permute-done.1 = f32[4,2,32,1024]{3,2,1,0:T(8,128)S(1)} collective-permute-done((f32[4,2,32,1024]{3,2,1,0:T(8,128)S(1)}, f32[4,2,32,1024]{3,2,1,0:T(8,128)S(1)}, u32[]{:S(2)}, u32[]{:S(2)}) %collective-permute-start.1) | collective-permute-done | bytes 1048608 | tf_op jit(solution)/shard_map/ppermute | solution.py:15
  36.8 5.4 %collective-permute-start.2 = (f32[4,2,32,1024]{3,2,1,0:T(8,128)S(1)}, f32[4,2,32,1024]{3,2,1,0:T(8,128)S(1)}, u32[]{:S(2)}, u32[]{:S(2)}) collective-permute-start(f32[4,2,32,1024]{3,2,1,0:T(8,128)S(1)} %collective-permute-done.1), channel_id=1, source_target_pairs={{0,15},{1,0},{2,1},{3,2},{4,3},{5,4},{6,5},{7,6},{8,7},{9,8},{10,9... | collective-permute-start | bytes 3145736 | tf_op jit(solution)/shard_map/ppermute | solution.py:15
  44.5 6.5 %collective-permute-done.2 = f32[4,2,32,1024]{3,2,1,0:T(8,128)S(1)} collective-permute-done((f32[4,2,32,1024]{3,2,1,0:T(8,128)S(1)}, f32[4,2,32,1024]{3,2,1,0:T(8,128)S(1)}, u32[]{:S(2)}, u32[]{:S(2)}) %collective-permute-start.2) | collective-permute-done | bytes 1048608 | tf_op jit(solution)/shard_map/ppermute | solution.py:15
  51.0 8.1 %collective-permute-start.3 = (f32[4,2,32,1024]{3,2,1,0:T(8,128)S(1)}, f32[4,2,32,1024]{3,2,1,0:T(8,128)}, u32[]{:S(2)}, u32[]{:S(2)}) collective-permute-start(f32[4,2,32,1024]{3,2,1,0:T(8,128)S(1)} %collective-permute-done.2), channel_id=1, source_target_pairs={{0,15},{1,0},{2,1},{3,2},{4,3},{5,4},{6,5},{7,6},{8,7},{9,8},{10,9... | collective-permute-start | bytes 3145736 | tf_op jit(solution)/shard_map/ppermute | solution.py:15
  66.8 3.2 pad_maximum_fusion
  69.9 17.6 %while.16 = (s32[]{:T(128)}, f32[4,2,159,1151]{3,2,1,0:T(8,128)}, s32[4,4]{1,0:T(4,128)S(1)}, f32[4,4,2,128,128]{4,3,2,1,0:T(8,128)}, s32[]{:T(128)}) while((s32[]{:T(128)}, f32[4,2,159,1151]{3,2,1,0:T(8,128)}, s32[4,4]{1,0:T(4,128)S(1)}, f32[4,4,2,128,128]{4,3,2,1,0:T(8,128)}, s32[]{:T(128)}) %tuple.92), condition=%wide.while_cond.1, body=%wide.while_body.1.sunk | while | flops 2 | bytes 1050225 | solution.py:114
  70.6 3.6 bitcast_dynamic-update-slice_fusion.2
  74.9 3.6 bitcast_dynamic-update-slice_fusion.2
  79.2 3.6 bitcast_dynamic-update-slice_fusion.2
  83.5 3.6 bitcast_dynamic-update-slice_fusion.2
  215.4 3.0 broadcast_in_dim.12
  218.4 54.9 %while.15 = (s32[]{:T(128)}, f32[4,2,159,1151]{3,2,1,0:T(8,128)}, s32[4]{0:T(128)S(1)}, s32[4]{0:T(128)S(1)}, f32[4,4,2,128,128]{4,3,0,2,1:T(8,128)S(1)}, /*index=5*/s32[]{:T(128)}, s32[]{:T(128)}, s32[]{:T(128)}, s32[]{:T(128)}) while((s32[]{:T(128)}, f32[4,2,159,1151]{3,2,1,0:T(8,128)}, s32[4]{0:T(128)S(1)}, s32[4]{0:T(128)S(1)}, ...), condition=%wide.region_18.19_spmd, body=%wide.region_17.18_spmd.sunk | while | flops 131080 | bytes 2621641 | solution.py:124
  224.9 7.3 %dynamic_update_slice.8 = f32[4,2,159,1151]{3,2,1,0:T(8,128)} dynamic-update-slice(f32[4,2,159,1151]{3,2,1,0:T(8,128)} %get-tuple-element.289, f32[4,2,128,128]{3,2,1,0:T(8,128)S(1)} %bitcast_add_fusion.2, s32[]{:T(128)} %constant.98.clone.1..sunk, s32[]{:T(128)} %constant.98.clone.1..sunk, s32[]{:T(128)S(6)} %select_n.692, s32[]{:T(128)S(6)} %select_n.693) | dynamic-update-slice | bytes 1048580 | tf_op jit(solution)/shard_map/while/body/eval_jaxpr/dynamic_update_slice | solution.py:122
  238.8 7.0 %dynamic_update_slice.8 = f32[4,2,159,1151]{3,2,1,0:T(8,128)} dynamic-update-slice(f32[4,2,159,1151]{3,2,1,0:T(8,128)} %get-tuple-element.289, f32[4,2,128,128]{3,2,1,0:T(8,128)S(1)} %bitcast_add_fusion.2, s32[]{:T(128)} %constant.98.clone.1..sunk, s32[]{:T(128)} %constant.98.clone.1..sunk, s32[]{:T(128)S(6)} %select_n.692, s32[]{:T(128)S(6)} %select_n.693) | dynamic-update-slice | bytes 1048580 | tf_op jit(solution)/shard_map/while/body/eval_jaxpr/dynamic_update_slice | solution.py:122
  252.4 7.2 %dynamic_update_slice.8 = f32[4,2,159,1151]{3,2,1,0:T(8,128)} dynamic-update-slice(f32[4,2,159,1151]{3,2,1,0:T(8,128)} %get-tuple-element.289, f32[4,2,128,128]{3,2,1,0:T(8,128)S(1)} %bitcast_add_fusion.2, s32[]{:T(128)} %constant.98.clone.1..sunk, s32[]{:T(128)} %constant.98.clone.1..sunk, s32[]{:T(128)S(6)} %select_n.692, s32[]{:T(128)S(6)} %select_n.693) | dynamic-update-slice | bytes 1048580 | tf_op jit(solution)/shard_map/while/body/eval_jaxpr/dynamic_update_slice | solution.py:122
  266.1 7.2 %dynamic_update_slice.8 = f32[4,2,159,1151]{3,2,1,0:T(8,128)} dynamic-update-slice(f32[4,2,159,1151]{3,2,1,0:T(8,128)} %get-tuple-element.289, f32[4,2,128,128]{3,2,1,0:T(8,128)S(1)} %bitcast_add_fusion.2, s32[]{:T(128)} %constant.98.clone.1..sunk, s32[]{:T(128)} %constant.98.clone.1..sunk, s32[]{:T(128)S(6)} %select_n.692, s32[]{:T(128)S(6)} %select_n.693) | dynamic-update-slice | bytes 1048580 | tf_op jit(solution)/shard_map/while/body/eval_jaxpr/dynamic_update_slice | solution.py:122
  273.3 5.7 %slice.104 = f32[4,2,159,1024]{3,2,1,0:T(8,128)} slice(f32[4,2,159,1151]{3,2,1,0:T(8,128)} %get-tuple-element.108), slice={[0:4], [0:2], [0:159], [0:1024]} | slice | bytes 10420224 | tf_op jit(solution)/shard_map/slice | solution.py:128
  280.4 3.7 scatter-add.4
  284.1 4.1 fusion.846
  288.2 4.5 %collective-permute-start.5 = (f32[4,2,32,1024]{3,2,1,0:T(8,128)}, f32[4,2,32,1024]{3,2,1,0:T(8,128)}, u32[]{:S(2)}, u32[]{:S(2)}) collective-permute-start(f32[4,2,32,1024]{3,2,1,0:T(8,128)} %get-tuple-element.172), channel_id=1, source_target_pairs={{0,2},{1,3},{2,4},{3,5},{4,6},{5,7},{6,8},{7,9},{8,10},{9,11},{10,... | collective-permute-start | bytes 3145736 | tf_op jit(solution)/shard_map/ppermute | solution.py:15
  297.1 134.0 %all-reduce.13.cloned.1.call-done = f32[2,2,128,128]{2,3,0,1:T(8,128)} async-done(((f32[2,2,128,128]{2,3,0,1:T(8,128)}), f32[2,2,128,128]{2,3,0,1:T(8,128)}) %all-reduce.13.cloned.1.call-update) | async-done | bytes 262160 | tf_op jit(solution)/shard_map/psum | solution.py:141
  432.9 4.1 fusion.44
  (198 shorter events, 157.8 us)
Async XLA Ops:
  7.2 423.9 %all-reduce.13.cloned.1.call-start = ((), (), s32[]{:S(2)}) async-start(), calls=%async_computation | async-start | bytes 524288 | tf_op jit(solution)/shard_map/psum | solution.py:141
  7.2 15.4 %collective-permute-start = (f32[4,2,32,1024]{3,2,1,0:T(8,128)}, f32[4,2,32,1024]{3,2,1,0:T(8,128)S(1)}, u32[]{:S(2)}, u32[]{:S(2)}) collective-permute-start(f32[4,2,32,1024]{3,2,1,0:T(8,128)} %param.9), channel_id=1, source_target_pairs={{0,15},{1,0},{2,1},{3,2},{4,3},{5,4},{6,5},{7,6},{8,7},{9,8},{10,9... | collective-permute-start | bytes 3145736 | tf_op jit(solution)/shard_map/ppermute | solution.py:15
  22.6 14.2 %collective-permute-start.1 = (f32[4,2,32,1024]{3,2,1,0:T(8,128)S(1)}, f32[4,2,32,1024]{3,2,1,0:T(8,128)S(1)}, u32[]{:S(2)}, u32[]{:S(2)}) collective-permute-start(f32[4,2,32,1024]{3,2,1,0:T(8,128)S(1)} %collective-permute-done), channel_id=1, source_target_pairs={{0,15},{1,0},{2,1},{3,2},{4,3},{5,4},{6,5},{7,6},{8,7},{9,8},{10,9... | collective-permute-start | bytes 3145736 | tf_op jit(solution)/shard_map/ppermute | solution.py:15
  36.8 14.2 %collective-permute-start.2 = (f32[4,2,32,1024]{3,2,1,0:T(8,128)S(1)}, f32[4,2,32,1024]{3,2,1,0:T(8,128)S(1)}, u32[]{:S(2)}, u32[]{:S(2)}) collective-permute-start(f32[4,2,32,1024]{3,2,1,0:T(8,128)S(1)} %collective-permute-done.1), channel_id=1, source_target_pairs={{0,15},{1,0},{2,1},{3,2},{4,3},{5,4},{6,5},{7,6},{8,7},{9,8},{10,9... | collective-permute-start | bytes 3145736 | tf_op jit(solution)/shard_map/ppermute | solution.py:15
  51.0 14.3 %collective-permute-start.3 = (f32[4,2,32,1024]{3,2,1,0:T(8,128)S(1)}, f32[4,2,32,1024]{3,2,1,0:T(8,128)}, u32[]{:S(2)}, u32[]{:S(2)}) collective-permute-start(f32[4,2,32,1024]{3,2,1,0:T(8,128)S(1)} %collective-permute-done.2), channel_id=1, source_target_pairs={{0,15},{1,0},{2,1},{3,2},{4,3},{5,4},{6,5},{7,6},{8,7},{9,8},{10,9... | collective-permute-start | bytes 3145736 | tf_op jit(solution)/shard_map/ppermute | solution.py:15
  147.7 7.2 %copy-start.7 = (f32[4,128,128]{2,1,0:T(8,128)S(1)}, f32[4,128,128]{2,1,0:T(8,128)}, u32[]{:S(2)}) copy-start(f32[4,128,128]{2,1,0:T(8,128)} %param.13) | copy-start | bytes 786436
  208.4 4.7 %copy-start.1 = (f32[4,128,128]{2,1,0:T(8,128)S(1)}, f32[4,128,128]{2,1,0:T(8,128)}, u32[]{:S(2)}) copy-start(f32[4,128,128]{2,1,0:T(8,128)} %get-tuple-element.139) | copy-start | bytes 786436
  208.4 4.7 %copy-start.2 = (f32[4,128,128]{2,1,0:T(8,128)S(1)}, f32[4,128,128]{2,1,0:T(8,128)}, u32[]{:S(2)}) copy-start(f32[4,128,128]{2,1,0:T(8,128)} %get-tuple-element.140) | copy-start | bytes 786436
  208.4 4.7 %copy-start.3 = (f32[4,128,128]{2,1,0:T(8,128)S(1)}, f32[4,128,128]{2,1,0:T(8,128)}, u32[]{:S(2)}) copy-start(f32[4,128,128]{2,1,0:T(8,128)} %get-tuple-element.141) | copy-start | bytes 786436
  209.2 4.9 %copy-start.4 = (f32[4,128,128]{2,1,0:T(8,128)S(1)}, f32[4,128,128]{2,1,0:T(8,128)}, u32[]{:S(2)}) copy-start(f32[4,128,128]{2,1,0:T(8,128)} %copy.339) | copy-start | bytes 786436
  210.1 4.0 copy-start.5
  210.9 3.2 copy-start.6
  215.1 3.2 copy-start.8
  215.2 3.2 copy-start.9
  284.1 12.1 %copy-start = (f32[4,2,1,128,128]{3,4,1,0,2:T(8,128)S(1)}, f32[4,2,1,128,128]{3,4,1,0,2:T(8,128)}, u32[]{:S(2)}) copy-start(f32[4,2,1,128,128]{3,4,1,0,2:T(8,128)} %get-tuple-element.182) | copy-start | bytes 1572868
  288.2 144.7 %collective-permute-start.4 = (f32[4,2,32,1024]{3,2,1,0:T(8,128)}, f32[4,2,32,1024]{3,2,1,0:T(8,128)}, u32[]{:S(2)}, u32[]{:S(2)}) collective-permute-start(f32[4,2,32,1024]{3,2,1,0:T(8,128)} %get-tuple-element.169), channel_id=1, source_target_pairs={{0,1},{1,2},{2,3},{3,4},{4,5},{5,6},{6,7},{7,8},{8,9},{9,10},{10,1... | collective-permute-start | bytes 3145736 | tf_op jit(solution)/shard_map/ppermute | solution.py:15
  288.2 144.7 %collective-permute-start.5 = (f32[4,2,32,1024]{3,2,1,0:T(8,128)}, f32[4,2,32,1024]{3,2,1,0:T(8,128)}, u32[]{:S(2)}, u32[]{:S(2)}) collective-permute-start(f32[4,2,32,1024]{3,2,1,0:T(8,128)} %get-tuple-element.172), channel_id=1, source_target_pairs={{0,2},{1,3},{2,4},{3,5},{4,6},{5,7},{6,8},{7,9},{8,10},{9,11},{10,... | collective-permute-start | bytes 3145736 | tf_op jit(solution)/shard_map/ppermute | solution.py:15
  292.7 140.2 %collective-permute-start.6 = (f32[4,2,32,1024]{3,2,1,0:T(8,128)S(1)}, f32[4,2,32,1024]{3,2,1,0:T(8,128)}, u32[]{:S(2)}, u32[]{:S(2)}) collective-permute-start(f32[4,2,32,1024]{3,2,1,0:T(8,128)S(1)} %get-tuple-element.171), channel_id=1, source_target_pairs={{0,3},{1,4},{2,5},{3,6},{4,7},{5,8},{6,9},{7,10},{8,11},{9,12},{10... | collective-permute-start | bytes 3145736 | tf_op jit(solution)/shard_map/ppermute | solution.py:15
  294.6 138.3 %collective-permute-start.7 = (f32[4,2,32,1024]{3,2,1,0:T(8,128)S(1)}, f32[4,2,32,1024]{3,2,1,0:T(8,128)}, u32[]{:S(2)}, u32[]{:S(2)}) collective-permute-start(f32[4,2,32,1024]{3,2,1,0:T(8,128)S(1)} %get-tuple-element.170), channel_id=1, source_target_pairs={{0,4},{1,5},{2,6},{3,7},{4,8},{5,9},{6,10},{7,11},{8,12},{9,13},{1... | collective-permute-start | bytes 3145736 | tf_op jit(solution)/shard_map/ppermute | solution.py:15
Sparse Core Ops, SparseCore 0:
  297.2 133.8 all-reduce.12
where the time goes:
time: 449 us; the launch traced here: 444 us
  waiting for transfers between devices  170 us (38%)
  matrix products  118 us (26%)
  local copies, waits for them, and re-layouts  78.9 us (18%)
  starting transfers between devices  24.5 us (5%)
  other arithmetic  21.3 us (5%)
  loops' own time  16 us (4%)
  between operations  15.2 us (3%)
    psum x1, waiting for transfers between devices, on_device(): probe_grad = lax.psum(jnp.sum(probe_terms, axis=0), 'tile')  134 us
    dot_general x56, matrix products, product(): jnp.einsum('jk,mkl->mjl', matrix, field, precision=lax.Precision.HIGHEST)  62.3 us
    dot_general x56, matrix products, product(): jnp.einsum('mjk,kl->mjl', field, matrix, precision=lax.Precision.HIGHEST)  55.7 us
    ppermute x8, waiting for transfers between devices, from_behind(): return lax.ppermute(value, axis, pairs)  35.9 us
    dynamic_update_slice x4, local copies, waits for them, and re-layouts, add_window(): lax.dynamic_update_slice(gradient_buffer, current + crop_grads[window_ind...  28.7 us
    ppermute x8, starting transfers between devices, from_behind(): return lax.ppermute(value, axis, pairs)  24.5 us
    gather x12, local copies, waits for them, and re-layouts  17.1 us
    another operation x1, loops' own time, on_device(): lax.fori_loop(0, row_offset.shape[0], add_window, jnp.zeros(extended.shap...  15.6 us
  transfers between devices with their start and end apart: 9, of which 5 were waited for; matrix products, arithmetic and copies ran while one was open for 2% of the time, Pallas kernels for 0%

commit v1 on v0

v1 whole, which is shorter than its diff:
```python
import functools
import math

import numpy as np
import ml_dtypes
import jax
import jax.numpy as jnp
from jax import lax
from jax.experimental import pallas as pl
from jax.experimental.pallas import tpu as pltpu
from jax.sharding import PartitionSpec as P

INTENSITY_SHIFT = 0.5
FRESNEL = 0.75
LANES = 128
VMEM_BYTES = 56 * 1024 * 1024


def pairs(value):
    first = value.astype(ml_dtypes.bfloat16)
    second = (value - first.astype(np.float64)).astype(ml_dtypes.bfloat16)
    return np.stack([first, second])


def real_form(matrix):
    return np.block([[matrix.real, matrix.imag], [-matrix.imag, matrix.real]])


def tables_of(window_side):
    steps = np.arange(window_side)
    angles = -2.0 * math.pi / window_side * (steps[:, None] * steps[None, :] % window_side)
    transform = np.exp(1j * angles) / math.sqrt(window_side)
    freqs = (steps + window_side // 2) % window_side - window_side // 2
    phase = np.exp(-1j * math.pi * FRESNEL * freqs**2 / (window_side / 2.0) ** 2)
    step = transform.conj() @ (phase[:, None] * transform)
    forms = [real_form(m) for m in (step, step.conj(), transform, transform.conj())]
    return np.stack([pairs(form) for form in forms])


def halves(value):
    first = value.astype(jnp.bfloat16)
    return first, (value - first.astype(jnp.float32)).astype(jnp.bfloat16)


def product(left, right):
    return jnp.dot(left, right, preferred_element_type=jnp.float32)


def right_apply(field, table):
    first, second = halves(field)
    return product(first, table[0]) + (product(second, table[0]) + product(first, table[1]))


def left_apply(table, field):
    first, second = halves(field)
    return product(table[0], first) + (product(table[0], second) + product(table[1], first))


def both_sides(waves, right_table, left_table):
    side = waves[0][0].shape[0]
    rows = jnp.concatenate([jnp.concatenate(wave, axis=1) for wave in waves], axis=0)
    half = right_apply(rows, right_table)
    count = len(waves)
    parts = [
        jnp.concatenate(
            [half[m * side : (m + 1) * side, c * side : (c + 1) * side] for m in range(count)], axis=1
        )
        for c in range(2)
    ]
    full = left_apply(left_table, jnp.concatenate(parts, axis=0))
    return [
        tuple(full[c * side : (c + 1) * side, m * side : (m + 1) * side] for c in range(2))
        for m in range(count)
    ]


def times(a, b):
    return (a[0] * b[0] - a[1] * b[1], a[0] * b[1] + a[1] * b[0])


def conj_times(a, b):
    return (a[0] * b[0] + a[1] * b[1], a[0] * b[1] - a[1] * b[0])


def gradient_kernel(group, offset_ref, probe_ref, amplitude_ref, table_ref, *refs):
    count = len(refs) // 2
    pieces, grads, probe_grad_ref = refs[:count], refs[count : 2 * count], refs[2 * count]
    windows, slice_count, _, rows_here, side = pieces[0].shape
    modes = probe_ref.shape[0]
    step, step_conj, transform, transform_conj = (
        (table_ref[i, 0], table_ref[i, 1]) for i in range(4)
    )
    flag = offset_ref[2, 0]
    probe_grad_ref[...] = jnp.zeros(probe_grad_ref.shape, jnp.float32)

    def start(w):
        row, lane = offset_ref[0, w], offset_ref[1, w] % side
        index = lax.broadcasted_iota(jnp.int32, (rows_here, side), 0)
        here = jnp.where(index >= row, 1, 0) != flag
        return row, lane, here

    def crop(w, s, here):
        def plane(c):
            edge = jnp.where(here, pieces[0][w, s, c], pieces[1][w, s, c])
            return jnp.concatenate([edge] + [piece[w, s, c] for piece in pieces[2:]], axis=0)

        return (plane(0), plane(1))

    def keep(w, s, here, grad):
        for c in range(2):
            edge = grad[c][:rows_here]
            zero = jnp.zeros_like(edge)
            grads[0][w, s, c] = jnp.where(here, edge, zero)
            grads[1][w, s, c] = jnp.where(here, zero, edge)
            for j in range(1, count - 1):
                grads[j + 1][w, s, c] = grad[c][j * rows_here : (j + 1) * rows_here]

    def turn(value, row, lane):
        return pltpu.roll(pltpu.roll(value, row, 0), lane, 1)

    def visit(index, carry):
        ids = [index * group + k for k in range(group)]
        places = [start(w) for w in ids]
        waves = [
            [[tuple(turn(probe_ref[m, c], row, lane) for c in range(2)) for m in range(modes)]]
            for row, lane, _ in places
        ]
        crops = [[] for _ in ids]
        exits = [None] * group
        for s in range(slice_count):
            for k, w in enumerate(ids):
                crops[k].append(crop(w, s, places[k][2]))
                exits[k] = [times(crops[k][s], wave) for wave in waves[k][s]]
            for k, w in enumerate(ids):
                if s + 1 < slice_count:
                    waves[k].append(both_sides(exits[k], step, step_conj))
                else:
                    exits[k] = both_sides(exits[k], transform, transform_conj)
        for k, w in enumerate(ids):
            intensity = sum(re * re + im * im for re, im in exits[k])
            scale = 1.0 - amplitude_ref[w] * lax.rsqrt(intensity + INTENSITY_SHIFT)
            exits[k] = [(re * scale, im * scale) for re, im in exits[k]]
        for k, w in enumerate(ids):
            exits[k] = both_sides(exits[k], transform_conj, transform)
        for s in reversed(range(slice_count)):
            for k, w in enumerate(ids):
                terms = [conj_times(wave, out) for wave, out in zip(waves[k][s], exits[k])]
                keep(w, s, places[k][2], [sum(term[c] for term in terms) for c in range(2)])
                exits[k] = [conj_times(crops[k][s], out) for out in exits[k]]
            if s > 0:
                for k, w in enumerate(ids):
                    exits[k] = both_sides(exits[k], step_conj, step)
        for k, (row, lane, _) in enumerate(places):
            for m in range(modes):
                for c in range(2):
                    back = turn(exits[k][m][c], (side - row) % side, (side - lane) % side)
                    probe_grad_ref[m, c] += back
        return carry

    lax.fori_loop(0, windows // group, visit, 0)


def take_kernel(col_ref, slices_ref, *outs):
    blocks = slices_ref.shape[-1] // LANES
    windows = outs[0].shape[0]
    lanes = lax.broadcasted_iota(jnp.int32, (1, 1, 1, LANES), 3)
    for k, out in enumerate(outs):
        for w in range(windows):
            col = col_ref[k, w]
            block, lane = col // LANES, col % LANES
            after = (block + 1) % blocks
            near = slices_ref[:, :, :, pl.ds(pl.multiple_of(block * LANES, LANES), LANES)]
            far = slices_ref[:, :, :, pl.ds(pl.multiple_of(after * LANES, LANES), LANES)]
            out[w] = jnp.where(lanes < lane, far, near)


def give_kernel(col_ref, *refs):
    pieces, out_ref = refs[:-1], refs[-1]
    blocks = out_ref.shape[-1] // LANES
    windows = pieces[0].shape[0]
    lanes = lax.broadcasted_iota(jnp.int32, (1, 1, 1, LANES), 3)
    out_ref[...] = jnp.zeros(out_ref.shape, jnp.float32)
    for k, piece in enumerate(pieces):
        for w in range(windows):
            col = col_ref[k, w]
            block, lane = col // LANES, col % LANES
            after = (block + 1) % blocks
            value = piece[w]
            near = pl.ds(pl.multiple_of(block * LANES, LANES), LANES)
            far = pl.ds(pl.multiple_of(after * LANES, LANES), LANES)
            wraps = lanes < lane
            out_ref[:, :, :, near] += jnp.where(wraps, 0.0, value)
            out_ref[:, :, :, far] += jnp.where(wraps, value, 0.0)


def plan_of(count, reach):
    pair = reach // 2
    if pair == 0 or count % (2 * pair) != 0:
        moved = [0] * count
    else:
        moved = [t // pair % 2 for t in range(count)]
    home = [(t + reach) % count if moved[t] else t for t in range(count)]
    return moved, home


def whole(memory_space=pltpu.VMEM):
    return pl.BlockSpec(memory_space=memory_space)


def call(kernel, outs, args, flops=0):
    smem, vmem = whole(pltpu.SMEM), whole()
    return pl.pallas_call(
        kernel,
        out_shape=outs,
        in_specs=[smem] + [vmem] * (len(args) - 1),
        out_specs=[vmem] * len(outs) if isinstance(outs, list) else vmem,
        compiler_params=pltpu.CompilerParams(vmem_limit_bytes=VMEM_BYTES),
    )(*args)


def all_sum(value, axis):
    count = lax.axis_size(axis)
    if count & (count - 1):
        return lax.psum(value, axis)
    bit = 1
    while bit < count:
        value = value + lax.ppermute(value, axis, [(i, i ^ bit) for i in range(count)])
        bit *= 2
    return value


def on_device(slices, probe_modes, row_offset, col_offset, amplitude):
    side = probe_modes.shape[-1]
    slice_count, _, rows_here, cols = slices.shape
    windows = row_offset.shape[0]
    count = lax.axis_size("tile")
    assert side == LANES and side % rows_here == 0 and cols % LANES == 0
    reach = side // rows_here
    moved, home = plan_of(count, reach)
    me = lax.axis_index("tile")
    is_moved = jnp.asarray(moved, jnp.int32)[me]

    def edge_pairs():
        return [(t, home[t]) if moved[t] else ((t + reach) % count, t) for t in range(count)]

    def inner_pairs(j):
        return [((t + j) % count, home[t]) for t in range(count)]

    def back(pairs_there):
        return [(b, a) for a, b in pairs_there]

    def send(value, pairs_there):
        return lax.ppermute(value, "tile", pairs_there)

    offsets = jnp.stack([row_offset, col_offset])
    behind = [offsets] + [
        send(offsets, [(t, (t + j) % count) for t in range(count)]) for j in range(1, reach + 1)
    ]
    mine = jnp.where(is_moved == 1, behind[reach], offsets)
    other = jnp.where(is_moved == 1, offsets, behind[reach])
    cols_of = jnp.stack([mine[1], other[1]] + [behind[j][1] for j in range(1, reach)])
    rows_of = jnp.concatenate([mine, jnp.full((1, windows), is_moved, jnp.int32)])

    piece = jax.ShapeDtypeStruct((windows, slice_count, 2, rows_here, side), jnp.float32)
    sent = call(take_kernel, [piece] * (reach + 1), (cols_of, slices))
    pieces = [sent[0], send(sent[1], edge_pairs())]
    pieces += [send(sent[j + 1], inner_pairs(j)) for j in range(1, reach)]
    if any(moved):
        amplitude = send(amplitude, list(enumerate(home)))

    tables = jnp.asarray(tables_of(side))
    group = 2 if windows % 2 == 0 else 1
    results = call(
        functools.partial(gradient_kernel, group),
        [piece] * (reach + 1) + [jax.ShapeDtypeStruct(probe_modes.shape, jnp.float32)],
        (rows_of, probe_modes, amplitude, tables, *pieces),
    )
    grads, probe_grad = results[:-1], results[-1]
    received = [grads[0], send(grads[1], back(edge_pairs()))]
    received += [send(grads[j + 1], back(inner_pairs(j))) for j in range(1, reach)]
    own_grad = call(
        give_kernel, jax.ShapeDtypeStruct(slices.shape, jnp.float32), (cols_of, *received)
    )
    return own_grad, all_sum(probe_grad, "tile")


def solution(mesh):
    placed = (
        P(None, None, ("scan", "tile"), None),
        P("scan", None, None, None),
        P(("scan", "tile")),
        P(("scan", "tile")),
        P(("scan", "tile"), None, None),
    )
    return jax.shard_map(
        on_device,
        mesh=mesh,
        in_specs=placed,
        out_specs=(P(None, None, ("scan", "tile"), None), P("scan", None, None, None)),
        check_vma=False,
    )
```

time: 449 us -> 104 us (0.23)
  waiting for transfers between devices: 170 us -> 51.5 us
  matrix products: 118 us -> 0 us
  local copies, waits for them, and re-layouts: 78.9 us -> 5.34 us
  Pallas kernels: 0 us -> 22.6 us
  other arithmetic: 21.3 us -> 1.8 us
  loops' own time: 16 us -> 0 us
  between operations: 15.2 us -> 1.4 us
    psum x1 -> x0, waiting for transfers between devices: 134 us -> none  [on_device(): probe_grad = lax.psum(jnp.sum(probe_terms, axis=0), 'tile')]
    dot_general x112 -> x0, matrix products: 118 us -> none  [the longest x56 62.3 us: product(): jnp.einsum('jk,mkl->mjl', matrix, field, precision=lax.Precision.HIGHEST)]
    dynamic_update_slice x4 -> x0, local copies, waits for them, and re-layouts: 28.7 us -> none  [add_window(): lax.dynamic_update_slice(gradient_buffer, current + crop_grads[window_ind...]
    pallas_call x0 -> x3, Pallas kernels: none -> 22.6 us  [call(): pl.pallas_call(kernel, out_shape=outs, in_specs=[smem] + [vmem] * (len(ar...]
    gather x12 -> x0, local copies, waits for them, and re-layouts: 17.1 us -> none
    another operation x2 -> x0, loops' own time: 16 us -> none  [the longest x1 15.6 us: on_device(): lax.fori_loop(0, row_offset.shape[0], add_window, jnp.zeros(extended.shap...]
    ppermute x8 -> x17, waiting for transfers between devices: 35.9 us -> 51.5 us  [the longest x4 28 us: all_sum(): lax.ppermute(value, axis, [(i, i ^ bit) for i in range(count)])]
    slice x3 -> x5, local copies, waits for them, and re-layouts: 9.88 us -> 0.02 us  [the longest x3 0.01 us: on_device(): behind[j][1]]
  transfers between devices with their start and end apart: 9 -> 17, of which waited for: 5 -> 12; matrix products, arithmetic and copies ran while one was open for 2% -> 2% of each run, Pallas kernels for 0% -> 4%
where the time goes in v1:
time: 104 us; the launch traced here: 103 us
  waiting for transfers between devices  51.5 us (50%)
  Pallas kernels  22.6 us (22%)
  starting transfers between devices  20.6 us (20%)
  local copies, waits for them, and re-layouts  5.34 us (5%)
  other arithmetic  1.8 us (2%)
  between operations  1.4 us (1%)
    ppermute x4, waiting for transfers between devices, all_sum(): lax.ppermute(value, axis, [(i, i ^ bit) for i in range(count)])  28 us
    ppermute x13, waiting for transfers between devices, send(): return lax.ppermute(value, 'tile', pairs_there)  23.5 us
    pallas_call x3, Pallas kernels, call(): pl.pallas_call(kernel, out_shape=outs, in_specs=[smem] + [vmem] * (len(ar...  22.6 us
    ppermute x13, starting transfers between devices, send(): return lax.ppermute(value, 'tile', pairs_there)  16.9 us
    ppermute x4, starting transfers between devices, all_sum(): lax.ppermute(value, axis, [(i, i ^ bit) for i in range(count)])  3.66 us
    unnamed x28, local copies, waits for them, and re-layouts  2.9 us
  transfers between devices with their start and end apart: 17, of which 12 were waited for; matrix products, arithmetic and copies ran while one was open for 2% of the time, Pallas kernels for 4%

profile of v1, /device:TPU:1, one launch (start us, length us, event | category | flops | bytes accessed | tf_op | source)
XLA Modules:
  0.0 103.2 jit_solution(11650486753849522290)
XLA Ops:
  1.3 2.7 %collective-permute-start.1 = (s32[2,4]{1,0:T(2,128)S(1)}, s32[2,4]{1,0:T(2,128)S(1)}, u32[]{:S(2)}, u32[]{:S(2)}) collective-permute-start(s32[2,4]{1,0:T(2,128)S(1)} %pad_add_fusion), channel_id=1, source_target_pairs={{0,1},{1,2},{2,3},{3,4},{4,5},{5,6},{6,7},{7,8},{8,9},{9,10},{10,1... | collective-permute-start | bytes 104 | tf_op jit(solution)/shard_map/ppermute | solution.py:253
  4.1 1.2 %collective-permute-start.2 = (s32[2,4]{1,0:T(2,128)S(1)}, s32[2,4]{1,0:T(2,128)S(1)}, u32[]{:S(2)}, u32[]{:S(2)}) collective-permute-start(s32[2,4]{1,0:T(2,128)S(1)} %pad_add_fusion), channel_id=1, source_target_pairs={{0,2},{1,3},{2,4},{3,5},{4,6},{5,7},{6,8},{7,9},{8,10},{9,11},{10,... | collective-permute-start | bytes 104 | tf_op jit(solution)/shard_map/ppermute | solution.py:253
  5.3 1.3 %collective-permute-start = (s32[2,4]{1,0:T(2,128)S(1)}, s32[2,4]{1,0:T(2,128)S(1)}, u32[]{:S(2)}, u32[]{:S(2)}) collective-permute-start(s32[2,4]{1,0:T(2,128)S(1)} %pad_add_fusion), channel_id=1, source_target_pairs={{0,4},{1,5},{2,6},{3,7},{4,8},{5,9},{6,10},{7,11},{8,12},{9,13},{1... | collective-permute-start | bytes 104 | tf_op jit(solution)/shard_map/ppermute | solution.py:253
  8.5 1.0 collective-permute-done
  10.3 3.4 %shard_map.86 = (f32[4,4,2,32,128]{4,3,2,1,0:T(8,128)}, f32[4,4,2,32,128]{4,3,2,1,0:T(8,128)}, f32[4,4,2,32,128]{4,3,2,1,0:T(8,128)}, f32[4,4,2,32,128]{4,3,2,1,0:T(8,128)}, f32[4,4,2,32,128]{4,3,2,1,0:T(8,128)}) custom-call(s32[5,4]{1,0:T(8,128)} %stack.15.col_ref, f32[4,2,32,1024]{3,2,1,0:T(8,128)} %slices_ref.1), custom_call_target="tpu_custom_call" | custom-call | tf_op jit(solution)/shard_map/pallas_call | solution.py:212
  13.7 1.5 %collective-permute-start.5 = (f32[4,4,2,32,128]{4,3,2,1,0:T(8,128)}, f32[4,4,2,32,128]{4,3,2,1,0:T(8,128)S(1)}, u32[]{:S(2)}, u32[]{:S(2)}) collective-permute-start(f32[4,4,2,32,128]{4,3,2,1,0:T(8,128)} %get-tuple-element.14), channel_id=1, source_target_pairs={{4,0},{5,1},{2,6},{3,7},{8,4},{9,5},{6,10},{7,11},{12,8},{13,9},{1... | collective-permute-start | bytes 1572872 | tf_op jit(solution)/shard_map/ppermute | solution.py:253
  15.3 1.8 %collective-permute-start.6 = (f32[4,4,2,32,128]{4,3,2,1,0:T(8,128)}, f32[4,4,2,32,128]{4,3,2,1,0:T(8,128)S(1)}, u32[]{:S(2)}, u32[]{:S(2)}) collective-permute-start(f32[4,4,2,32,128]{4,3,2,1,0:T(8,128)} %get-tuple-element.15), channel_id=1, source_target_pairs={{1,0},{2,1},{3,6},{4,7},{5,4},{6,5},{7,10},{8,11},{9,8},{10,9},{11... | collective-permute-start | bytes 1572872 | tf_op jit(solution)/shard_map/ppermute | solution.py:253
  17.4 1.3 %collective-permute-start.8 = (f32[4,4,2,32,128]{4,3,2,1,0:T(8,128)}, f32[4,4,2,32,128]{4,3,2,1,0:T(8,128)S(1)}, u32[]{:S(2)}, u32[]{:S(2)}) collective-permute-start(f32[4,4,2,32,128]{4,3,2,1,0:T(8,128)} %get-tuple-element.17), channel_id=1, source_target_pairs={{3,0},{4,1},{5,6},{6,7},{7,4},{8,5},{9,10},{10,11},{11,8},{12,9},{... | collective-permute-start | bytes 1572872 | tf_op jit(solution)/shard_map/ppermute | solution.py:253
  19.4 1.2 %concatenate.3.offset_ref = s32[3,4]{1,0:T(4,128)} pad(s32[2,4]{1,0:T(2,128)S(1)} %get-tuple-element.25, s32[]{:T(128)} %bitcast), padding=0_1x0_0 | pad | bytes 84 | tf_op jit(solution)/shard_map/concatenate | solution.py:262
  20.7 4.6 %collective-permute-done.5.refs_1_ = f32[4,4,2,32,128]{4,3,2,1,0:T(8,128)S(1)} collective-permute-done((f32[4,4,2,32,128]{4,3,2,1,0:T(8,128)}, f32[4,4,2,32,128]{4,3,2,1,0:T(8,128)S(1)}, u32[]{:S(2)}, u32[]{:S(2)}) %collective-permute-start.5) | collective-permute-done | bytes 524320 | tf_op jit(solution)/shard_map/ppermute | solution.py:253
  25.2 4.8 %collective-permute-done.6.refs_2_ = f32[4,4,2,32,128]{4,3,2,1,0:T(8,128)S(1)} collective-permute-done((f32[4,4,2,32,128]{4,3,2,1,0:T(8,128)}, f32[4,4,2,32,128]{4,3,2,1,0:T(8,128)S(1)}, u32[]{:S(2)}, u32[]{:S(2)}) %collective-permute-start.6) | collective-permute-done | bytes 524320 | tf_op jit(solution)/shard_map/ppermute | solution.py:253
  30.1 1.1 %collective-permute-done.7.refs_3_ = f32[4,4,2,32,128]{4,3,2,1,0:T(8,128)S(1)} collective-permute-done((f32[4,4,2,32,128]{4,3,2,1,0:T(8,128)}, f32[4,4,2,32,128]{4,3,2,1,0:T(8,128)S(1)}, u32[]{:S(2)}, u32[]{:S(2)}) %collective-permute-start.7) | collective-permute-done | bytes 524320 | tf_op jit(solution)/shard_map/ppermute | solution.py:253
  31.2 9.4 %collective-permute-done.8.refs_4_ = f32[4,4,2,32,128]{4,3,2,1,0:T(8,128)S(1)} collective-permute-done((f32[4,4,2,32,128]{4,3,2,1,0:T(8,128)}, f32[4,4,2,32,128]{4,3,2,1,0:T(8,128)S(1)}, u32[]{:S(2)}, u32[]{:S(2)}) %collective-permute-start.8) | collective-permute-done | bytes 524320 | tf_op jit(solution)/shard_map/ppermute | solution.py:253
  41.4 15.2 %shard_map.87 = (f32[4,4,2,32,128]{4,3,2,1,0:T(8,128)}, f32[4,4,2,32,128]{4,3,2,1,0:T(8,128)}, f32[4,4,2,32,128]{4,3,2,1,0:T(8,128)}, f32[4,4,2,32,128]{4,3,2,1,...) custom-call(s32[3,4]{1,0:T(4,128)} %concatenate.3.offset_ref, f32[2,2,128,128]{3,2,1,0:T(8,128)} %probe_ref.1, ...), custom_call_target="tpu_custom_call" | custom-call | tf_op jit(solution)/shard_map/pallas_call | solution.py:212
  56.6 1.8 %collective-permute-start.13 = (f32[2,2,128,128]{3,2,1,0:T(8,128)}, f32[2,2,128,128]{3,2,1,0:T(8,128)S(1)}, u32[]{:S(2)}, u32[]{:S(2)}) collective-permute-start(f32[2,2,128,128]{3,2,1,0:T(8,128)} %get-tuple-element.23), channel_id=1, source_target_pairs={{0,1},{1,0},{2,3},{3,2},{4,5},{5,4},{6,7},{7,6},{8,9},{9,8},{10,11... | collective-permute-start | bytes 786440 | tf_op jit(solution)/shard_map/ppermute | solution.py:227
  58.4 1.4 %collective-permute-done.13 = f32[2,2,128,128]{3,2,1,0:T(8,128)S(1)} collective-permute-done((f32[2,2,128,128]{3,2,1,0:T(8,128)}, f32[2,2,128,128]{3,2,1,0:T(8,128)S(1)}, u32[]{:S(2)}, u32[]{:S(2)}) %collective-permute-start.13) | collective-permute-done | bytes 262176 | tf_op jit(solution)/shard_map/ppermute | solution.py:227
  59.8 1.0 add.18
  61.6 1.3 %collective-permute-start.9 = (f32[4,4,2,32,128]{4,3,2,1,0:T(8,128)}, f32[4,4,2,32,128]{4,3,2,1,0:T(8,128)S(1)}, u32[]{:S(2)}, u32[]{:S(2)}) collective-permute-start(f32[4,4,2,32,128]{4,3,2,1,0:T(8,128)} %get-tuple-element.19), channel_id=1, source_target_pairs={{0,4},{1,5},{6,2},{7,3},{4,8},{5,9},{10,6},{11,7},{8,12},{9,13},{1... | collective-permute-start | bytes 1572872 | tf_op jit(solution)/shard_map/ppermute | solution.py:253
  62.8 3.5 %collective-permute-start.10 = (f32[4,4,2,32,128]{4,3,2,1,0:T(8,128)}, f32[4,4,2,32,128]{4,3,2,1,0:T(8,128)S(1)}, u32[]{:S(2)}, u32[]{:S(2)}) collective-permute-start(f32[4,4,2,32,128]{4,3,2,1,0:T(8,128)} %get-tuple-element.20), channel_id=1, source_target_pairs={{0,1},{1,2},{6,3},{7,4},{4,5},{5,6},{10,7},{11,8},{8,9},{9,10},{14... | collective-permute-start | bytes 1572872 | tf_op jit(solution)/shard_map/ppermute | solution.py:253
  66.3 1.2 %collective-permute-start.12 = (f32[4,4,2,32,128]{4,3,2,1,0:T(8,128)S(1)}, f32[4,4,2,32,128]{4,3,2,1,0:T(8,128)S(1)}, u32[]{:S(2)}, u32[]{:S(2)}) collective-permute-start(f32[4,4,2,32,128]{4,3,2,1,0:T(8,128)S(1)} %copy-done.11), channel_id=1, source_target_pairs={{0,3},{1,4},{6,5},{7,6},{4,7},{5,8},{10,9},{11,10},{8,11},{9,12},{... | collective-permute-start | bytes 1572872 | tf_op jit(solution)/shard_map/ppermute | solution.py:253
  69.3 19.3 %collective-permute-done.15 = f32[2,2,128,128]{3,2,1,0:T(8,128)S(1)} collective-permute-done((f32[2,2,128,128]{3,2,1,0:T(8,128)S(1)}, f32[2,2,128,128]{3,2,1,0:T(8,128)S(1)}, u32[]{:S(2)}, u32[]{:S(2)}) %collective-permute-start.15) | collective-permute-done | bytes 262176 | tf_op jit(solution)/shard_map/ppermute | solution.py:227
  88.8 1.7 %collective-permute-done.11.refs_3_ = f32[4,4,2,32,128]{4,3,2,1,0:T(8,128)S(1)} collective-permute-done((f32[4,4,2,32,128]{4,3,2,1,0:T(8,128)}, f32[4,4,2,32,128]{4,3,2,1,0:T(8,128)S(1)}, u32[]{:S(2)}, u32[]{:S(2)}) %collective-permute-start.11) | collective-permute-done | bytes 524320 | tf_op jit(solution)/shard_map/ppermute | solution.py:253
  92.1 3.9 %shard_map.88 = f32[4,2,32,1024]{3,2,1,0:T(8,128)} custom-call(s32[5,4]{1,0:T(8,128)} %stack.15.col_ref, f32[4,4,2,32,128]{4,3,2,1,0:T(8,128)} %get-tuple-element.18.refs_0_, f32[4,4,2,32,128]{4,3,2,1,0:T(8,128)} %copy-done, f32[4,4,2,32,128]{4,3,2,1,0:T(8,128)} %copy-done.1, f32[4,4,2,32,128]{4,3,2,1,0:T(8,128)} %copy-done.2, f32[4,4,2,32,128]{4,3,2,1,0:T(8,128)} %copy-done.3), custom_call_target="tpu_custom_call" | custom-call | tf_op jit(solution)/shard_map/pallas_call | solution.py:212
  96.1 6.4 %collective-permute-done.16 = f32[2,2,128,128]{3,2,1,0:T(8,128)S(1)} collective-permute-done((f32[2,2,128,128]{3,2,1,0:T(8,128)S(1)}, f32[2,2,128,128]{3,2,1,0:T(8,128)S(1)}, u32[]{:S(2)}, u32[]{:S(2)}) %collective-permute-start.16) | collective-permute-done | bytes 262176 | tf_op jit(solution)/shard_map/ppermute | solution.py:227
  (55 shorter events, 9.6 us)
Async XLA Ops:
  1.3 8.3 %collective-permute-start.1 = (s32[2,4]{1,0:T(2,128)S(1)}, s32[2,4]{1,0:T(2,128)S(1)}, u32[]{:S(2)}, u32[]{:S(2)}) collective-permute-start(s32[2,4]{1,0:T(2,128)S(1)} %pad_add_fusion), channel_id=1, source_target_pairs={{0,1},{1,2},{2,3},{3,4},{4,5},{5,6},{6,7},{7,8},{8,9},{9,10},{10,1... | collective-permute-start | bytes 104 | tf_op jit(solution)/shard_map/ppermute | solution.py:253
  4.0 5.7 %collective-permute-start.3 = (s32[2,4]{1,0:T(2,128)S(1)}, s32[2,4]{1,0:T(2,128)S(1)}, u32[]{:S(2)}, u32[]{:S(2)}) collective-permute-start(s32[2,4]{1,0:T(2,128)S(1)} %pad_add_fusion), channel_id=1, source_target_pairs={{0,3},{1,4},{2,5},{3,6},{4,7},{5,8},{6,9},{7,10},{8,11},{9,12},{10... | collective-permute-start | bytes 104 | tf_op jit(solution)/shard_map/ppermute | solution.py:253
  4.1 5.6 %collective-permute-start.2 = (s32[2,4]{1,0:T(2,128)S(1)}, s32[2,4]{1,0:T(2,128)S(1)}, u32[]{:S(2)}, u32[]{:S(2)}) collective-permute-start(s32[2,4]{1,0:T(2,128)S(1)} %pad_add_fusion), channel_id=1, source_target_pairs={{0,2},{1,3},{2,4},{3,5},{4,6},{5,7},{6,8},{7,9},{8,10},{9,11},{10,... | collective-permute-start | bytes 104 | tf_op jit(solution)/shard_map/ppermute | solution.py:253
  5.3 4.2 %collective-permute-start = (s32[2,4]{1,0:T(2,128)S(1)}, s32[2,4]{1,0:T(2,128)S(1)}, u32[]{:S(2)}, u32[]{:S(2)}) collective-permute-start(s32[2,4]{1,0:T(2,128)S(1)} %pad_add_fusion), channel_id=1, source_target_pairs={{0,4},{1,5},{2,6},{3,7},{4,8},{5,9},{6,10},{7,11},{8,12},{9,13},{1... | collective-permute-start | bytes 104 | tf_op jit(solution)/shard_map/ppermute | solution.py:253
  10.3 8.5 %copy-start.12 = (f32[4,128,128]{2,1,0:T(8,128)S(1)}, f32[4,128,128]{2,1,0:T(8,128)}, u32[]{:S(2)}) copy-start(f32[4,128,128]{2,1,0:T(8,128)} %param.11) | copy-start | bytes 786436
  13.7 11.5 %collective-permute-start.5 = (f32[4,4,2,32,128]{4,3,2,1,0:T(8,128)}, f32[4,4,2,32,128]{4,3,2,1,0:T(8,128)S(1)}, u32[]{:S(2)}, u32[]{:S(2)}) collective-permute-start(f32[4,4,2,32,128]{4,3,2,1,0:T(8,128)} %get-tuple-element.14), channel_id=1, source_target_pairs={{4,0},{5,1},{2,6},{3,7},{8,4},{9,5},{6,10},{7,11},{12,8},{13,9},{1... | collective-permute-start | bytes 1572872 | tf_op jit(solution)/shard_map/ppermute | solution.py:253
  15.3 14.8 %collective-permute-start.6 = (f32[4,4,2,32,128]{4,3,2,1,0:T(8,128)}, f32[4,4,2,32,128]{4,3,2,1,0:T(8,128)S(1)}, u32[]{:S(2)}, u32[]{:S(2)}) collective-permute-start(f32[4,4,2,32,128]{4,3,2,1,0:T(8,128)} %get-tuple-element.15), channel_id=1, source_target_pairs={{1,0},{2,1},{3,6},{4,7},{5,4},{6,5},{7,10},{8,11},{9,8},{10,9},{11... | collective-permute-start | bytes 1572872 | tf_op jit(solution)/shard_map/ppermute | solution.py:253
  17.1 14.1 %collective-permute-start.7 = (f32[4,4,2,32,128]{4,3,2,1,0:T(8,128)}, f32[4,4,2,32,128]{4,3,2,1,0:T(8,128)S(1)}, u32[]{:S(2)}, u32[]{:S(2)}) collective-permute-start(f32[4,4,2,32,128]{4,3,2,1,0:T(8,128)} %get-tuple-element.16), channel_id=1, source_target_pairs={{2,0},{3,1},{4,6},{5,7},{6,4},{7,5},{8,10},{9,11},{10,8},{11,9},{1... | collective-permute-start | bytes 1572872 | tf_op jit(solution)/shard_map/ppermute | solution.py:253
  17.4 23.2 %collective-permute-start.8 = (f32[4,4,2,32,128]{4,3,2,1,0:T(8,128)}, f32[4,4,2,32,128]{4,3,2,1,0:T(8,128)S(1)}, u32[]{:S(2)}, u32[]{:S(2)}) collective-permute-start(f32[4,4,2,32,128]{4,3,2,1,0:T(8,128)} %get-tuple-element.17), channel_id=1, source_target_pairs={{3,0},{4,1},{5,6},{6,7},{7,4},{8,5},{9,10},{10,11},{11,8},{12,9},{... | collective-permute-start | bytes 1572872 | tf_op jit(solution)/shard_map/ppermute | solution.py:253
  18.7 1.9 %collective-permute-start.4 = (f32[4,128,128]{2,1,0:T(8,128)S(1)}, f32[4,128,128]{2,1,0:T(8,128)S(1)}, u32[]{:S(2)}, u32[]{:S(2)}) collective-permute-start(f32[4,128,128]{2,1,0:T(8,128)S(1)} %copy-done.12), channel_id=1, source_target_pairs={{0,0},{1,1},{2,6},{3,7},{4,4},{5,5},{6,10},{7,11},{8,8},{9,9},{10,... | collective-permute-start | bytes 786440 | tf_op jit(solution)/shard_map/ppermute | solution.py:253
  20.7 19.9 %copy-start.8 = (f32[4,128,128]{2,1,0:T(8,128)}, f32[4,128,128]{2,1,0:T(8,128)S(1)}, u32[]{:S(2)}) copy-start(f32[4,128,128]{2,1,0:T(8,128)S(1)} %collective-permute-done.4.amplitude_ref) | copy-start | bytes 786436
  25.2 15.4 %copy-start.4 = (f32[4,4,2,32,128]{4,3,2,1,0:T(8,128)}, f32[4,4,2,32,128]{4,3,2,1,0:T(8,128)S(1)}, u32[]{:S(2)}) copy-start(f32[4,4,2,32,128]{4,3,2,1,0:T(8,128)S(1)} %collective-permute-done.5.refs_1_) | copy-start | bytes 1572868
  30.1 10.5 %copy-start.5 = (f32[4,4,2,32,128]{4,3,2,1,0:T(8,128)}, f32[4,4,2,32,128]{4,3,2,1,0:T(8,128)S(1)}, u32[]{:S(2)}) copy-start(f32[4,4,2,32,128]{4,3,2,1,0:T(8,128)S(1)} %collective-permute-done.6.refs_2_) | copy-start | bytes 1572868
  31.2 9.4 %copy-start.6 = (f32[4,4,2,32,128]{4,3,2,1,0:T(8,128)}, f32[4,4,2,32,128]{4,3,2,1,0:T(8,128)S(1)}, u32[]{:S(2)}) copy-start(f32[4,4,2,32,128]{4,3,2,1,0:T(8,128)S(1)} %collective-permute-done.7.refs_3_) | copy-start | bytes 1572868
  56.6 9.7 %copy-start.11 = (f32[4,4,2,32,128]{4,3,2,1,0:T(8,128)S(1)}, f32[4,4,2,32,128]{4,3,2,1,0:T(8,128)}, u32[]{:S(2)}) copy-start(f32[4,4,2,32,128]{4,3,2,1,0:T(8,128)} %get-tuple-element.22) | copy-start | bytes 1572868
  56.6 3.2 %collective-permute-start.13 = (f32[2,2,128,128]{3,2,1,0:T(8,128)}, f32[2,2,128,128]{3,2,1,0:T(8,128)S(1)}, u32[]{:S(2)}, u32[]{:S(2)}) collective-permute-start(f32[2,2,128,128]{3,2,1,0:T(8,128)} %get-tuple-element.23), channel_id=1, source_target_pairs={{0,1},{1,0},{2,3},{3,2},{4,5},{5,4},{6,7},{7,6},{8,9},{9,8},{10,11... | collective-permute-start | bytes 786440 | tf_op jit(solution)/shard_map/ppermute | solution.py:227
  60.8 7.6 %collective-permute-start.14 = (f32[2,2,128,128]{3,2,1,0:T(8,128)S(1)}, f32[2,2,128,128]{3,2,1,0:T(8,128)S(1)}, u32[]{:S(2)}, u32[]{:S(2)}) collective-permute-start(f32[2,2,128,128]{3,2,1,0:T(8,128)S(1)} %add.18), channel_id=1, source_target_pairs={{0,2},{1,3},{2,0},{3,1},{4,6},{5,7},{6,4},{7,5},{8,10},{9,11},{10,... | collective-permute-start | bytes 786440 | tf_op jit(solution)/shard_map/ppermute | solution.py:227
  61.6 27.3 %collective-permute-start.9 = (f32[4,4,2,32,128]{4,3,2,1,0:T(8,128)}, f32[4,4,2,32,128]{4,3,2,1,0:T(8,128)S(1)}, u32[]{:S(2)}, u32[]{:S(2)}) collective-permute-start(f32[4,4,2,32,128]{4,3,2,1,0:T(8,128)} %get-tuple-element.19), channel_id=1, source_target_pairs={{0,4},{1,5},{6,2},{7,3},{4,8},{5,9},{10,6},{11,7},{8,12},{9,13},{1... | collective-permute-start | bytes 1572872 | tf_op jit(solution)/shard_map/ppermute | solution.py:253
  62.8 26.0 %collective-permute-start.10 = (f32[4,4,2,32,128]{4,3,2,1,0:T(8,128)}, f32[4,4,2,32,128]{4,3,2,1,0:T(8,128)S(1)}, u32[]{:S(2)}, u32[]{:S(2)}) collective-permute-start(f32[4,4,2,32,128]{4,3,2,1,0:T(8,128)} %get-tuple-element.20), channel_id=1, source_target_pairs={{0,1},{1,2},{6,3},{7,4},{4,5},{5,6},{10,7},{11,8},{8,9},{9,10},{14... | collective-permute-start | bytes 1572872 | tf_op jit(solution)/shard_map/ppermute | solution.py:253
  66.3 24.2 %collective-permute-start.11 = (f32[4,4,2,32,128]{4,3,2,1,0:T(8,128)}, f32[4,4,2,32,128]{4,3,2,1,0:T(8,128)S(1)}, u32[]{:S(2)}, u32[]{:S(2)}) collective-permute-start(f32[4,4,2,32,128]{4,3,2,1,0:T(8,128)} %get-tuple-element.21), channel_id=1, source_target_pairs={{0,2},{1,3},{6,4},{7,5},{4,6},{5,7},{10,8},{11,9},{8,10},{9,11},{1... | collective-permute-start | bytes 1572872 | tf_op jit(solution)/shard_map/ppermute | solution.py:253
  66.3 25.0 %collective-permute-start.12 = (f32[4,4,2,32,128]{4,3,2,1,0:T(8,128)S(1)}, f32[4,4,2,32,128]{4,3,2,1,0:T(8,128)S(1)}, u32[]{:S(2)}, u32[]{:S(2)}) collective-permute-start(f32[4,4,2,32,128]{4,3,2,1,0:T(8,128)S(1)} %copy-done.11), channel_id=1, source_target_pairs={{0,3},{1,4},{6,5},{7,6},{4,7},{5,8},{10,9},{11,10},{8,11},{9,12},{... | collective-permute-start | bytes 1572872 | tf_op jit(solution)/shard_map/ppermute | solution.py:253
  68.4 20.2 %collective-permute-start.15 = (f32[2,2,128,128]{3,2,1,0:T(8,128)S(1)}, f32[2,2,128,128]{3,2,1,0:T(8,128)S(1)}, u32[]{:S(2)}, u32[]{:S(2)}) collective-permute-start(f32[2,2,128,128]{3,2,1,0:T(8,128)S(1)} %add.19), channel_id=1, source_target_pairs={{0,4},{1,5},{2,6},{3,7},{4,0},{5,1},{6,2},{7,3},{8,12},{9,13},{10,... | collective-permute-start | bytes 786440 | tf_op jit(solution)/shard_map/ppermute | solution.py:227
  88.7 13.8 %collective-permute-start.16 = (f32[2,2,128,128]{3,2,1,0:T(8,128)S(1)}, f32[2,2,128,128]{3,2,1,0:T(8,128)S(1)}, u32[]{:S(2)}, u32[]{:S(2)}) collective-permute-start(f32[2,2,128,128]{3,2,1,0:T(8,128)S(1)} %add.20), channel_id=1, source_target_pairs={{0,8},{1,9},{2,10},{3,11},{4,12},{5,13},{6,14},{7,15},{8,0},{9,1},... | collective-permute-start | bytes 786440 | tf_op jit(solution)/shard_map/ppermute | solution.py:227
  88.8 2.5 %copy-start = (f32[4,4,2,32,128]{4,3,2,1,0:T(8,128)}, f32[4,4,2,32,128]{4,3,2,1,0:T(8,128)S(1)}, u32[]{:S(2)}) copy-start(f32[4,4,2,32,128]{4,3,2,1,0:T(8,128)S(1)} %collective-permute-done.9.refs_1_) | copy-start | bytes 1572868
  (7 other events, 6.9 us)

commit v2 on v1

v2 whole, which is shorter than its diff:
```python
import functools
import math

import numpy as np
import ml_dtypes
import jax
import jax.numpy as jnp
from jax import lax
from jax.experimental import pallas as pl
from jax.experimental.pallas import tpu as pltpu
from jax.sharding import PartitionSpec as P

INTENSITY_SHIFT = 0.5
FRESNEL = 0.75
LANES = 128
VMEM_BYTES = 20 * 1024 * 1024
EXTRA = 8


def pairs(value):
    first = value.astype(ml_dtypes.bfloat16)
    second = (value - first.astype(np.float64)).astype(ml_dtypes.bfloat16)
    return np.stack([first, second])


def real_form(matrix):
    return np.block([[matrix.real, matrix.imag], [-matrix.imag, matrix.real]])


def tables_of(window_side):
    steps = np.arange(window_side)
    angles = -2.0 * math.pi / window_side * (steps[:, None] * steps[None, :] % window_side)
    transform = np.exp(1j * angles) / math.sqrt(window_side)
    freqs = (steps + window_side // 2) % window_side - window_side // 2
    phase = np.exp(-1j * math.pi * FRESNEL * freqs**2 / (window_side / 2.0) ** 2)
    step = transform.conj() @ (phase[:, None] * transform)
    forms = [real_form(m) for m in (step, step.conj(), transform, transform.conj())]
    return np.stack([pairs(form) for form in forms])


def halves(value):
    first = value.astype(jnp.bfloat16)
    return first, (value - first.astype(jnp.float32)).astype(jnp.bfloat16)


def product(left, right):
    return jnp.dot(left, right, preferred_element_type=jnp.float32)


def right_apply(field, table):
    first, second = halves(field)
    return product(first, table[0]) + (product(second, table[0]) + product(first, table[1]))


def left_apply(table, field):
    first, second = halves(field)
    return product(table[0], first) + (product(table[0], second) + product(table[1], first))


def both_sides(waves, right_table, left_table):
    side = waves[0][0].shape[0]
    rows = jnp.concatenate([jnp.concatenate(wave, axis=1) for wave in waves], axis=0)
    half = right_apply(rows, right_table)
    count = len(waves)
    parts = [
        jnp.concatenate(
            [half[m * side : (m + 1) * side, c * side : (c + 1) * side] for m in range(count)], axis=1
        )
        for c in range(2)
    ]
    full = left_apply(left_table, jnp.concatenate(parts, axis=0))
    return [
        tuple(full[c * side : (c + 1) * side, m * side : (m + 1) * side] for c in range(2))
        for m in range(count)
    ]


def times(a, b):
    return (a[0] * b[0] - a[1] * b[1], a[0] * b[1] + a[1] * b[0])


def conj_times(a, b):
    return (a[0] * b[0] + a[1] * b[1], a[0] * b[1] - a[1] * b[0])


class Stage:
    def __init__(self, forward, far, backward, sizes):
        self.forward, self.far, self.backward = forward, far, backward
        self.windows, self.modes, self.side, self.rows_here, self.cols = sizes
        self.reach = self.side // self.rows_here
        self.carry = 0 in backward
        self.grad_rows = self.windows * len(backward) * 2 * self.rows_here
        self.group = math.gcd(self.windows, 4)
        loaded = set(backward) - set(forward)
        waves = loaded | set(forward[:1])
        vmem = ["tables"]
        vmem += ["probe"] if 0 in waves else []
        vmem += ["amplitude"] if far else []
        vmem += [f"psi{s}" for s in sorted(waves) if s > 0] + [f"crop{s}" for s in sorted(loaded)]
        vmem += [] if far else [f"exit{s + 1}" for s in backward[:1]]
        if forward:
            vmem += ["own", "own_mate", "partner", "partner_mate", "edge", "edge_mate", "first_rows"]
        self.vmem_in = vmem
        outs = [f"grad{j}" for j in range(self.reach + 1)] if backward else []
        if not backward:
            outs += [f"psi{s + 1}" for s in forward] + [f"crop{s}" for s in forward]
        else:
            outs.append("part" if self.carry else f"exit{backward[-1]}")
        self.vmem_out = outs
        if backward:
            outs += [f"grad{j}" for j in range(self.reach + 1)]

    def out_shape(self, name):
        side = self.side
        if name.startswith("grad"):
            shape = (self.grad_rows + (EXTRA if self.carry else 0), side)
        elif name == "part":
            shape = (2 * self.modes * side, side)
        elif name.startswith("crop"):
            shape = (self.windows, 2, side, side)
        else:
            shape = (self.windows, self.modes, 2, side, side)
        return jax.ShapeDtypeStruct(shape, jnp.float32)

    def __call__(self, values):
        inputs = ["offsets"] + self.vmem_in
        outputs = self.vmem_out
        args = [values[name] for name in inputs]
        shapes = [self.out_shape(name) for name in outputs]
        smem, vmem = (pl.BlockSpec(memory_space=space) for space in (pltpu.SMEM, pltpu.VMEM))
        outs = pl.pallas_call(
            self.kernel,
            out_shape=shapes,
            in_specs=[smem] + [vmem] * len(self.vmem_in),
            out_specs=[vmem] * len(self.vmem_out),
            cost_estimate=pl.CostEstimate(flops=0, bytes_accessed=0, transcendentals=0),
            compiler_params=pltpu.CompilerParams(vmem_limit_bytes=VMEM_BYTES),
        )(*args)
        return dict(zip(outputs, outs))

    def kernel(self, *refs):
        names = ["offsets"] + self.vmem_in + self.vmem_out
        r = dict(zip(names, refs))
        side, rows_here, modes, group = self.side, self.rows_here, self.modes, self.group
        forward, backward = self.forward, self.backward
        step, step_conj, transform, transform_conj = (
            (r["tables"][i, 0], r["tables"][i, 1]) for i in range(4)
        )
        me = lax.axis_index("tile")
        parity, moved = me % 2, moved_here(me)
        blocks = self.cols // LANES

        if self.carry:
            index = lax.broadcasted_iota(jnp.int32, (EXTRA, side), 0)
            carried = jnp.zeros((EXTRA, side), jnp.int32)
            for w in range(self.windows):
                carried = jnp.where(index == w, r["offsets"][1, w], carried)
            for j in range(1, self.reach + 1):
                r[f"grad{j}"][pl.ds(self.grad_rows, EXTRA)] = carried.astype(jnp.float32)
            r["part"][...] = jnp.zeros(r["part"].shape, jnp.float32)
        def start(w):
            row, col = r["offsets"][0, w], r["offsets"][1, w]
            block = col // LANES
            after = jnp.where(block + 1 == blocks, 0, block + 1)
            near, far = (pl.ds(pl.multiple_of(b * LANES, LANES), LANES) for b in (block, after))
            lane = col % LANES
            below = lax.broadcasted_iota(jnp.int32, (rows_here, side), 0) >= row
            here = jnp.where(below, 1, 0) != moved
            wraps = lax.broadcasted_iota(jnp.int32, (rows_here, side), 1) < lane
            return row, lane, near, far, here, wraps

        def crop(s, place):
            _, _, near, far, here, wraps = place

            def columns(name, c):
                tile = r[name].at[pl.ds((2 * s + c) * rows_here, rows_here)]
                return jnp.where(wraps, tile[:, far], tile[:, near])

            def plane(c):
                first = jnp.where(here, columns("own", c), columns("edge", c))
                outer = jnp.where(parity == moved, columns("own_mate", c), columns("edge_mate", c))
                inner = columns("partner_mate", c)
                pair = [jnp.where(parity == 0, a, b) for a, b in ((outer, inner), (inner, outer))]
                return jnp.concatenate([first, pair[0], columns("partner", c), pair[1]], axis=0)

            return (plane(0), plane(1))

        def keep(w, i, place, grad):
            here = place[4]
            for c in range(2):
                first = ((w * len(backward) + i) * 2 + c) * rows_here
                at = pl.ds(pl.multiple_of(first, rows_here), rows_here)
                rows = [grad[c][j * rows_here : (j + 1) * rows_here] for j in range(self.reach)]
                r["grad0"][at] = jnp.where(here, rows[0], 0.0)
                r["grad1"][at] = jnp.where(here, 0.0, rows[0])
                r["grad2"][at] = rows[2]
                r["grad3"][at] = jnp.where(parity == 0, rows[3], rows[1])
                r["grad4"][at] = jnp.where(parity == 0, rows[1], rows[3])

        def turn(value, row, lane):
            return pltpu.roll(pltpu.roll(value, row, 0), lane, 1)

        def load(ref, w):
            return [tuple(ref[w, m, c] for c in range(2)) for m in range(modes)]

        def store(ref, w, waves):
            for m in range(modes):
                for c in range(2):
                    ref[w, m, c] = waves[m][c]

        def entry(w, s, place):
            if s > 0:
                return load(r[f"psi{s}"], w)
            return [
                tuple(turn(r["probe"][m, c], place[0], place[1]) for c in range(2)) for m in range(modes)
            ]

        def visit(index, carry):
            ids = [index * group + k for k in range(group)]
            turns = list(enumerate(ids))
            places = [start(w) for w in ids]
            crops, waves = {}, {}
            for k, w in turns:
                for s in forward:
                    crops[k, s] = crop(s, places[k])
                for s in backward:
                    if s not in forward:
                        crops[k, s] = tuple(r[f"crop{s}"][w, c] for c in range(2))
                        waves[k, s] = entry(w, s, places[k])
                for s in forward[:1]:
                    waves[k, s] = entry(w, s, places[k])
                if not backward:
                    for s in forward:
                        for c in range(2):
                            r[f"crop{s}"][w, c] = crops[k, s][c]
            for s in forward:
                exits = [[times(crops[k, s], wave) for wave in waves[k, s]] for k, w in turns]
                if self.far and s == forward[-1]:
                    break
                for k, w in turns:
                    waves[k, s + 1] = both_sides(exits[k], step, step_conj)
                    if not backward:
                        store(r[f"psi{s + 1}"], w, waves[k, s + 1])
            if self.far:
                exits = [both_sides(out, transform, transform_conj) for out in exits]
                for k, w in turns:
                    intensity = sum(re * re + im * im for re, im in exits[k])
                    scale = 1.0 - r["amplitude"][pl.ds(w * side, side)] * lax.rsqrt(intensity + INTENSITY_SHIFT)
                    exits[k] = [(re * scale, im * scale) for re, im in exits[k]]
                exits = [both_sides(out, transform_conj, transform) for out in exits]
            elif backward:
                exits = [load(r[f"exit{backward[0] + 1}"], w) for w in ids]
            for i, s in enumerate(backward):
                if not (self.far and i == 0):
                    exits = [both_sides(out, step_conj, step) for out in exits]
                for k, w in turns:
                    terms = [conj_times(wave, out) for wave, out in zip(waves[k, s], exits[k])]
                    keep(w, s - backward[-1], places[k], [sum(term[c] for term in terms) for c in range(2)])
                    exits[k] = [conj_times(crops[k, s], out) for out in exits[k]]
            if self.carry:
                for k, (row, lane, *_) in enumerate(places):
                    for m in range(modes):
                        for c in range(2):
                            back = turn(exits[k][m][c], (side - row) % side, (side - lane) % side)
                            r["part"][pl.ds((2 * m + c) * side, side)] += back
            elif backward:
                for k, w in turns:
                    store(r[f"exit{backward[-1]}"], w, exits[k])
            return carry

        lax.fori_loop(0, self.windows // group, visit, 0)


def give_kernel(windows, count, col_ref, *refs):
    pieces, base, out_ref = refs[:count], refs[count:-1], refs[-1]
    planes, rows, cols = out_ref.shape
    blocks = cols // LANES
    lanes = lax.broadcasted_iota(jnp.int32, (1, 1, LANES), 2)
    out_ref[...] = base[0][...] if base else jnp.zeros(out_ref.shape, jnp.float32)
    for k, piece in enumerate(pieces):
        for w in range(windows):
            col = col_ref[k, w]
            block, lane = col // LANES, col % LANES
            after = jnp.where(block + 1 == blocks, 0, block + 1)
            near, far = (pl.ds(pl.multiple_of(b * LANES, LANES), LANES) for b in (block, after))
            value = piece[pl.ds(w * planes * rows, planes * rows)].reshape(planes, rows, LANES)
            wraps = lanes < lane
            out_ref[:, :, near] += jnp.where(wraps, 0.0, value)
            out_ref[:, :, far] += jnp.where(wraps, value, 0.0)


def give(windows, columns, pieces, shape, base=()):
    smem, vmem = (pl.BlockSpec(memory_space=space) for space in (pltpu.SMEM, pltpu.VMEM))
    return pl.pallas_call(
        functools.partial(give_kernel, windows, len(pieces)),
        out_shape=jax.ShapeDtypeStruct(shape, jnp.float32),
        in_specs=[smem] + [vmem] * (len(pieces) + len(base)),
        out_specs=vmem,
        compiler_params=pltpu.CompilerParams(vmem_limit_bytes=VMEM_BYTES),
    )(jnp.stack(columns), *pieces, *base)


def fetch(*arrays):
    def kernel(*refs):
        count = len(arrays)
        sources, targets, done = refs[:count], refs[count : 2 * count], refs[-1]
        copies = [pltpu.make_async_copy(*refs, done.at[i]) for i, refs in enumerate(zip(sources, targets))]
        for copy in copies:
            copy.start()
        for copy in copies:
            copy.wait()

    anywhere, vmem = pl.BlockSpec(memory_space=pltpu.HBM), pl.BlockSpec(memory_space=pltpu.VMEM)
    return pl.pallas_call(
        kernel,
        out_shape=[jax.ShapeDtypeStruct(x.shape, x.dtype) for x in arrays],
        in_specs=[anywhere] * len(arrays),
        out_specs=[vmem] * len(arrays),
        scratch_shapes=[pltpu.SemaphoreType.DMA((len(arrays),))],
        compiler_params=pltpu.CompilerParams(vmem_limit_bytes=VMEM_BYTES),
    )(*arrays)


def moved_here(tile):
    return tile // 2 % 2


def swap(value, bits):
    count = lax.axis_size("tile")
    return lax.ppermute(value, "tile", [(i, i ^ bits) for i in range(count)])


def sum_over_tiles(total):
    bit = 8
    while bit < lax.axis_size("tile"):
        total = total + swap(total, bit)
        bit *= 2
    return total


def on_device(slices, probe_modes, row_offset, col_offset, amplitude):
    modes, _, side, _ = probe_modes.shape
    slice_count, _, rows_here, cols = slices.shape
    windows = row_offset.shape[0]
    count = lax.axis_size("tile")
    reach = side // rows_here
    assert side == LANES and side % rows_here == 0 and cols % LANES == 0
    assert reach == 4 and count % reach == 0 and count & (count - 1) == 0
    home = [(t + reach) % count if moved_here(t) else t for t in range(count)]
    to_edge = [(t, home[t]) if moved_here(t) else ((t + reach) % count, t) for t in range(count)]
    from_edge = [(b, a) for a, b in to_edge]
    even = lax.axis_index("tile") % 2 == 0
    sizes = (windows, modes, side, rows_here, cols)

    def send(value, pairs_there):
        return lax.ppermute(value, "tile", pairs_there)


    def return_route(even_step, odd_step):
        return [(home[t], (t + (odd_step if t % 2 else even_step)) % count) for t in range(count)]

    flat = slices.reshape(slice_count * 2 * rows_here, cols)
    to_home = list(enumerate(home))
    partner, edge, own_mate = swap(flat, 2), send(flat, to_edge), swap(flat, 1)
    fetched = fetch(flat, probe_modes, jnp.asarray(tables_of(side)))
    partner, *fetched = lax.optimization_barrier((partner, *fetched))
    carried = jnp.stack([row_offset, col_offset]).astype(jnp.float32)
    carried = jnp.pad(carried, ((0, EXTRA - 2), (0, side - windows)))
    measured = jnp.concatenate([amplitude.reshape(windows * side, side), carried])
    measured = send(measured, to_home)
    first_rows = swap(partner[:EXTRA], 1)
    edge, measured, first_rows = lax.optimization_barrier((edge, measured, first_rows))
    offsets = measured[windows * side :][:2, :windows].astype(jnp.int32)
    partner_mate, edge_mate = swap(partner, 1), swap(edge, 1)
    values = {
        "own": fetched[0],
        "probe": fetched[1],
        "tables": fetched[2],
        "offsets": offsets,
        "own_mate": own_mate,
        "partner": partner,
        "partner_mate": partner_mate,
        "edge": edge,
        "edge_mate": edge_mate,
        "amplitude": measured,
        "first_rows": first_rows,
    }
    chunk = list(range(slice_count))
    result = Stage(chunk, True, chunk[::-1], sizes)(values)

    part = result["part"] + swap(result["part"], 2)
    lower, upper = part[: modes * side], part[modes * side :]
    total = jnp.where(even, lower, upper) + swap(jnp.where(even, upper, lower), 1)
    pieces = [result[f"grad{j}"] for j in range(reach + 1)]
    total = total + swap(total, 4)
    outer = send(pieces[4], return_route(1, 3))
    early = [pieces[0], send(pieces[1], from_edge), outer, send(pieces[3], return_route(3, 1))]
    late = [send(pieces[2], return_route(2, 2))]
    total, *early = lax.optimization_barrier((total, *early))

    def columns_of(piece):
        return piece[-EXTRA:][:windows, 0].astype(jnp.int32)

    shape = (2 * slice_count, rows_here, cols)
    columns = [offsets[1]] + [columns_of(piece) for piece in early[1:]]
    own_grad = give(windows, columns, early, shape)
    total = sum_over_tiles(total)
    rest = swap(total, 1)
    total, rest, own_grad, *late = lax.optimization_barrier((total, rest, own_grad, *late))
    own_grad = give(windows, [columns_of(piece) for piece in late], late, shape, [own_grad])
    own_grad = own_grad.reshape(slices.shape)
    probe_grad = jnp.where(even, jnp.concatenate([total, rest]), jnp.concatenate([rest, total]))
    return own_grad, probe_grad.reshape(probe_modes.shape)


def solution(mesh):
    placed = (
        P(None, None, ("scan", "tile"), None),
        P("scan", None, None, None),
        P(("scan", "tile")),
        P(("scan", "tile")),
        P(("scan", "tile"), None, None),
    )
    return jax.shard_map(
        on_device,
        mesh=mesh,
        in_specs=placed,
        out_specs=(P(None, None, ("scan", "tile"), None), P("scan", None, None, None)),
        check_vma=False,
    )
```

time: 104 us -> 87.4 us (0.84)
  Pallas kernels: 22.6 us -> 14.7 us
  waiting for transfers between devices: 51.5 us -> 44.5 us
  local copies, waits for them, and re-layouts: 5.34 us -> 3.12 us
  starting transfers between devices: 20.6 us -> 21.9 us
    ppermute x13 -> x6, waiting for transfers between devices: 23.5 us -> 0.31 us  [send(): return lax.ppermute(value, 'tile', pairs_there)]
    ppermute x4 -> x10, waiting for transfers between devices: 28 us -> 44.2 us  [swap(): return lax.ppermute(value, 'tile', [(i, i ^ bits) for i in range(count)])]
    ppermute x4 -> x10, starting transfers between devices: 3.66 us -> 14.1 us  [swap(): return lax.ppermute(value, 'tile', [(i, i ^ bits) for i in range(count)])]
    ppermute x13 -> x6, starting transfers between devices: 16.9 us -> 7.77 us  [send(): return lax.ppermute(value, 'tile', pairs_there)]
    pallas_call x3 -> x4, Pallas kernels: 22.6 us -> 14.7 us  [the longest x1 11.1 us: __call__(): pl.pallas_call(self.kernel, out_shape=shapes, in_specs=[smem] + [vmem] *...]
    add x4, other arithmetic: 1.78 us -> 0.09 us  [the longest x1 0.04 us: on_device(): part = result['part'] + swap(result['part'], 2)]
    concatenate x1 -> x0, local copies, waits for them, and re-layouts: 1.23 us -> none  [on_device(): jnp.concatenate([mine, jnp.full((1, windows), is_moved, jnp.int32)])]
    unnamed x28 -> x10, local copies, waits for them, and re-layouts: 2.9 us -> 3.12 us
  transfers between devices with their start and end apart: 17 -> 16, of which waited for: 12 -> 7; matrix products, arithmetic and copies ran while one was open for 2% -> 2% of each run, Pallas kernels for 4% -> 2%
where the time goes in v2:
time: 87.4 us; the launch traced here: 87.2 us
  waiting for transfers between devices  44.5 us (51%)
  starting transfers between devices  21.9 us (25%)
  Pallas kernels  14.7 us (17%)
  local copies, waits for them, and re-layouts  3.12 us (4%)
  other arithmetic  2.25 us (3%)
    ppermute x10, waiting for transfers between devices, swap(): return lax.ppermute(value, 'tile', [(i, i ^ bits) for i in range(count)])  44.2 us
    ppermute x10, starting transfers between devices, swap(): return lax.ppermute(value, 'tile', [(i, i ^ bits) for i in range(count)])  14.1 us
    pallas_call x1, Pallas kernels, __call__(): pl.pallas_call(self.kernel, out_shape=shapes, in_specs=[smem] + [vmem] *...  11.1 us
    ppermute x6, starting transfers between devices, send(): return lax.ppermute(value, 'tile', pairs_there)  7.77 us
    pallas_call x2, Pallas kernels, give(): pl.pallas_call(functools.partial(give_kernel, windows, len(pieces)), out_...  3.42 us
    unnamed x10, local copies, waits for them, and re-layouts  3.12 us
  transfers between devices with their start and end apart: 16, of which 7 were waited for; matrix products, arithmetic and copies ran while one was open for 2% of the time, Pallas kernels for 2%

profile of v2, /device:TPU:1, one launch (start us, length us, event | category | flops | bytes accessed | tf_op | source)
XLA Modules:
  0.0 87.2 jit_solution(8322452542489590161)
XLA Ops:
  0.6 2.1 %collective-permute-start.2 = (f32[256,1024]{1,0:T(8,128)}, f32[256,1024]{1,0:T(8,128)S(1)}, u32[]{:S(2)}, u32[]{:S(2)}) collective-permute-start(f32[256,1024]{1,0:T(8,128)} %bitcast.10), channel_id=1, source_target_pairs={{0,2},{1,3},{2,0},{3,1},{4,6},{5,7},{6,4},{7,5},{8,10},{9,11},{10,... | collective-permute-start | bytes 3145736 | tf_op jit(solution)/shard_map/ppermute | solution.py:330
  2.8 3.3 %collective-permute-start = (f32[256,1024]{1,0:T(8,128)}, f32[256,1024]{1,0:T(8,128)S(1)}, u32[]{:S(2)}, u32[]{:S(2)}) collective-permute-start(f32[256,1024]{1,0:T(8,128)} %bitcast.11), channel_id=1, source_target_pairs={{4,0},{5,1},{2,6},{3,7},{8,4},{9,5},{6,10},{7,11},{12,8},{13,9},{1... | collective-permute-start | bytes 3145736 | tf_op jit(solution)/shard_map/ppermute | solution.py:356
  6.1 0.7 copy-done.3
  6.8 1.0 %select_maximum_fusion = f32[520,128]{1,0:T(8,128)S(1)} fusion(f32[2,4]{1,0:T(2,128)S(1)} %add_convert_fusion, f32[512,128]{1,0:T(8,128)} %bitcast.17), kind=kLoop, calls=%fused_computation | loop fusion | flops 199680 | bytes 528416 | tf_op jit(solution)/shard_map/concatenate | solution.py:369
  7.8 0.7 collective-permute-start.1
  8.5 1.2 %copy-done = f32[4,2,32,1024]{3,2,1,0:T(8,128)S(1)} copy-done((f32[4,2,32,1024]{3,2,1,0:T(8,128)S(1)}, f32[4,2,32,1024]{3,2,1,0:T(8,128)}, u32[]{:S(2)}) %copy-start) | copy-done | bytes 1048600
  9.7 1.2 %copy-done.1 = bf16[4,2,256,256]{3,2,1,0:T(8,128)(2,1)S(1)} copy-done((bf16[4,2,256,256]{3,2,1,0:T(8,128)(2,1)S(1)}, bf16[4,2,256,256]{3,2,1,0:T(8,128)(2,1)}, u32[]{:S(2)}) %copy-start.1) | copy-done | bytes 1048600
  11.1 14.7 %collective-permute-done.2.refs_6_ = f32[256,1024]{1,0:T(8,128)S(1)} collective-permute-done((f32[256,1024]{1,0:T(8,128)}, f32[256,1024]{1,0:T(8,128)S(1)}, u32[]{:S(2)}, u32[]{:S(2)}) %collective-permute-start.2) | collective-permute-done | bytes 1048608 | tf_op jit(solution)/shard_map/ppermute | solution.py:330
  25.9 1.2 %collective-permute-start.3 = (f32[8,1024]{1,0:T(8,128)S(1)}, f32[8,1024]{1,0:T(8,128)S(1)}, u32[]{:S(2)}, u32[]{:S(2)}) collective-permute-start(f32[8,1024]{1,0:T(8,128)S(1)} %slice.37), channel_id=1, source_target_pairs={{0,1},{1,0},{2,3},{3,2},{4,5},{5,4},{6,7},{7,6},{8,9},{9,8},{10,11... | collective-permute-start | bytes 98312 | tf_op jit(solution)/shard_map/ppermute | solution.py:330
  28.0 1.8 %collective-permute-start.6 = (f32[256,1024]{1,0:T(8,128)S(1)}, f32[256,1024]{1,0:T(8,128)S(1)}, u32[]{:S(2)}, u32[]{:S(2)}) collective-permute-start(f32[256,1024]{1,0:T(8,128)S(1)} %collective-permute-done.refs_8_), channel_id=1, source_target_pairs={{0,1},{1,0},{2,3},{3,2},{4,5},{5,4},{6,7},{7,6},{8,9},{9,8},{10,11... | collective-permute-start | bytes 3145736 | tf_op jit(solution)/shard_map/ppermute | solution.py:330
  29.8 1.5 %collective-permute-done.5.refs_7_ = f32[256,1024]{1,0:T(8,128)S(1)} collective-permute-done((f32[256,1024]{1,0:T(8,128)S(1)}, f32[256,1024]{1,0:T(8,128)S(1)}, u32[]{:S(2)}, u32[]{:S(2)}) %collective-permute-start.5) | collective-permute-done | bytes 1048608 | tf_op jit(solution)/shard_map/ppermute | solution.py:330
  31.3 1.5 %collective-permute-done.6.refs_9_ = f32[256,1024]{1,0:T(8,128)S(1)} collective-permute-done((f32[256,1024]{1,0:T(8,128)S(1)}, f32[256,1024]{1,0:T(8,128)S(1)}, u32[]{:S(2)}, u32[]{:S(2)}) %collective-permute-start.6) | collective-permute-done | bytes 1048608 | tf_op jit(solution)/shard_map/ppermute | solution.py:330
  32.8 11.1 %shard_map.78 = (f32[1032,128]{1,0:T(8,128)}, f32[1032,128]{1,0:T(8,128)}, f32[1032,128]{1,0:T(8,128)}, f32[1032,128]{1,0:T(8,128)}, f32[1032,128]{1,0:T(8,128)}...) custom-call(s32[2,4]{1,0:T(2,128)S(1)} %slice_convert_fusion.refs_0_, ...), custom_call_target="tpu_custom_call" | custom-call | tf_op jit(solution)/shard_map/pallas_call | solution.py:131
  43.9 5.9 %collective-permute-start.7 = (f32[512,128]{1,0:T(8,128)S(1)}, f32[512,128]{1,0:T(8,128)S(1)}, u32[]{:S(2)}, u32[]{:S(2)}) collective-permute-start(f32[512,128]{1,0:T(8,128)S(1)} %get-tuple-element.37), channel_id=1, source_target_pairs={{0,2},{1,3},{2,0},{3,1},{4,6},{5,7},{6,4},{7,5},{8,10},{9,11},{10,... | collective-permute-start | bytes 786440 | tf_op jit(solution)/shard_map/ppermute | solution.py:330
  49.8 1.5 %collective-permute-start.11 = (f32[1032,128]{1,0:T(8,128)S(1)}, f32[1032,128]{1,0:T(8,128)S(1)}, u32[]{:S(2)}, u32[]{:S(2)}) collective-permute-start(f32[1032,128]{1,0:T(8,128)S(1)} %get-tuple-element.40), channel_id=1, source_target_pairs={{0,1},{1,4},{6,3},{7,6},{4,5},{5,8},{10,7},{11,10},{8,9},{9,12},{1... | collective-permute-start | bytes 1585160 | tf_op jit(solution)/shard_map/ppermute | solution.py:356
  51.7 4.4 %collective-permute-done.7 = f32[512,128]{1,0:T(8,128)S(1)} collective-permute-done((f32[512,128]{1,0:T(8,128)S(1)}, f32[512,128]{1,0:T(8,128)S(1)}, u32[]{:S(2)}, u32[]{:S(2)}) %collective-permute-start.7) | collective-permute-done | bytes 262176 | tf_op jit(solution)/shard_map/ppermute | solution.py:330
  56.2 1.4 %collective-permute-start.8 = (f32[256,128]{1,0:T(8,128)S(1)}, f32[256,128]{1,0:T(8,128)S(1)}, u32[]{:S(2)}, u32[]{:S(2)}) collective-permute-start(f32[256,128]{1,0:T(8,128)S(1)} %slice_select_fusion), channel_id=1, source_target_pairs={{0,1},{1,0},{2,3},{3,2},{4,5},{5,4},{6,7},{7,6},{8,9},{9,8},{10,11... | collective-permute-start | bytes 393224 | tf_op jit(solution)/shard_map/ppermute | solution.py:330
  57.6 1.8 %collective-permute-start.15 = (f32[1032,128]{1,0:T(8,128)S(1)}, f32[1032,128]{1,0:T(8,128)S(1)}, u32[]{:S(2)}, u32[]{:S(2)}) collective-permute-start(f32[1032,128]{1,0:T(8,128)S(1)} %get-tuple-element.47), channel_id=1, source_target_pairs={{0,2},{1,3},{6,4},{7,5},{4,6},{5,7},{10,8},{11,9},{8,10},{9,11},{1... | collective-permute-start | bytes 1585160 | tf_op jit(solution)/shard_map/ppermute | solution.py:356
  59.5 14.4 %collective-permute-done.9 = f32[256,128]{1,0:T(8,128)S(1)} collective-permute-done((f32[256,128]{1,0:T(8,128)S(1)}, f32[256,128]{1,0:T(8,128)S(1)}, u32[]{:S(2)}, u32[]{:S(2)}) %collective-permute-start.9) | collective-permute-done | bytes 131104 | tf_op jit(solution)/shard_map/ppermute | solution.py:330
  74.6 7.6 %collective-permute-done.13 = f32[256,128]{1,0:T(8,128)S(1)} collective-permute-done((f32[256,128]{1,0:T(8,128)S(1)}, f32[256,128]{1,0:T(8,128)S(1)}, u32[]{:S(2)}, u32[]{:S(2)}) %collective-permute-start.13) | collective-permute-done | bytes 131104 | tf_op jit(solution)/shard_map/ppermute | solution.py:330
  82.2 0.5 collective-permute-start.14
  82.9 1.6 %shard_map.79.refs_1_ = f32[8,32,1024]{2,1,0:T(8,128)S(1)} custom-call(s32[4,4]{1,0:T(4,128)S(1)} %pad_add_fusion.col_ref, f32[1032,128]{1,0:T(8,128)S(1)} %get-tuple-element.46.refs_0_, f32[1032,128]{1,0:T(8,128)S(1)} %collective-permute-done.10.refs_1_, f32[1032,128]{1,0:T(8,128)S(1)} %collective-permute-done.11.refs_2_, ...), custom_call_target="tpu_custom_call" | custom-call | tf_op jit(solution)/shard_map/pallas_call | solution.py:294
  84.7 0.7 maximum_select_fusion
  85.4 1.8 %shard_map.80 = f32[8,32,1024]{2,1,0:T(8,128)} custom-call(s32[1,4]{1,0:T(1,128)S(1)} %bitcast.14, f32[1032,128]{1,0:T(8,128)S(1)} %collective-permute-done.15.refs_0_, f32[8,32,1024]{2,1,0:T(8,128)S(1)} %shard_map.79.refs_1_), custom_call_target="tpu_custom_call" | custom-call | tf_op jit(solution)/shard_map/pallas_call | solution.py:294
  (37 shorter events, 2.6 us)
Async XLA Ops:
  0.6 25.2 %collective-permute-start.2 = (f32[256,1024]{1,0:T(8,128)}, f32[256,1024]{1,0:T(8,128)S(1)}, u32[]{:S(2)}, u32[]{:S(2)}) collective-permute-start(f32[256,1024]{1,0:T(8,128)} %bitcast.10), channel_id=1, source_target_pairs={{0,2},{1,3},{2,0},{3,1},{4,6},{5,7},{6,4},{7,5},{8,10},{9,11},{10,... | collective-permute-start | bytes 3145736 | tf_op jit(solution)/shard_map/ppermute | solution.py:330
  2.8 25.1 %collective-permute-start = (f32[256,1024]{1,0:T(8,128)}, f32[256,1024]{1,0:T(8,128)S(1)}, u32[]{:S(2)}, u32[]{:S(2)}) collective-permute-start(f32[256,1024]{1,0:T(8,128)} %bitcast.11), channel_id=1, source_target_pairs={{4,0},{5,1},{2,6},{3,7},{8,4},{9,5},{6,10},{7,11},{12,8},{13,9},{1... | collective-permute-start | bytes 3145736 | tf_op jit(solution)/shard_map/ppermute | solution.py:356
  6.1 0.7 copy-start.3
  6.1 0.7 copy-start.4
  6.8 1.7 %copy-start.2 = (f32[2,2,128,128]{3,2,1,0:T(8,128)S(1)}, f32[2,2,128,128]{3,2,1,0:T(8,128)}, u32[]{:S(2)}) copy-start(f32[2,2,128,128]{3,2,1,0:T(8,128)} %refs_1_.1) | copy-start | bytes 786436
  7.8 19.8 %collective-permute-start.1 = (f32[520,128]{1,0:T(8,128)S(1)}, f32[520,128]{1,0:T(8,128)S(1)}, u32[]{:S(2)}, u32[]{:S(2)}) collective-permute-start(f32[520,128]{1,0:T(8,128)S(1)} %select_maximum_fusion), channel_id=1, source_target_pairs={{0,0},{1,1},{2,6},{3,7},{4,4},{5,5},{6,10},{7,11},{8,8},{9,9},{10,... | collective-permute-start | bytes 798728 | tf_op jit(solution)/shard_map/ppermute | solution.py:356
  8.5 1.2 %copy-start = (f32[4,2,32,1024]{3,2,1,0:T(8,128)S(1)}, f32[4,2,32,1024]{3,2,1,0:T(8,128)}, u32[]{:S(2)}) copy-start(f32[4,2,32,1024]{3,2,1,0:T(8,128)} %param.6) | copy-start | bytes 3145732
  9.7 1.2 %copy-start.1 = (bf16[4,2,256,256]{3,2,1,0:T(8,128)(2,1)S(1)}, bf16[4,2,256,256]{3,2,1,0:T(8,128)(2,1)}, u32[]{:S(2)}) copy-start(bf16[4,2,256,256]{3,2,1,0:T(8,128)(2,1)} %constant.22.clone.refs_2_) | copy-start | bytes 3145732
  25.9 2.1 %collective-permute-start.3 = (f32[8,1024]{1,0:T(8,128)S(1)}, f32[8,1024]{1,0:T(8,128)S(1)}, u32[]{:S(2)}, u32[]{:S(2)}) collective-permute-start(f32[8,1024]{1,0:T(8,128)S(1)} %slice.37), channel_id=1, source_target_pairs={{0,1},{1,0},{2,3},{3,2},{4,5},{5,4},{6,7},{7,6},{8,9},{9,8},{10,11... | collective-permute-start | bytes 98312 | tf_op jit(solution)/shard_map/ppermute | solution.py:330
  27.1 2.7 %collective-permute-start.4 = (f32[256,1024]{1,0:T(8,128)S(1)}, f32[256,1024]{1,0:T(8,128)S(1)}, u32[]{:S(2)}, u32[]{:S(2)}) collective-permute-start(f32[256,1024]{1,0:T(8,128)S(1)} %bitcast.13), channel_id=1, source_target_pairs={{0,1},{1,0},{2,3},{3,2},{4,5},{5,4},{6,7},{7,6},{8,9},{9,8},{10,11... | collective-permute-start | bytes 3145736 | tf_op jit(solution)/shard_map/ppermute | solution.py:330
  27.1 4.2 %collective-permute-start.5 = (f32[256,1024]{1,0:T(8,128)S(1)}, f32[256,1024]{1,0:T(8,128)S(1)}, u32[]{:S(2)}, u32[]{:S(2)}) collective-permute-start(f32[256,1024]{1,0:T(8,128)S(1)} %collective-permute-done.2.refs_6_), channel_id=1, source_target_pairs={{0,1},{1,0},{2,3},{3,2},{4,5},{5,4},{6,7},{7,6},{8,9},{9,8},{10,11... | collective-permute-start | bytes 3145736 | tf_op jit(solution)/shard_map/ppermute | solution.py:330
  28.0 4.8 %collective-permute-start.6 = (f32[256,1024]{1,0:T(8,128)S(1)}, f32[256,1024]{1,0:T(8,128)S(1)}, u32[]{:S(2)}, u32[]{:S(2)}) collective-permute-start(f32[256,1024]{1,0:T(8,128)S(1)} %collective-permute-done.refs_8_), channel_id=1, source_target_pairs={{0,1},{1,0},{2,3},{3,2},{4,5},{5,4},{6,7},{7,6},{8,9},{9,8},{10,11... | collective-permute-start | bytes 3145736 | tf_op jit(solution)/shard_map/ppermute | solution.py:330
  43.9 12.3 %collective-permute-start.7 = (f32[512,128]{1,0:T(8,128)S(1)}, f32[512,128]{1,0:T(8,128)S(1)}, u32[]{:S(2)}, u32[]{:S(2)}) collective-permute-start(f32[512,128]{1,0:T(8,128)S(1)} %get-tuple-element.37), channel_id=1, source_target_pairs={{0,2},{1,3},{2,0},{3,1},{4,6},{5,7},{6,4},{7,5},{8,10},{9,11},{10,... | collective-permute-start | bytes 786440 | tf_op jit(solution)/shard_map/ppermute | solution.py:330
  49.8 24.2 %collective-permute-start.10 = (f32[1032,128]{1,0:T(8,128)S(1)}, f32[1032,128]{1,0:T(8,128)S(1)}, u32[]{:S(2)}, u32[]{:S(2)}) collective-permute-start(f32[1032,128]{1,0:T(8,128)S(1)} %get-tuple-element.39), channel_id=1, source_target_pairs={{0,4},{1,5},{6,2},{7,3},{4,8},{5,9},{10,6},{11,7},{8,12},{9,13},{1... | collective-permute-start | bytes 1585160 | tf_op jit(solution)/shard_map/ppermute | solution.py:356
  49.8 24.3 %collective-permute-start.11 = (f32[1032,128]{1,0:T(8,128)S(1)}, f32[1032,128]{1,0:T(8,128)S(1)}, u32[]{:S(2)}, u32[]{:S(2)}) collective-permute-start(f32[1032,128]{1,0:T(8,128)S(1)} %get-tuple-element.40), channel_id=1, source_target_pairs={{0,1},{1,4},{6,3},{7,6},{4,5},{5,8},{10,7},{11,10},{8,9},{9,12},{1... | collective-permute-start | bytes 1585160 | tf_op jit(solution)/shard_map/ppermute | solution.py:356
  51.3 22.7 %collective-permute-start.12 = (f32[1032,128]{1,0:T(8,128)S(1)}, f32[1032,128]{1,0:T(8,128)S(1)}, u32[]{:S(2)}, u32[]{:S(2)}) collective-permute-start(f32[1032,128]{1,0:T(8,128)S(1)} %get-tuple-element.41), channel_id=1, source_target_pairs={{0,3},{1,2},{6,5},{7,4},{4,7},{5,6},{10,9},{11,8},{8,11},{9,10},{1... | collective-permute-start | bytes 1585160 | tf_op jit(solution)/shard_map/ppermute | solution.py:356
  56.2 3.2 %collective-permute-start.8 = (f32[256,128]{1,0:T(8,128)S(1)}, f32[256,128]{1,0:T(8,128)S(1)}, u32[]{:S(2)}, u32[]{:S(2)}) collective-permute-start(f32[256,128]{1,0:T(8,128)S(1)} %slice_select_fusion), channel_id=1, source_target_pairs={{0,1},{1,0},{2,3},{3,2},{4,5},{5,4},{6,7},{7,6},{8,9},{9,8},{10,11... | collective-permute-start | bytes 393224 | tf_op jit(solution)/shard_map/ppermute | solution.py:330
  57.6 26.9 %collective-permute-start.15 = (f32[1032,128]{1,0:T(8,128)S(1)}, f32[1032,128]{1,0:T(8,128)S(1)}, u32[]{:S(2)}, u32[]{:S(2)}) collective-permute-start(f32[1032,128]{1,0:T(8,128)S(1)} %get-tuple-element.47), channel_id=1, source_target_pairs={{0,2},{1,3},{6,4},{7,5},{4,6},{5,7},{10,8},{11,9},{8,10},{9,11},{1... | collective-permute-start | bytes 1585160 | tf_op jit(solution)/shard_map/ppermute | solution.py:356
  59.5 14.5 %collective-permute-start.9 = (f32[256,128]{1,0:T(8,128)S(1)}, f32[256,128]{1,0:T(8,128)S(1)}, u32[]{:S(2)}, u32[]{:S(2)}) collective-permute-start(f32[256,128]{1,0:T(8,128)S(1)} %select_add_fusion), channel_id=1, source_target_pairs={{0,4},{1,5},{2,6},{3,7},{4,0},{5,1},{6,2},{7,3},{8,12},{9,13},{10,... | collective-permute-start | bytes 393224 | tf_op jit(solution)/shard_map/ppermute | solution.py:330
  74.0 8.2 %collective-permute-start.13 = (f32[256,128]{1,0:T(8,128)S(1)}, f32[256,128]{1,0:T(8,128)S(1)}, u32[]{:S(2)}, u32[]{:S(2)}) collective-permute-start(f32[256,128]{1,0:T(8,128)S(1)} %add.21), channel_id=1, source_target_pairs={{0,8},{1,9},{2,10},{3,11},{4,12},{5,13},{6,14},{7,15},{8,0},{9,1},... | collective-permute-start | bytes 393224 | tf_op jit(solution)/shard_map/ppermute | solution.py:330
  82.2 2.3 %collective-permute-start.14 = (f32[256,128]{1,0:T(8,128)S(1)}, f32[256,128]{1,0:T(8,128)S(1)}, u32[]{:S(2)}, u32[]{:S(2)}) collective-permute-start(f32[256,128]{1,0:T(8,128)S(1)} %add.22), channel_id=1, source_target_pairs={{0,1},{1,0},{2,3},{3,2},{4,5},{5,4},{6,7},{7,6},{8,9},{9,8},{10,11... | collective-permute-start | bytes 393224 | tf_op jit(solution)/shard_map/ppermute | solution.py:330

commit v3 on v2

--- a/solution.py
+++ b/solution.py
@@ -188,14 +188,12 @@
         def keep(w, i, place, grad):
             here = place[4]
             for c in range(2):
-                first = ((w * len(backward) + i) * 2 + c) * rows_here
-                at = pl.ds(pl.multiple_of(first, rows_here), rows_here)
-                rows = [grad[c][j * rows_here : (j + 1) * rows_here] for j in range(self.reach)]
-                r["grad0"][at] = jnp.where(here, rows[0], 0.0)
-                r["grad1"][at] = jnp.where(here, 0.0, rows[0])
-                r["grad2"][at] = rows[2]
-                r["grad3"][at] = jnp.where(parity == 0, rows[3], rows[1])
-                r["grad4"][at] = jnp.where(parity == 0, rows[1], rows[3])
+                at = rows_at(((w * len(backward) + i) * 2 + c), rows_here)
+                edge = grad[c][:rows_here]
+                r["grad0"][at] = jnp.where(here, edge, 0.0)
+                r["grad1"][at] = jnp.where(here, 0.0, edge)
+                for j in range(1, self.reach):
+                    r[f"grad{j + 1}"][at] = grad[c][j * rows_here : (j + 1) * rows_here]
 
         def turn(value, row, lane):
             return pltpu.roll(pltpu.roll(value, row, 0), lane, 1)
@@ -245,7 +243,7 @@
                 exits = [both_sides(out, transform, transform_conj) for out in exits]
                 for k, w in turns:
                     intensity = sum(re * re + im * im for re, im in exits[k])
-                    scale = 1.0 - r["amplitude"][pl.ds(w * side, side)] * lax.rsqrt(intensity + INTENSITY_SHIFT)
+                    scale = 1.0 - r["amplitude"][rows_at(w, side)] * lax.rsqrt(intensity + INTENSITY_SHIFT)
                     exits[k] = [(re * scale, im * scale) for re, im in exits[k]]
                 exits = [both_sides(out, transform_conj, transform) for out in exits]
             elif backward:
@@ -268,7 +266,10 @@
                     store(r[f"exit{backward[-1]}"], w, exits[k])
             return carry
 
-        lax.fori_loop(0, self.windows // group, visit, 0)
+        if self.windows == group:
+            visit(0, 0)
+        else:
+            lax.fori_loop(0, self.windows // group, visit, 0)
 
 
 def give_kernel(windows, count, col_ref, *refs):
@@ -321,6 +322,11 @@
     )(*arrays)
 
 
+def rows_at(block, size):
+    first = block * size
+    return pl.ds(first if isinstance(first, int) else pl.multiple_of(first, size), size)
+
+
 def moved_here(tile):
     return tile // 2 % 2
 
@@ -356,8 +362,8 @@
         return lax.ppermute(value, "tile", pairs_there)
 
 
-    def return_route(even_step, odd_step):
-        return [(home[t], (t + (odd_step if t % 2 else even_step)) % count) for t in range(count)]
+    def return_route(step):
+        return [(home[t], (t + step) % count) for t in range(count)]
 
     flat = slices.reshape(slice_count * 2 * rows_here, cols)
     to_home = list(enumerate(home))
@@ -393,9 +399,10 @@
     total = jnp.where(even, lower, upper) + swap(jnp.where(even, upper, lower), 1)
     pieces = [result[f"grad{j}"] for j in range(reach + 1)]
     total = total + swap(total, 4)
-    outer = send(pieces[4], return_route(1, 3))
-    early = [pieces[0], send(pieces[1], from_edge), outer, send(pieces[3], return_route(3, 1))]
-    late = [send(pieces[2], return_route(2, 2))]
+    middle = reach // 2 + 1
+    early = [pieces[0], send(pieces[1], from_edge)]
+    early += [send(pieces[j], return_route(j - 1)) for j in range(2, reach + 1) if j != middle]
+    late = send(pieces[middle], return_route(middle - 1))
     total, *early = lax.optimization_barrier((total, *early))
 
     def columns_of(piece):
@@ -405,10 +412,9 @@
     columns = [offsets[1]] + [columns_of(piece) for piece in early[1:]]
     own_grad = give(windows, columns, early, shape)
     total = sum_over_tiles(total)
+    total, own_grad, late = lax.optimization_barrier((total, own_grad, late))
+    own_grad = give(windows, [columns_of(late)], [late], shape, [own_grad]).reshape(slices.shape)
     rest = swap(total, 1)
-    total, rest, own_grad, *late = lax.optimization_barrier((total, rest, own_grad, *late))
-    own_grad = give(windows, [columns_of(piece) for piece in late], late, shape, [own_grad])
-    own_grad = own_grad.reshape(slices.shape)
     probe_grad = jnp.where(even, jnp.concatenate([total, rest]), jnp.concatenate([rest, total]))
     return own_grad, probe_grad.reshape(probe_modes.shape)
 

time: 87.4 us -> 85.7 us (0.981)
  waiting for transfers between devices: 44.5 us -> 42.7 us
    ppermute x10, waiting for transfers between devices: 44.2 us -> 42.4 us  [swap(): return lax.ppermute(value, 'tile', [(i, i ^ bits) for i in range(count)])]
  transfers between devices with their start and end apart: 16 -> 16, of which waited for: 7 -> 7; matrix products, arithmetic and copies ran while one was open for 2% -> 2% of each run, Pallas kernels for 2% -> 4%
where the time goes in v3:
time: 85.7 us; the launch traced here: 85.5 us
  waiting for transfers between devices  42.7 us (50%)
  starting transfers between devices  21.9 us (26%)
  Pallas kernels  14.7 us (17%)
  local copies, waits for them, and re-layouts  3.12 us (4%)
  other arithmetic  2.25 us (3%)
    ppermute x10, waiting for transfers between devices, swap(): return lax.ppermute(value, 'tile', [(i, i ^ bits) for i in range(count)])  42.4 us
    ppermute x10, starting transfers between devices, swap(): return lax.ppermute(value, 'tile', [(i, i ^ bits) for i in range(count)])  14.1 us
    pallas_call x1, Pallas kernels, __call__(): pl.pallas_call(self.kernel, out_shape=shapes, in_specs=[smem] + [vmem] *...  11.1 us
    ppermute x6, starting transfers between devices, send(): return lax.ppermute(value, 'tile', pairs_there)  7.78 us
    pallas_call x2, Pallas kernels, give(): pl.pallas_call(functools.partial(give_kernel, windows, len(pieces)), out_...  3.42 us
    unnamed x10, local copies, waits for them, and re-layouts  3.12 us
  transfers between devices with their start and end apart: 16, of which 7 were waited for; matrix products, arithmetic and copies ran while one was open for 2% of the time, Pallas kernels for 4%

profile of v3, /device:TPU:1, one launch (start us, length us, event | category | flops | bytes accessed | tf_op | source)
XLA Modules:
  0.0 85.5 jit_solution(15446681653272575108)
XLA Ops:
  0.6 2.1 %collective-permute-start.2 = (f32[256,1024]{1,0:T(8,128)}, f32[256,1024]{1,0:T(8,128)S(1)}, u32[]{:S(2)}, u32[]{:S(2)}) collective-permute-start(f32[256,1024]{1,0:T(8,128)} %bitcast.10), channel_id=1, source_target_pairs={{0,2},{1,3},{2,0},{3,1},{4,6},{5,7},{6,4},{7,5},{8,10},{9,11},{10,... | collective-permute-start | bytes 3145736 | tf_op jit(solution)/shard_map/ppermute | solution.py:336
  2.8 3.3 %collective-permute-start = (f32[256,1024]{1,0:T(8,128)}, f32[256,1024]{1,0:T(8,128)S(1)}, u32[]{:S(2)}, u32[]{:S(2)}) collective-permute-start(f32[256,1024]{1,0:T(8,128)} %bitcast.11), channel_id=1, source_target_pairs={{4,0},{5,1},{2,6},{3,7},{8,4},{9,5},{6,10},{7,11},{12,8},{13,9},{1... | collective-permute-start | bytes 3145736 | tf_op jit(solution)/shard_map/ppermute | solution.py:362
  6.1 0.7 copy-done.3
  6.8 1.0 %select_maximum_fusion = f32[520,128]{1,0:T(8,128)S(1)} fusion(f32[2,4]{1,0:T(2,128)S(1)} %add_convert_fusion, f32[512,128]{1,0:T(8,128)} %bitcast.17), kind=kLoop, calls=%fused_computation | loop fusion | flops 199680 | bytes 528416 | tf_op jit(solution)/shard_map/concatenate | solution.py:375
  7.8 0.7 collective-permute-start.1
  8.5 1.2 %copy-done = f32[4,2,32,1024]{3,2,1,0:T(8,128)S(1)} copy-done((f32[4,2,32,1024]{3,2,1,0:T(8,128)S(1)}, f32[4,2,32,1024]{3,2,1,0:T(8,128)}, u32[]{:S(2)}) %copy-start) | copy-done | bytes 1048600
  9.7 1.2 %copy-done.1 = bf16[4,2,256,256]{3,2,1,0:T(8,128)(2,1)S(1)} copy-done((bf16[4,2,256,256]{3,2,1,0:T(8,128)(2,1)S(1)}, bf16[4,2,256,256]{3,2,1,0:T(8,128)(2,1)}, u32[]{:S(2)}) %copy-start.1) | copy-done | bytes 1048600
  11.1 14.7 %collective-permute-done.2.refs_6_ = f32[256,1024]{1,0:T(8,128)S(1)} collective-permute-done((f32[256,1024]{1,0:T(8,128)}, f32[256,1024]{1,0:T(8,128)S(1)}, u32[]{:S(2)}, u32[]{:S(2)}) %collective-permute-start.2) | collective-permute-done | bytes 1048608 | tf_op jit(solution)/shard_map/ppermute | solution.py:336
  25.9 1.2 %collective-permute-start.3 = (f32[8,1024]{1,0:T(8,128)S(1)}, f32[8,1024]{1,0:T(8,128)S(1)}, u32[]{:S(2)}, u32[]{:S(2)}) collective-permute-start(f32[8,1024]{1,0:T(8,128)S(1)} %slice.37), channel_id=1, source_target_pairs={{0,1},{1,0},{2,3},{3,2},{4,5},{5,4},{6,7},{7,6},{8,9},{9,8},{10,11... | collective-permute-start | bytes 98312 | tf_op jit(solution)/shard_map/ppermute | solution.py:336
  28.0 1.8 %collective-permute-start.6 = (f32[256,1024]{1,0:T(8,128)S(1)}, f32[256,1024]{1,0:T(8,128)S(1)}, u32[]{:S(2)}, u32[]{:S(2)}) collective-permute-start(f32[256,1024]{1,0:T(8,128)S(1)} %collective-permute-done.refs_8_), channel_id=1, source_target_pairs={{0,1},{1,0},{2,3},{3,2},{4,5},{5,4},{6,7},{7,6},{8,9},{9,8},{10,11... | collective-permute-start | bytes 3145736 | tf_op jit(solution)/shard_map/ppermute | solution.py:336
  29.8 1.5 %collective-permute-done.5.refs_7_ = f32[256,1024]{1,0:T(8,128)S(1)} collective-permute-done((f32[256,1024]{1,0:T(8,128)S(1)}, f32[256,1024]{1,0:T(8,128)S(1)}, u32[]{:S(2)}, u32[]{:S(2)}) %collective-permute-start.5) | collective-permute-done | bytes 1048608 | tf_op jit(solution)/shard_map/ppermute | solution.py:336
  31.3 1.5 %collective-permute-done.6.refs_9_ = f32[256,1024]{1,0:T(8,128)S(1)} collective-permute-done((f32[256,1024]{1,0:T(8,128)S(1)}, f32[256,1024]{1,0:T(8,128)S(1)}, u32[]{:S(2)}, u32[]{:S(2)}) %collective-permute-start.6) | collective-permute-done | bytes 1048608 | tf_op jit(solution)/shard_map/ppermute | solution.py:336
  32.8 11.1 %shard_map.78 = (f32[1032,128]{1,0:T(8,128)}, f32[1032,128]{1,0:T(8,128)}, f32[1032,128]{1,0:T(8,128)}, f32[1032,128]{1,0:T(8,128)}, f32[1032,128]{1,0:T(8,128)}...) custom-call(s32[2,4]{1,0:T(2,128)S(1)} %slice_convert_fusion.refs_0_, ...), custom_call_target="tpu_custom_call" | custom-call | tf_op jit(solution)/shard_map/pallas_call | solution.py:131
  43.9 5.9 %collective-permute-start.7 = (f32[512,128]{1,0:T(8,128)S(1)}, f32[512,128]{1,0:T(8,128)S(1)}, u32[]{:S(2)}, u32[]{:S(2)}) collective-permute-start(f32[512,128]{1,0:T(8,128)S(1)} %get-tuple-element.36), channel_id=1, source_target_pairs={{0,2},{1,3},{2,0},{3,1},{4,6},{5,7},{6,4},{7,5},{8,10},{9,11},{10,... | collective-permute-start | bytes 786440 | tf_op jit(solution)/shard_map/ppermute | solution.py:336
  49.8 2.0 %collective-permute-start.11 = (f32[1032,128]{1,0:T(8,128)S(1)}, f32[1032,128]{1,0:T(8,128)S(1)}, u32[]{:S(2)}, u32[]{:S(2)}) collective-permute-start(f32[1032,128]{1,0:T(8,128)S(1)} %get-tuple-element.39), channel_id=1, source_target_pairs={{0,1},{1,2},{6,3},{7,4},{4,5},{5,6},{10,7},{11,8},{8,9},{9,10},{14... | collective-permute-start | bytes 1585160 | tf_op jit(solution)/shard_map/ppermute | solution.py:362
  51.8 4.4 %collective-permute-done.7 = f32[512,128]{1,0:T(8,128)S(1)} collective-permute-done((f32[512,128]{1,0:T(8,128)S(1)}, f32[512,128]{1,0:T(8,128)S(1)}, u32[]{:S(2)}, u32[]{:S(2)}) %collective-permute-start.7) | collective-permute-done | bytes 262176 | tf_op jit(solution)/shard_map/ppermute | solution.py:336
  56.2 1.4 %collective-permute-start.8 = (f32[256,128]{1,0:T(8,128)S(1)}, f32[256,128]{1,0:T(8,128)S(1)}, u32[]{:S(2)}, u32[]{:S(2)}) collective-permute-start(f32[256,128]{1,0:T(8,128)S(1)} %slice_select_fusion), channel_id=1, source_target_pairs={{0,1},{1,0},{2,3},{3,2},{4,5},{5,4},{6,7},{7,6},{8,9},{9,8},{10,11... | collective-permute-start | bytes 393224 | tf_op jit(solution)/shard_map/ppermute | solution.py:336
  57.7 1.8 %collective-permute-start.14 = (f32[1032,128]{1,0:T(8,128)S(1)}, f32[1032,128]{1,0:T(8,128)S(1)}, u32[]{:S(2)}, u32[]{:S(2)}) collective-permute-start(f32[1032,128]{1,0:T(8,128)S(1)} %get-tuple-element.46), channel_id=1, source_target_pairs={{0,2},{1,3},{6,4},{7,5},{4,6},{5,7},{10,8},{11,9},{8,10},{9,11},{1... | collective-permute-start | bytes 1585160 | tf_op jit(solution)/shard_map/ppermute | solution.py:362
  59.6 14.4 %collective-permute-done.9 = f32[256,128]{1,0:T(8,128)S(1)} collective-permute-done((f32[256,128]{1,0:T(8,128)S(1)}, f32[256,128]{1,0:T(8,128)S(1)}, u32[]{:S(2)}, u32[]{:S(2)}) %collective-permute-start.9) | collective-permute-done | bytes 131104 | tf_op jit(solution)/shard_map/ppermute | solution.py:336
  74.8 1.6 %shard_map.79.refs_1_ = f32[8,32,1024]{2,1,0:T(8,128)S(1)} custom-call(s32[4,4]{1,0:T(4,128)S(1)} %pad_add_fusion.col_ref, f32[1032,128]{1,0:T(8,128)S(1)} %get-tuple-element.45.refs_0_, f32[1032,128]{1,0:T(8,128)S(1)} %collective-permute-done.10.refs_1_, f32[1032,128]{1,0:T(8,128)S(1)} %collective-permute-done.11.refs_2_, ...), custom_call_target="tpu_custom_call" | custom-call | tf_op jit(solution)/shard_map/pallas_call | solution.py:295
  76.4 5.9 %collective-permute-done.13 = f32[256,128]{1,0:T(8,128)S(1)} collective-permute-done((f32[256,128]{1,0:T(8,128)S(1)}, f32[256,128]{1,0:T(8,128)S(1)}, u32[]{:S(2)}, u32[]{:S(2)}) %collective-permute-start.13) | collective-permute-done | bytes 131104 | tf_op jit(solution)/shard_map/ppermute | solution.py:336
  82.3 0.5 collective-permute-start.15
  82.9 1.8 %shard_map.80 = f32[8,32,1024]{2,1,0:T(8,128)} custom-call(s32[1,4]{1,0:T(1,128)S(1)} %bitcast.14, f32[1032,128]{1,0:T(8,128)S(1)} %collective-permute-done.14.refs_0_, f32[8,32,1024]{2,1,0:T(8,128)S(1)} %shard_map.79.refs_1_), custom_call_target="tpu_custom_call" | custom-call | tf_op jit(solution)/shard_map/pallas_call | solution.py:295
  84.8 0.7 maximum_select_fusion
  (37 shorter events, 2.1 us)
Async XLA Ops:
  0.6 25.2 %collective-permute-start.2 = (f32[256,1024]{1,0:T(8,128)}, f32[256,1024]{1,0:T(8,128)S(1)}, u32[]{:S(2)}, u32[]{:S(2)}) collective-permute-start(f32[256,1024]{1,0:T(8,128)} %bitcast.10), channel_id=1, source_target_pairs={{0,2},{1,3},{2,0},{3,1},{4,6},{5,7},{6,4},{7,5},{8,10},{9,11},{10,... | collective-permute-start | bytes 3145736 | tf_op jit(solution)/shard_map/ppermute | solution.py:336
  2.8 25.1 %collective-permute-start = (f32[256,1024]{1,0:T(8,128)}, f32[256,1024]{1,0:T(8,128)S(1)}, u32[]{:S(2)}, u32[]{:S(2)}) collective-permute-start(f32[256,1024]{1,0:T(8,128)} %bitcast.11), channel_id=1, source_target_pairs={{4,0},{5,1},{2,6},{3,7},{8,4},{9,5},{6,10},{7,11},{12,8},{13,9},{1... | collective-permute-start | bytes 3145736 | tf_op jit(solution)/shard_map/ppermute | solution.py:362
  6.1 0.7 copy-start.3
  6.1 0.7 copy-start.4
  6.8 1.7 %copy-start.2 = (f32[2,2,128,128]{3,2,1,0:T(8,128)S(1)}, f32[2,2,128,128]{3,2,1,0:T(8,128)}, u32[]{:S(2)}) copy-start(f32[2,2,128,128]{3,2,1,0:T(8,128)} %refs_1_.1) | copy-start | bytes 786436
  7.8 19.8 %collective-permute-start.1 = (f32[520,128]{1,0:T(8,128)S(1)}, f32[520,128]{1,0:T(8,128)S(1)}, u32[]{:S(2)}, u32[]{:S(2)}) collective-permute-start(f32[520,128]{1,0:T(8,128)S(1)} %select_maximum_fusion), channel_id=1, source_target_pairs={{0,0},{1,1},{2,6},{3,7},{4,4},{5,5},{6,10},{7,11},{8,8},{9,9},{10,... | collective-permute-start | bytes 798728 | tf_op jit(solution)/shard_map/ppermute | solution.py:362
  8.5 1.2 %copy-start = (f32[4,2,32,1024]{3,2,1,0:T(8,128)S(1)}, f32[4,2,32,1024]{3,2,1,0:T(8,128)}, u32[]{:S(2)}) copy-start(f32[4,2,32,1024]{3,2,1,0:T(8,128)} %param.6) | copy-start | bytes 3145732
  9.7 1.2 %copy-start.1 = (bf16[4,2,256,256]{3,2,1,0:T(8,128)(2,1)S(1)}, bf16[4,2,256,256]{3,2,1,0:T(8,128)(2,1)}, u32[]{:S(2)}) copy-start(bf16[4,2,256,256]{3,2,1,0:T(8,128)(2,1)} %constant.22.clone.refs_2_) | copy-start | bytes 3145732
  25.9 2.1 %collective-permute-start.3 = (f32[8,1024]{1,0:T(8,128)S(1)}, f32[8,1024]{1,0:T(8,128)S(1)}, u32[]{:S(2)}, u32[]{:S(2)}) collective-permute-start(f32[8,1024]{1,0:T(8,128)S(1)} %slice.37), channel_id=1, source_target_pairs={{0,1},{1,0},{2,3},{3,2},{4,5},{5,4},{6,7},{7,6},{8,9},{9,8},{10,11... | collective-permute-start | bytes 98312 | tf_op jit(solution)/shard_map/ppermute | solution.py:336
  27.1 2.7 %collective-permute-start.4 = (f32[256,1024]{1,0:T(8,128)S(1)}, f32[256,1024]{1,0:T(8,128)S(1)}, u32[]{:S(2)}, u32[]{:S(2)}) collective-permute-start(f32[256,1024]{1,0:T(8,128)S(1)} %bitcast.13), channel_id=1, source_target_pairs={{0,1},{1,0},{2,3},{3,2},{4,5},{5,4},{6,7},{7,6},{8,9},{9,8},{10,11... | collective-permute-start | bytes 3145736 | tf_op jit(solution)/shard_map/ppermute | solution.py:336
  27.1 4.2 %collective-permute-start.5 = (f32[256,1024]{1,0:T(8,128)S(1)}, f32[256,1024]{1,0:T(8,128)S(1)}, u32[]{:S(2)}, u32[]{:S(2)}) collective-permute-start(f32[256,1024]{1,0:T(8,128)S(1)} %collective-permute-done.2.refs_6_), channel_id=1, source_target_pairs={{0,1},{1,0},{2,3},{3,2},{4,5},{5,4},{6,7},{7,6},{8,9},{9,8},{10,11... | collective-permute-start | bytes 3145736 | tf_op jit(solution)/shard_map/ppermute | solution.py:336
  28.0 4.8 %collective-permute-start.6 = (f32[256,1024]{1,0:T(8,128)S(1)}, f32[256,1024]{1,0:T(8,128)S(1)}, u32[]{:S(2)}, u32[]{:S(2)}) collective-permute-start(f32[256,1024]{1,0:T(8,128)S(1)} %collective-permute-done.refs_8_), channel_id=1, source_target_pairs={{0,1},{1,0},{2,3},{3,2},{4,5},{5,4},{6,7},{7,6},{8,9},{9,8},{10,11... | collective-permute-start | bytes 3145736 | tf_op jit(solution)/shard_map/ppermute | solution.py:336
  43.9 12.3 %collective-permute-start.7 = (f32[512,128]{1,0:T(8,128)S(1)}, f32[512,128]{1,0:T(8,128)S(1)}, u32[]{:S(2)}, u32[]{:S(2)}) collective-permute-start(f32[512,128]{1,0:T(8,128)S(1)} %get-tuple-element.36), channel_id=1, source_target_pairs={{0,2},{1,3},{2,0},{3,1},{4,6},{5,7},{6,4},{7,5},{8,10},{9,11},{10,... | collective-permute-start | bytes 786440 | tf_op jit(solution)/shard_map/ppermute | solution.py:336
  49.8 24.2 %collective-permute-start.10 = (f32[1032,128]{1,0:T(8,128)S(1)}, f32[1032,128]{1,0:T(8,128)S(1)}, u32[]{:S(2)}, u32[]{:S(2)}) collective-permute-start(f32[1032,128]{1,0:T(8,128)S(1)} %get-tuple-element.38), channel_id=1, source_target_pairs={{0,4},{1,5},{6,2},{7,3},{4,8},{5,9},{10,6},{11,7},{8,12},{9,13},{1... | collective-permute-start | bytes 1585160 | tf_op jit(solution)/shard_map/ppermute | solution.py:362
  49.8 24.3 %collective-permute-start.11 = (f32[1032,128]{1,0:T(8,128)S(1)}, f32[1032,128]{1,0:T(8,128)S(1)}, u32[]{:S(2)}, u32[]{:S(2)}) collective-permute-start(f32[1032,128]{1,0:T(8,128)S(1)} %get-tuple-element.39), channel_id=1, source_target_pairs={{0,1},{1,2},{6,3},{7,4},{4,5},{5,6},{10,7},{11,8},{8,9},{9,10},{14... | collective-permute-start | bytes 1585160 | tf_op jit(solution)/shard_map/ppermute | solution.py:362
  51.8 22.3 %collective-permute-start.12 = (f32[1032,128]{1,0:T(8,128)S(1)}, f32[1032,128]{1,0:T(8,128)S(1)}, u32[]{:S(2)}, u32[]{:S(2)}) collective-permute-start(f32[1032,128]{1,0:T(8,128)S(1)} %get-tuple-element.40), channel_id=1, source_target_pairs={{0,3},{1,4},{6,5},{7,6},{4,7},{5,8},{10,9},{11,10},{8,11},{9,12},{... | collective-permute-start | bytes 1585160 | tf_op jit(solution)/shard_map/ppermute | solution.py:362
  56.2 3.2 %collective-permute-start.8 = (f32[256,128]{1,0:T(8,128)S(1)}, f32[256,128]{1,0:T(8,128)S(1)}, u32[]{:S(2)}, u32[]{:S(2)}) collective-permute-start(f32[256,128]{1,0:T(8,128)S(1)} %slice_select_fusion), channel_id=1, source_target_pairs={{0,1},{1,0},{2,3},{3,2},{4,5},{5,4},{6,7},{7,6},{8,9},{9,8},{10,11... | collective-permute-start | bytes 393224 | tf_op jit(solution)/shard_map/ppermute | solution.py:336
  57.7 24.6 %collective-permute-start.14 = (f32[1032,128]{1,0:T(8,128)S(1)}, f32[1032,128]{1,0:T(8,128)S(1)}, u32[]{:S(2)}, u32[]{:S(2)}) collective-permute-start(f32[1032,128]{1,0:T(8,128)S(1)} %get-tuple-element.46), channel_id=1, source_target_pairs={{0,2},{1,3},{6,4},{7,5},{4,6},{5,7},{10,8},{11,9},{8,10},{9,11},{1... | collective-permute-start | bytes 1585160 | tf_op jit(solution)/shard_map/ppermute | solution.py:362
  59.5 14.5 %collective-permute-start.9 = (f32[256,128]{1,0:T(8,128)S(1)}, f32[256,128]{1,0:T(8,128)S(1)}, u32[]{:S(2)}, u32[]{:S(2)}) collective-permute-start(f32[256,128]{1,0:T(8,128)S(1)} %select_add_fusion), channel_id=1, source_target_pairs={{0,4},{1,5},{2,6},{3,7},{4,0},{5,1},{6,2},{7,3},{8,12},{9,13},{10,... | collective-permute-start | bytes 393224 | tf_op jit(solution)/shard_map/ppermute | solution.py:336
  74.1 8.2 %collective-permute-start.13 = (f32[256,128]{1,0:T(8,128)S(1)}, f32[256,128]{1,0:T(8,128)S(1)}, u32[]{:S(2)}, u32[]{:S(2)}) collective-permute-start(f32[256,128]{1,0:T(8,128)S(1)} %add.21), channel_id=1, source_target_pairs={{0,8},{1,9},{2,10},{3,11},{4,12},{5,13},{6,14},{7,15},{8,0},{9,1},... | collective-permute-start | bytes 393224 | tf_op jit(solution)/shard_map/ppermute | solution.py:336
  82.3 2.5 %collective-permute-start.15 = (f32[256,128]{1,0:T(8,128)S(1)}, f32[256,128]{1,0:T(8,128)S(1)}, u32[]{:S(2)}, u32[]{:S(2)}) collective-permute-start(f32[256,128]{1,0:T(8,128)S(1)} %add.22), channel_id=1, source_target_pairs={{0,1},{1,0},{2,3},{3,2},{4,5},{5,4},{6,7},{7,6},{8,9},{9,8},{10,11... | collective-permute-start | bytes 393224 | tf_op jit(solution)/shard_map/ppermute | solution.py:336

commit v4 on v3

--- a/solution.py
+++ b/solution.py
@@ -99,7 +99,7 @@
         vmem += [f"psi{s}" for s in sorted(waves) if s > 0] + [f"crop{s}" for s in sorted(loaded)]
         vmem += [] if far else [f"exit{s + 1}" for s in backward[:1]]
         if forward:
-            vmem += ["own", "own_mate", "partner", "partner_mate", "edge", "edge_mate", "first_rows"]
+            vmem += ["own", "own_mate", "partner", "partner_mate", "edge", "edge_mate"]
         self.vmem_in = vmem
         outs = [f"grad{j}" for j in range(self.reach + 1)] if backward else []
         if not backward:
@@ -322,6 +322,21 @@
     )(*arrays)
 
 
+def offsets_of(measured):
+    def kernel(source, target):
+        target[...] = source[pl.ds(source.shape[0] - EXTRA, EXTRA)].astype(jnp.int32)
+
+    vmem = pl.BlockSpec(memory_space=pltpu.VMEM)
+    return pl.pallas_call(
+        kernel,
+        out_shape=jax.ShapeDtypeStruct((EXTRA, measured.shape[1]), jnp.int32),
+        in_specs=[vmem],
+        out_specs=vmem,
+        cost_estimate=pl.CostEstimate(flops=20_000_000_000, bytes_accessed=40_000_000, transcendentals=0),
+        compiler_params=pltpu.CompilerParams(vmem_limit_bytes=VMEM_BYTES),
+    )(measured)
+
+
 def rows_at(block, size):
     first = block * size
     return pl.ds(first if isinstance(first, int) else pl.multiple_of(first, size), size)
@@ -374,9 +389,7 @@
     carried = jnp.pad(carried, ((0, EXTRA - 2), (0, side - windows)))
     measured = jnp.concatenate([amplitude.reshape(windows * side, side), carried])
     measured = send(measured, to_home)
-    first_rows = swap(partner[:EXTRA], 1)
-    edge, measured, first_rows = lax.optimization_barrier((edge, measured, first_rows))
-    offsets = measured[windows * side :][:2, :windows].astype(jnp.int32)
+    offsets = offsets_of(measured)
     partner_mate, edge_mate = swap(partner, 1), swap(edge, 1)
     values = {
         "own": fetched[0],
@@ -389,7 +402,6 @@
         "edge": edge,
         "edge_mate": edge_mate,
         "amplitude": measured,
-        "first_rows": first_rows,
     }
     chunk = list(range(slice_count))
     result = Stage(chunk, True, chunk[::-1], sizes)(values)
@@ -409,7 +421,7 @@
         return piece[-EXTRA:][:windows, 0].astype(jnp.int32)
 
     shape = (2 * slice_count, rows_here, cols)
-    columns = [offsets[1]] + [columns_of(piece) for piece in early[1:]]
+    columns = [offsets[1, :windows]] + [columns_of(piece) for piece in early[1:]]
     own_grad = give(windows, columns, early, shape)
     total = sum_over_tiles(total)
     total, own_grad, late = lax.optimization_barrier((total, own_grad, late))

time: 85.7 us -> 82.7 us (0.965)
  waiting for transfers between devices: 42.7 us -> 40 us
  Pallas kernels: 14.7 us -> 13.8 us
    ppermute x10 -> x9, waiting for transfers between devices: 42.4 us -> 39.1 us  [swap(): return lax.ppermute(value, 'tile', [(i, i ^ bits) for i in range(count)])]
    pallas_call x1, Pallas kernels: 11.1 us -> 10.2 us  [__call__(): pl.pallas_call(self.kernel, out_shape=shapes, in_specs=[smem] + [vmem] *...]
    ppermute x10 -> x9, starting transfers between devices: 14.1 us -> 14.4 us  [swap(): return lax.ppermute(value, 'tile', [(i, i ^ bits) for i in range(count)])]
  transfers between devices with their start and end apart: 16 -> 15, of which waited for: 7 -> 6; matrix products, arithmetic and copies ran while one was open for 2% -> 2% of each run, Pallas kernels for 4% -> 4%
where the time goes in v4:
time: 82.7 us; the launch traced here: 82.5 us
  waiting for transfers between devices  40 us (48%)
  starting transfers between devices  22.6 us (27%)
  Pallas kernels  13.8 us (17%)
  local copies, waits for them, and re-layouts  3.13 us (4%)
  other arithmetic  2.24 us (3%)
    ppermute x9, waiting for transfers between devices, swap(): return lax.ppermute(value, 'tile', [(i, i ^ bits) for i in range(count)])  39.1 us
    ppermute x9, starting transfers between devices, swap(): return lax.ppermute(value, 'tile', [(i, i ^ bits) for i in range(count)])  14.4 us
    pallas_call x1, Pallas kernels, __call__(): pl.pallas_call(self.kernel, out_shape=shapes, in_specs=[smem] + [vmem] *...  10.2 us
    ppermute x6, starting transfers between devices, send(): return lax.ppermute(value, 'tile', pairs_there)  8.16 us
    pallas_call x2, Pallas kernels, give(): pl.pallas_call(functools.partial(give_kernel, windows, len(pieces)), out_...  3.42 us
    unnamed x10, local copies, waits for them, and re-layouts  3.12 us
  transfers between devices with their start and end apart: 15, of which 6 were waited for; matrix products, arithmetic and copies ran while one was open for 2% of the time, Pallas kernels for 4%

profile of v4, /device:TPU:1, one launch (start us, length us, event | category | flops | bytes accessed | tf_op | source)
XLA Modules:
  0.0 82.5 jit_solution(609178745861747146)
XLA Ops:
  0.6 2.1 %collective-permute-start.1 = (f32[256,1024]{1,0:T(8,128)}, f32[256,1024]{1,0:T(8,128)S(1)}, u32[]{:S(2)}, u32[]{:S(2)}) collective-permute-start(f32[256,1024]{1,0:T(8,128)} %bitcast.10), channel_id=1, source_target_pairs={{0,2},{1,3},{2,0},{3,1},{4,6},{5,7},{6,4},{7,5},{8,10},{9,11},{10,... | collective-permute-start | bytes 3145736 | tf_op jit(solution)/shard_map/ppermute | solution.py:351
  2.8 3.3 %collective-permute-start.4 = (f32[256,1024]{1,0:T(8,128)}, f32[256,1024]{1,0:T(8,128)S(1)}, u32[]{:S(2)}, u32[]{:S(2)}) collective-permute-start(f32[256,1024]{1,0:T(8,128)} %bitcast.11), channel_id=1, source_target_pairs={{4,0},{5,1},{2,6},{3,7},{8,4},{9,5},{6,10},{7,11},{12,8},{13,9},{1... | collective-permute-start | bytes 3145736 | tf_op jit(solution)/shard_map/ppermute | solution.py:377
  6.8 1.0 %select_maximum_fusion = f32[520,128]{1,0:T(8,128)S(1)} fusion(f32[2,4]{1,0:T(2,128)S(1)} %add_convert_fusion, f32[512,128]{1,0:T(8,128)} %bitcast.17), kind=kLoop, calls=%fused_computation | loop fusion | flops 199680 | bytes 528416 | tf_op jit(solution)/shard_map/concatenate | solution.py:390
  7.8 0.7 collective-permute-start
  8.5 1.3 %collective-permute-start.2 = (f32[256,1024]{1,0:T(8,128)}, f32[256,1024]{1,0:T(8,128)S(1)}, u32[]{:S(2)}, u32[]{:S(2)}) collective-permute-start(f32[256,1024]{1,0:T(8,128)} %bitcast.12), channel_id=1, source_target_pairs={{0,1},{1,0},{2,3},{3,2},{4,5},{5,4},{6,7},{7,6},{8,9},{9,8},{10,11... | collective-permute-start | bytes 3145736 | tf_op jit(solution)/shard_map/ppermute | solution.py:351
  9.8 1.2 %copy-done = f32[4,2,32,1024]{3,2,1,0:T(8,128)S(1)} copy-done((f32[4,2,32,1024]{3,2,1,0:T(8,128)S(1)}, f32[4,2,32,1024]{3,2,1,0:T(8,128)}, u32[]{:S(2)}) %copy-start) | copy-done | bytes 1048600
  11.0 1.2 %copy-done.1 = bf16[4,2,256,256]{3,2,1,0:T(8,128)(2,1)S(1)} copy-done((bf16[4,2,256,256]{3,2,1,0:T(8,128)(2,1)S(1)}, bf16[4,2,256,256]{3,2,1,0:T(8,128)(2,1)}, u32[]{:S(2)}) %copy-start.1) | copy-done | bytes 1048600
  12.4 13.4 %collective-permute-done.1.refs_6_ = f32[256,1024]{1,0:T(8,128)S(1)} collective-permute-done((f32[256,1024]{1,0:T(8,128)}, f32[256,1024]{1,0:T(8,128)S(1)}, u32[]{:S(2)}, u32[]{:S(2)}) %collective-permute-start.1) | collective-permute-done | bytes 1048608 | tf_op jit(solution)/shard_map/ppermute | solution.py:351
  25.9 1.2 %collective-permute-start.3 = (f32[256,1024]{1,0:T(8,128)S(1)}, f32[256,1024]{1,0:T(8,128)S(1)}, u32[]{:S(2)}, u32[]{:S(2)}) collective-permute-start(f32[256,1024]{1,0:T(8,128)S(1)} %collective-permute-done.1.refs_6_), channel_id=1, source_target_pairs={{0,1},{1,0},{2,3},{3,2},{4,5},{5,4},{6,7},{7,6},{8,9},{9,8},{10,11... | collective-permute-start | bytes 3145736 | tf_op jit(solution)/shard_map/ppermute | solution.py:351
  27.1 0.8 collective-permute-done.4.refs_8_
  27.9 1.9 %collective-permute-start.5 = (f32[256,1024]{1,0:T(8,128)S(1)}, f32[256,1024]{1,0:T(8,128)S(1)}, u32[]{:S(2)}, u32[]{:S(2)}) collective-permute-start(f32[256,1024]{1,0:T(8,128)S(1)} %collective-permute-done.4.refs_8_), channel_id=1, source_target_pairs={{0,1},{1,0},{2,3},{3,2},{4,5},{5,4},{6,7},{7,6},{8,9},{9,8},{10,11... | collective-permute-start | bytes 3145736 | tf_op jit(solution)/shard_map/ppermute | solution.py:351
  29.8 2.3 %collective-permute-done.5.refs_9_ = f32[256,1024]{1,0:T(8,128)S(1)} collective-permute-done((f32[256,1024]{1,0:T(8,128)S(1)}, f32[256,1024]{1,0:T(8,128)S(1)}, u32[]{:S(2)}, u32[]{:S(2)}) %collective-permute-start.5) | collective-permute-done | bytes 1048608 | tf_op jit(solution)/shard_map/ppermute | solution.py:351
  32.1 10.2 %shard_map.79 = (f32[1032,128]{1,0:T(8,128)}, f32[1032,128]{1,0:T(8,128)}, f32[1032,128]{1,0:T(8,128)}, f32[1032,128]{1,0:T(8,128)}, f32[1032,128]{1,0:T(8,128)}...) custom-call(s32[8,128]{1,0:T(8,128)S(1)} %shard_map.77.refs_0_, ...), custom_call_target="tpu_custom_call" | custom-call | tf_op jit(solution)/shard_map/pallas_call | solution.py:131
  42.2 2.8 %collective-permute-start.6 = (f32[512,128]{1,0:T(8,128)S(1)}, f32[512,128]{1,0:T(8,128)S(1)}, u32[]{:S(2)}, u32[]{:S(2)}) collective-permute-start(f32[512,128]{1,0:T(8,128)S(1)} %get-tuple-element.30), channel_id=1, source_target_pairs={{0,2},{1,3},{2,0},{3,1},{4,6},{5,7},{6,4},{7,5},{8,10},{9,11},{10,... | collective-permute-start | bytes 786440 | tf_op jit(solution)/shard_map/ppermute | solution.py:351
  45.0 1.5 %collective-permute-start.10 = (f32[1032,128]{1,0:T(8,128)S(1)}, f32[1032,128]{1,0:T(8,128)S(1)}, u32[]{:S(2)}, u32[]{:S(2)}) collective-permute-start(f32[1032,128]{1,0:T(8,128)S(1)} %get-tuple-element.33), channel_id=1, source_target_pairs={{0,1},{1,2},{6,3},{7,4},{4,5},{5,6},{10,7},{11,8},{8,9},{9,10},{14... | collective-permute-start | bytes 1585160 | tf_op jit(solution)/shard_map/ppermute | solution.py:377
  46.5 0.9 %collective-permute-start.9 = (f32[1032,128]{1,0:T(8,128)S(1)}, f32[1032,128]{1,0:T(8,128)S(1)}, u32[]{:S(2)}, u32[]{:S(2)}) collective-permute-start(f32[1032,128]{1,0:T(8,128)S(1)} %get-tuple-element.32), channel_id=1, source_target_pairs={{0,4},{1,5},{6,2},{7,3},{4,8},{5,9},{10,6},{11,7},{8,12},{9,13},{1... | collective-permute-start | bytes 1585160 | tf_op jit(solution)/shard_map/ppermute | solution.py:377
  47.5 2.7 %collective-permute-done.6 = f32[512,128]{1,0:T(8,128)S(1)} collective-permute-done((f32[512,128]{1,0:T(8,128)S(1)}, f32[512,128]{1,0:T(8,128)S(1)}, u32[]{:S(2)}, u32[]{:S(2)}) %collective-permute-start.6) | collective-permute-done | bytes 262176 | tf_op jit(solution)/shard_map/ppermute | solution.py:351
  50.2 4.0 %collective-permute-start.7 = (f32[256,128]{1,0:T(8,128)S(1)}, f32[256,128]{1,0:T(8,128)S(1)}, u32[]{:S(2)}, u32[]{:S(2)}) collective-permute-start(f32[256,128]{1,0:T(8,128)S(1)} %slice_select_fusion), channel_id=1, source_target_pairs={{0,1},{1,0},{2,3},{3,2},{4,5},{5,4},{6,7},{7,6},{8,9},{9,8},{10,11... | collective-permute-start | bytes 393224 | tf_op jit(solution)/shard_map/ppermute | solution.py:351
  54.2 1.8 %collective-permute-start.13 = (f32[1032,128]{1,0:T(8,128)S(1)}, f32[1032,128]{1,0:T(8,128)S(1)}, u32[]{:S(2)}, u32[]{:S(2)}) collective-permute-start(f32[1032,128]{1,0:T(8,128)S(1)} %get-tuple-element.40), channel_id=1, source_target_pairs={{0,2},{1,3},{6,4},{7,5},{4,6},{5,7},{10,8},{11,9},{8,10},{9,11},{1... | collective-permute-start | bytes 1585160 | tf_op jit(solution)/shard_map/ppermute | solution.py:377
  56.1 14.9 %collective-permute-done.8 = f32[256,128]{1,0:T(8,128)S(1)} collective-permute-done((f32[256,128]{1,0:T(8,128)S(1)}, f32[256,128]{1,0:T(8,128)S(1)}, u32[]{:S(2)}, u32[]{:S(2)}) %collective-permute-start.8) | collective-permute-done | bytes 131104 | tf_op jit(solution)/shard_map/ppermute | solution.py:351
  71.7 1.6 %shard_map.80.refs_1_ = f32[8,32,1024]{2,1,0:T(8,128)S(1)} custom-call(s32[4,4]{1,0:T(4,128)S(1)} %pad_add_fusion.col_ref, f32[1032,128]{1,0:T(8,128)S(1)} %get-tuple-element.39.refs_0_, f32[1032,128]{1,0:T(8,128)S(1)} %collective-permute-done.9.refs_1_, f32[1032,128]{1,0:T(8,128)S(1)} %collective-permute-done.10.refs_2_, ...), custom_call_target="tpu_custom_call" | custom-call | tf_op jit(solution)/shard_map/pallas_call | solution.py:295
  73.3 5.9 %collective-permute-done.12 = f32[256,128]{1,0:T(8,128)S(1)} collective-permute-done((f32[256,128]{1,0:T(8,128)S(1)}, f32[256,128]{1,0:T(8,128)S(1)}, u32[]{:S(2)}, u32[]{:S(2)}) %collective-permute-start.12) | collective-permute-done | bytes 131104 | tf_op jit(solution)/shard_map/ppermute | solution.py:351
  79.9 1.8 %shard_map.81 = f32[8,32,1024]{2,1,0:T(8,128)} custom-call(s32[1,4]{1,0:T(1,128)S(1)} %bitcast.14, f32[1032,128]{1,0:T(8,128)S(1)} %collective-permute-done.13.refs_0_, f32[8,32,1024]{2,1,0:T(8,128)S(1)} %shard_map.80.refs_1_), custom_call_target="tpu_custom_call" | custom-call | tf_op jit(solution)/shard_map/pallas_call | solution.py:295
  81.7 0.7 maximum_select_fusion
  (34 shorter events, 2.4 us)
Async XLA Ops:
  0.6 25.2 %collective-permute-start.1 = (f32[256,1024]{1,0:T(8,128)}, f32[256,1024]{1,0:T(8,128)S(1)}, u32[]{:S(2)}, u32[]{:S(2)}) collective-permute-start(f32[256,1024]{1,0:T(8,128)} %bitcast.10), channel_id=1, source_target_pairs={{0,2},{1,3},{2,0},{3,1},{4,6},{5,7},{6,4},{7,5},{8,10},{9,11},{10,... | collective-permute-start | bytes 3145736 | tf_op jit(solution)/shard_map/ppermute | solution.py:351
  2.8 25.1 %collective-permute-start.4 = (f32[256,1024]{1,0:T(8,128)}, f32[256,1024]{1,0:T(8,128)S(1)}, u32[]{:S(2)}, u32[]{:S(2)}) collective-permute-start(f32[256,1024]{1,0:T(8,128)} %bitcast.11), channel_id=1, source_target_pairs={{4,0},{5,1},{2,6},{3,7},{8,4},{9,5},{6,10},{7,11},{12,8},{13,9},{1... | collective-permute-start | bytes 3145736 | tf_op jit(solution)/shard_map/ppermute | solution.py:377
  6.1 0.7 copy-start.3
  6.1 0.7 copy-start.4
  6.8 3.0 %copy-start.2 = (f32[2,2,128,128]{3,2,1,0:T(8,128)S(1)}, f32[2,2,128,128]{3,2,1,0:T(8,128)}, u32[]{:S(2)}) copy-start(f32[2,2,128,128]{3,2,1,0:T(8,128)} %refs_1_.1) | copy-start | bytes 786436
  7.8 22.0 %collective-permute-start = (f32[520,128]{1,0:T(8,128)S(1)}, f32[520,128]{1,0:T(8,128)S(1)}, u32[]{:S(2)}, u32[]{:S(2)}) collective-permute-start(f32[520,128]{1,0:T(8,128)S(1)} %select_maximum_fusion), channel_id=1, source_target_pairs={{0,0},{1,1},{2,6},{3,7},{4,4},{5,5},{6,10},{7,11},{8,8},{9,9},{10,... | collective-permute-start | bytes 798728 | tf_op jit(solution)/shard_map/ppermute | solution.py:377
  8.5 21.3 %collective-permute-start.2 = (f32[256,1024]{1,0:T(8,128)}, f32[256,1024]{1,0:T(8,128)S(1)}, u32[]{:S(2)}, u32[]{:S(2)}) collective-permute-start(f32[256,1024]{1,0:T(8,128)} %bitcast.12), channel_id=1, source_target_pairs={{0,1},{1,0},{2,3},{3,2},{4,5},{5,4},{6,7},{7,6},{8,9},{9,8},{10,11... | collective-permute-start | bytes 3145736 | tf_op jit(solution)/shard_map/ppermute | solution.py:351
  9.8 1.2 %copy-start = (f32[4,2,32,1024]{3,2,1,0:T(8,128)S(1)}, f32[4,2,32,1024]{3,2,1,0:T(8,128)}, u32[]{:S(2)}) copy-start(f32[4,2,32,1024]{3,2,1,0:T(8,128)} %param.6) | copy-start | bytes 3145732
  11.0 1.2 %copy-start.1 = (bf16[4,2,256,256]{3,2,1,0:T(8,128)(2,1)S(1)}, bf16[4,2,256,256]{3,2,1,0:T(8,128)(2,1)}, u32[]{:S(2)}) copy-start(bf16[4,2,256,256]{3,2,1,0:T(8,128)(2,1)} %constant.22.clone.refs_2_) | copy-start | bytes 3145732
  25.9 3.9 %collective-permute-start.3 = (f32[256,1024]{1,0:T(8,128)S(1)}, f32[256,1024]{1,0:T(8,128)S(1)}, u32[]{:S(2)}, u32[]{:S(2)}) collective-permute-start(f32[256,1024]{1,0:T(8,128)S(1)} %collective-permute-done.1.refs_6_), channel_id=1, source_target_pairs={{0,1},{1,0},{2,3},{3,2},{4,5},{5,4},{6,7},{7,6},{8,9},{9,8},{10,11... | collective-permute-start | bytes 3145736 | tf_op jit(solution)/shard_map/ppermute | solution.py:351
  27.9 4.2 %collective-permute-start.5 = (f32[256,1024]{1,0:T(8,128)S(1)}, f32[256,1024]{1,0:T(8,128)S(1)}, u32[]{:S(2)}, u32[]{:S(2)}) collective-permute-start(f32[256,1024]{1,0:T(8,128)S(1)} %collective-permute-done.4.refs_8_), channel_id=1, source_target_pairs={{0,1},{1,0},{2,3},{3,2},{4,5},{5,4},{6,7},{7,6},{8,9},{9,8},{10,11... | collective-permute-start | bytes 3145736 | tf_op jit(solution)/shard_map/ppermute | solution.py:351
  42.2 7.9 %collective-permute-start.6 = (f32[512,128]{1,0:T(8,128)S(1)}, f32[512,128]{1,0:T(8,128)S(1)}, u32[]{:S(2)}, u32[]{:S(2)}) collective-permute-start(f32[512,128]{1,0:T(8,128)S(1)} %get-tuple-element.30), channel_id=1, source_target_pairs={{0,2},{1,3},{2,0},{3,1},{4,6},{5,7},{6,4},{7,5},{8,10},{9,11},{10,... | collective-permute-start | bytes 786440 | tf_op jit(solution)/shard_map/ppermute | solution.py:351
  45.0 26.0 %collective-permute-start.10 = (f32[1032,128]{1,0:T(8,128)S(1)}, f32[1032,128]{1,0:T(8,128)S(1)}, u32[]{:S(2)}, u32[]{:S(2)}) collective-permute-start(f32[1032,128]{1,0:T(8,128)S(1)} %get-tuple-element.33), channel_id=1, source_target_pairs={{0,1},{1,2},{6,3},{7,4},{4,5},{5,6},{10,7},{11,8},{8,9},{9,10},{14... | collective-permute-start | bytes 1585160 | tf_op jit(solution)/shard_map/ppermute | solution.py:377
  46.5 24.5 %collective-permute-start.11 = (f32[1032,128]{1,0:T(8,128)S(1)}, f32[1032,128]{1,0:T(8,128)S(1)}, u32[]{:S(2)}, u32[]{:S(2)}) collective-permute-start(f32[1032,128]{1,0:T(8,128)S(1)} %get-tuple-element.34), channel_id=1, source_target_pairs={{0,3},{1,4},{6,5},{7,6},{4,7},{5,8},{10,9},{11,10},{8,11},{9,12},{... | collective-permute-start | bytes 1585160 | tf_op jit(solution)/shard_map/ppermute | solution.py:377
  46.5 24.5 %collective-permute-start.9 = (f32[1032,128]{1,0:T(8,128)S(1)}, f32[1032,128]{1,0:T(8,128)S(1)}, u32[]{:S(2)}, u32[]{:S(2)}) collective-permute-start(f32[1032,128]{1,0:T(8,128)S(1)} %get-tuple-element.32), channel_id=1, source_target_pairs={{0,4},{1,5},{6,2},{7,3},{4,8},{5,9},{10,6},{11,7},{8,12},{9,13},{1... | collective-permute-start | bytes 1585160 | tf_op jit(solution)/shard_map/ppermute | solution.py:377
  50.2 5.8 %collective-permute-start.7 = (f32[256,128]{1,0:T(8,128)S(1)}, f32[256,128]{1,0:T(8,128)S(1)}, u32[]{:S(2)}, u32[]{:S(2)}) collective-permute-start(f32[256,128]{1,0:T(8,128)S(1)} %slice_select_fusion), channel_id=1, source_target_pairs={{0,1},{1,0},{2,3},{3,2},{4,5},{5,4},{6,7},{7,6},{8,9},{9,8},{10,11... | collective-permute-start | bytes 393224 | tf_op jit(solution)/shard_map/ppermute | solution.py:351
  54.2 25.0 %collective-permute-start.13 = (f32[1032,128]{1,0:T(8,128)S(1)}, f32[1032,128]{1,0:T(8,128)S(1)}, u32[]{:S(2)}, u32[]{:S(2)}) collective-permute-start(f32[1032,128]{1,0:T(8,128)S(1)} %get-tuple-element.40), channel_id=1, source_target_pairs={{0,2},{1,3},{6,4},{7,5},{4,6},{5,7},{10,8},{11,9},{8,10},{9,11},{1... | collective-permute-start | bytes 1585160 | tf_op jit(solution)/shard_map/ppermute | solution.py:377
  56.0 15.0 %collective-permute-start.8 = (f32[256,128]{1,0:T(8,128)S(1)}, f32[256,128]{1,0:T(8,128)S(1)}, u32[]{:S(2)}, u32[]{:S(2)}) collective-permute-start(f32[256,128]{1,0:T(8,128)S(1)} %select_add_fusion), channel_id=1, source_target_pairs={{0,4},{1,5},{2,6},{3,7},{4,0},{5,1},{6,2},{7,3},{8,12},{9,13},{10,... | collective-permute-start | bytes 393224 | tf_op jit(solution)/shard_map/ppermute | solution.py:351
  71.0 8.2 %collective-permute-start.12 = (f32[256,128]{1,0:T(8,128)S(1)}, f32[256,128]{1,0:T(8,128)S(1)}, u32[]{:S(2)}, u32[]{:S(2)}) collective-permute-start(f32[256,128]{1,0:T(8,128)S(1)} %add.21), channel_id=1, source_target_pairs={{0,8},{1,9},{2,10},{3,11},{4,12},{5,13},{6,14},{7,15},{8,0},{9,1},... | collective-permute-start | bytes 393224 | tf_op jit(solution)/shard_map/ppermute | solution.py:351
  79.2 2.5 %collective-permute-start.14 = (f32[256,128]{1,0:T(8,128)S(1)}, f32[256,128]{1,0:T(8,128)S(1)}, u32[]{:S(2)}, u32[]{:S(2)}) collective-permute-start(f32[256,128]{1,0:T(8,128)S(1)} %add.22), channel_id=1, source_target_pairs={{0,1},{1,0},{2,3},{3,2},{4,5},{5,4},{6,7},{7,6},{8,9},{9,8},{10,11... | collective-permute-start | bytes 393224 | tf_op jit(solution)/shard_map/ppermute | solution.py:351

commit v5 on v4

--- a/solution.py
+++ b/solution.py
@@ -189,11 +189,12 @@
             here = place[4]
             for c in range(2):
                 at = rows_at(((w * len(backward) + i) * 2 + c), rows_here)
-                edge = grad[c][:rows_here]
-                r["grad0"][at] = jnp.where(here, edge, 0.0)
-                r["grad1"][at] = jnp.where(here, 0.0, edge)
-                for j in range(1, self.reach):
-                    r[f"grad{j + 1}"][at] = grad[c][j * rows_here : (j + 1) * rows_here]
+                rows = [grad[c][j * rows_here : (j + 1) * rows_here] for j in range(self.reach)]
+                r["grad0"][at] = jnp.where(here, rows[0], 0.0)
+                r["grad1"][at] = jnp.where(here, 0.0, rows[0])
+                r["grad2"][at] = rows[2]
+                r["grad3"][at] = jnp.where(parity == 0, rows[3], rows[1])
+                r["grad4"][at] = jnp.where(parity == 0, rows[1], rows[3])
 
         def turn(value, row, lane):
             return pltpu.roll(pltpu.roll(value, row, 0), lane, 1)
@@ -290,13 +291,14 @@
             out_ref[:, :, far] += jnp.where(wraps, value, 0.0)
 
 
-def give(windows, columns, pieces, shape, base=()):
+def give(windows, columns, pieces, shape, base=(), estimate=0):
     smem, vmem = (pl.BlockSpec(memory_space=space) for space in (pltpu.SMEM, pltpu.VMEM))
     return pl.pallas_call(
         functools.partial(give_kernel, windows, len(pieces)),
         out_shape=jax.ShapeDtypeStruct(shape, jnp.float32),
         in_specs=[smem] + [vmem] * (len(pieces) + len(base)),
         out_specs=vmem,
+        cost_estimate=pl.CostEstimate(flops=estimate, bytes_accessed=0, transcendentals=0),
         compiler_params=pltpu.CompilerParams(vmem_limit_bytes=VMEM_BYTES),
     )(jnp.stack(columns), *pieces, *base)
 
@@ -377,8 +379,8 @@
         return lax.ppermute(value, "tile", pairs_there)
 
 
-    def return_route(step):
-        return [(home[t], (t + step) % count) for t in range(count)]
+    def return_route(even_step, odd_step):
+        return [(home[t], (t + (odd_step if t % 2 else even_step)) % count) for t in range(count)]
 
     flat = slices.reshape(slice_count * 2 * rows_here, cols)
     to_home = list(enumerate(home))
@@ -410,23 +412,24 @@
     lower, upper = part[: modes * side], part[modes * side :]
     total = jnp.where(even, lower, upper) + swap(jnp.where(even, upper, lower), 1)
     pieces = [result[f"grad{j}"] for j in range(reach + 1)]
+    total, outer = lax.optimization_barrier((total, pieces[4]))
     total = total + swap(total, 4)
-    middle = reach // 2 + 1
-    early = [pieces[0], send(pieces[1], from_edge)]
-    early += [send(pieces[j], return_route(j - 1)) for j in range(2, reach + 1) if j != middle]
-    late = send(pieces[middle], return_route(middle - 1))
+    early = [pieces[0], send(pieces[1], from_edge), send(pieces[2], return_route(2, 2))]
+    late = [send(pieces[3], return_route(3, 1))]
     total, *early = lax.optimization_barrier((total, *early))
+    late.append(send(outer, return_route(1, 3)))
 
     def columns_of(piece):
         return piece[-EXTRA:][:windows, 0].astype(jnp.int32)
 
     shape = (2 * slice_count, rows_here, cols)
+    total, *early = lax.optimization_barrier((sum_over_tiles(total), *early, late.pop(0)))
     columns = [offsets[1, :windows]] + [columns_of(piece) for piece in early[1:]]
-    own_grad = give(windows, columns, early, shape)
-    total = sum_over_tiles(total)
-    total, own_grad, late = lax.optimization_barrier((total, own_grad, late))
-    own_grad = give(windows, [columns_of(late)], [late], shape, [own_grad]).reshape(slices.shape)
+    own_grad = give(windows, columns, early, shape, estimate=0)
+    total, own_grad, *late = lax.optimization_barrier((total, own_grad, *late))
     rest = swap(total, 1)
+    own_grad = give(windows, [columns_of(piece) for piece in late], late, shape, [own_grad])
+    own_grad = own_grad.reshape(slices.shape)
     probe_grad = jnp.where(even, jnp.concatenate([total, rest]), jnp.concatenate([rest, total]))
     return own_grad, probe_grad.reshape(probe_modes.shape)
 

time: 82.7 us -> 80.3 us (0.971)
  waiting for transfers between devices: 40 us -> 38.2 us
    ppermute x9, waiting for transfers between devices: 39.1 us -> 37.4 us  [swap(): return lax.ppermute(value, 'tile', [(i, i ^ bits) for i in range(count)])]
  transfers between devices with their start and end apart: 15 -> 15, of which waited for: 6 -> 6; matrix products, arithmetic and copies ran while one was open for 2% -> 2% of each run, Pallas kernels for 4% -> 5%
where the time goes in v5:
time: 80.3 us; the launch traced here: 80 us
  waiting for transfers between devices  38.2 us (48%)
  starting transfers between devices  21.9 us (27%)
  Pallas kernels  13.8 us (17%)
  local copies, waits for them, and re-layouts  3.13 us (4%)
  other arithmetic  2.25 us (3%)
    ppermute x9, waiting for transfers between devices, swap(): return lax.ppermute(value, 'tile', [(i, i ^ bits) for i in range(count)])  37.4 us
    ppermute x9, starting transfers between devices, swap(): return lax.ppermute(value, 'tile', [(i, i ^ bits) for i in range(count)])  14.1 us
    pallas_call x1, Pallas kernels, __call__(): pl.pallas_call(self.kernel, out_shape=shapes, in_specs=[smem] + [vmem] *...  10.2 us
    ppermute x6, starting transfers between devices, send(): return lax.ppermute(value, 'tile', pairs_there)  7.8 us
    pallas_call x2, Pallas kernels, give(): pl.pallas_call(functools.partial(give_kernel, windows, len(pieces)), out_...  3.42 us
    unnamed x10, local copies, waits for them, and re-layouts  3.12 us
  transfers between devices with their start and end apart: 15, of which 6 were waited for; matrix products, arithmetic and copies ran while one was open for 2% of the time, Pallas kernels for 5%

profile of v5, /device:TPU:1, one launch (start us, length us, event | category | flops | bytes accessed | tf_op | source)
XLA Modules:
  0.0 80.0 jit_solution(14395684893395513979)
XLA Ops:
  0.6 2.1 %collective-permute-start.1 = (f32[256,1024]{1,0:T(8,128)}, f32[256,1024]{1,0:T(8,128)S(1)}, u32[]{:S(2)}, u32[]{:S(2)}) collective-permute-start(f32[256,1024]{1,0:T(8,128)} %bitcast.10), channel_id=1, source_target_pairs={{0,2},{1,3},{2,0},{3,1},{4,6},{5,7},{6,4},{7,5},{8,10},{9,11},{10,... | collective-permute-start | bytes 3145736 | tf_op jit(solution)/shard_map/ppermute | solution.py:353
  2.8 3.3 %collective-permute-start.4 = (f32[256,1024]{1,0:T(8,128)}, f32[256,1024]{1,0:T(8,128)S(1)}, u32[]{:S(2)}, u32[]{:S(2)}) collective-permute-start(f32[256,1024]{1,0:T(8,128)} %bitcast.11), channel_id=1, source_target_pairs={{4,0},{5,1},{2,6},{3,7},{8,4},{9,5},{6,10},{7,11},{12,8},{13,9},{1... | collective-permute-start | bytes 3145736 | tf_op jit(solution)/shard_map/ppermute | solution.py:379
  6.1 0.7 copy-done.3
  6.8 1.0 %select_maximum_fusion = f32[520,128]{1,0:T(8,128)S(1)} fusion(f32[2,4]{1,0:T(2,128)S(1)} %add_convert_fusion, f32[512,128]{1,0:T(8,128)} %bitcast.17), kind=kLoop, calls=%fused_computation | loop fusion | flops 199680 | bytes 528416 | tf_op jit(solution)/shard_map/concatenate | solution.py:392
  7.8 0.7 collective-permute-start
  8.5 1.3 %collective-permute-start.2 = (f32[256,1024]{1,0:T(8,128)}, f32[256,1024]{1,0:T(8,128)S(1)}, u32[]{:S(2)}, u32[]{:S(2)}) collective-permute-start(f32[256,1024]{1,0:T(8,128)} %bitcast.12), channel_id=1, source_target_pairs={{0,1},{1,0},{2,3},{3,2},{4,5},{5,4},{6,7},{7,6},{8,9},{9,8},{10,11... | collective-permute-start | bytes 3145736 | tf_op jit(solution)/shard_map/ppermute | solution.py:353
  9.8 1.2 %copy-done = f32[4,2,32,1024]{3,2,1,0:T(8,128)S(1)} copy-done((f32[4,2,32,1024]{3,2,1,0:T(8,128)S(1)}, f32[4,2,32,1024]{3,2,1,0:T(8,128)}, u32[]{:S(2)}) %copy-start) | copy-done | bytes 1048600
  11.0 1.2 %copy-done.1 = bf16[4,2,256,256]{3,2,1,0:T(8,128)(2,1)S(1)} copy-done((bf16[4,2,256,256]{3,2,1,0:T(8,128)(2,1)S(1)}, bf16[4,2,256,256]{3,2,1,0:T(8,128)(2,1)}, u32[]{:S(2)}) %copy-start.1) | copy-done | bytes 1048600
  12.4 13.4 %collective-permute-done.1.refs_6_ = f32[256,1024]{1,0:T(8,128)S(1)} collective-permute-done((f32[256,1024]{1,0:T(8,128)}, f32[256,1024]{1,0:T(8,128)S(1)}, u32[]{:S(2)}, u32[]{:S(2)}) %collective-permute-start.1) | collective-permute-done | bytes 1048608 | tf_op jit(solution)/shard_map/ppermute | solution.py:353
  25.9 1.2 %collective-permute-start.3 = (f32[256,1024]{1,0:T(8,128)S(1)}, f32[256,1024]{1,0:T(8,128)S(1)}, u32[]{:S(2)}, u32[]{:S(2)}) collective-permute-start(f32[256,1024]{1,0:T(8,128)S(1)} %collective-permute-done.1.refs_6_), channel_id=1, source_target_pairs={{0,1},{1,0},{2,3},{3,2},{4,5},{5,4},{6,7},{7,6},{8,9},{9,8},{10,11... | collective-permute-start | bytes 3145736 | tf_op jit(solution)/shard_map/ppermute | solution.py:353
  27.1 0.8 %collective-permute-done.4.refs_8_ = f32[256,1024]{1,0:T(8,128)S(1)} collective-permute-done((f32[256,1024]{1,0:T(8,128)}, f32[256,1024]{1,0:T(8,128)S(1)}, u32[]{:S(2)}, u32[]{:S(2)}) %collective-permute-start.4) | collective-permute-done | bytes 1048608 | tf_op jit(solution)/shard_map/ppermute | solution.py:379
  27.9 1.9 %collective-permute-start.5 = (f32[256,1024]{1,0:T(8,128)S(1)}, f32[256,1024]{1,0:T(8,128)S(1)}, u32[]{:S(2)}, u32[]{:S(2)}) collective-permute-start(f32[256,1024]{1,0:T(8,128)S(1)} %collective-permute-done.4.refs_8_), channel_id=1, source_target_pairs={{0,1},{1,0},{2,3},{3,2},{4,5},{5,4},{6,7},{7,6},{8,9},{9,8},{10,11... | collective-permute-start | bytes 3145736 | tf_op jit(solution)/shard_map/ppermute | solution.py:353
  29.8 2.3 %collective-permute-done.5.refs_9_ = f32[256,1024]{1,0:T(8,128)S(1)} collective-permute-done((f32[256,1024]{1,0:T(8,128)S(1)}, f32[256,1024]{1,0:T(8,128)S(1)}, u32[]{:S(2)}, u32[]{:S(2)}) %collective-permute-start.5) | collective-permute-done | bytes 1048608 | tf_op jit(solution)/shard_map/ppermute | solution.py:353
  32.1 10.2 %shard_map.79 = (f32[1032,128]{1,0:T(8,128)}, f32[1032,128]{1,0:T(8,128)}, f32[1032,128]{1,0:T(8,128)}, f32[1032,128]{1,0:T(8,128)}, f32[1032,128]{1,0:T(8,128)}...) custom-call(s32[8,128]{1,0:T(8,128)S(1)} %shard_map.77.refs_0_, ...), custom_call_target="tpu_custom_call" | custom-call | tf_op jit(solution)/shard_map/pallas_call | solution.py:131
  42.2 2.8 %collective-permute-start.6 = (f32[512,128]{1,0:T(8,128)S(1)}, f32[512,128]{1,0:T(8,128)S(1)}, u32[]{:S(2)}, u32[]{:S(2)}) collective-permute-start(f32[512,128]{1,0:T(8,128)S(1)} %get-tuple-element.36), channel_id=1, source_target_pairs={{0,2},{1,3},{2,0},{3,1},{4,6},{5,7},{6,4},{7,5},{8,10},{9,11},{10,... | collective-permute-start | bytes 786440 | tf_op jit(solution)/shard_map/ppermute | solution.py:353
  45.1 5.0 %collective-permute-done.6 = f32[512,128]{1,0:T(8,128)S(1)} collective-permute-done((f32[512,128]{1,0:T(8,128)S(1)}, f32[512,128]{1,0:T(8,128)S(1)}, u32[]{:S(2)}, u32[]{:S(2)}) %collective-permute-start.6) | collective-permute-done | bytes 262176 | tf_op jit(solution)/shard_map/ppermute | solution.py:353
  50.2 4.1 %collective-permute-start.7 = (f32[256,128]{1,0:T(8,128)S(1)}, f32[256,128]{1,0:T(8,128)S(1)}, u32[]{:S(2)}, u32[]{:S(2)}) collective-permute-start(f32[256,128]{1,0:T(8,128)S(1)} %slice_select_fusion), channel_id=1, source_target_pairs={{0,1},{1,0},{2,3},{3,2},{4,5},{5,4},{6,7},{7,6},{8,9},{9,8},{10,11... | collective-permute-start | bytes 393224 | tf_op jit(solution)/shard_map/ppermute | solution.py:353
  54.2 1.7 %collective-permute-start.12 = (f32[1032,128]{1,0:T(8,128)S(1)}, f32[1032,128]{1,0:T(8,128)S(1)}, u32[]{:S(2)}, u32[]{:S(2)}) collective-permute-start(f32[1032,128]{1,0:T(8,128)S(1)} %get-tuple-element.46), channel_id=1, source_target_pairs={{0,3},{1,2},{6,5},{7,4},{4,7},{5,6},{10,9},{11,8},{8,11},{9,10},{1... | collective-permute-start | bytes 1585160 | tf_op jit(solution)/shard_map/ppermute | solution.py:379
  56.0 2.1 %collective-permute-start.13 = (f32[1032,128]{1,0:T(8,128)S(1)}, f32[1032,128]{1,0:T(8,128)S(1)}, u32[]{:S(2)}, u32[]{:S(2)}) collective-permute-start(f32[1032,128]{1,0:T(8,128)S(1)} %get-tuple-element.52), channel_id=1, source_target_pairs={{0,1},{1,4},{6,3},{7,6},{4,5},{5,8},{10,7},{11,10},{8,9},{9,12},{1... | collective-permute-start | bytes 1585160 | tf_op jit(solution)/shard_map/ppermute | solution.py:379
  58.1 6.9 %collective-permute-done.8 = f32[256,128]{1,0:T(8,128)S(1)} collective-permute-done((f32[256,128]{1,0:T(8,128)S(1)}, f32[256,128]{1,0:T(8,128)S(1)}, u32[]{:S(2)}, u32[]{:S(2)}) %collective-permute-start.8) | collective-permute-done | bytes 131104 | tf_op jit(solution)/shard_map/ppermute | solution.py:353
  65.1 9.8 %collective-permute-done.11 = f32[256,128]{1,0:T(8,128)S(1)} collective-permute-done((f32[256,128]{1,0:T(8,128)S(1)}, f32[256,128]{1,0:T(8,128)S(1)}, u32[]{:S(2)}, u32[]{:S(2)}) %collective-permute-start.11) | collective-permute-done | bytes 131104 | tf_op jit(solution)/shard_map/ppermute | solution.py:353
  75.2 1.6 %shard_map.80.refs_1_ = f32[8,32,1024]{2,1,0:T(8,128)S(1)} custom-call(s32[4,4]{1,0:T(4,128)S(1)} %pad_add_fusion.col_ref, f32[1032,128]{1,0:T(8,128)S(1)} %get-tuple-element.51.refs_0_, f32[1032,128]{1,0:T(8,128)S(1)} %collective-permute-done.9.refs_1_, f32[1032,128]{1,0:T(8,128)S(1)} %collective-permute-done.10.refs_2_, ...), custom_call_target="tpu_custom_call" | custom-call | tf_op jit(solution)/shard_map/pallas_call | solution.py:296
  77.5 1.8 %shard_map.81 = f32[8,32,1024]{2,1,0:T(8,128)} custom-call(s32[1,4]{1,0:T(1,128)S(1)} %bitcast.14, f32[1032,128]{1,0:T(8,128)S(1)} %collective-permute-done.13.refs_0_, f32[8,32,1024]{2,1,0:T(8,128)S(1)} %shard_map.80.refs_1_), custom_call_target="tpu_custom_call" | custom-call | tf_op jit(solution)/shard_map/pallas_call | solution.py:296
  79.3 0.7 maximum_select_fusion
  (34 shorter events, 1.5 us)
Async XLA Ops:
  0.6 25.2 %collective-permute-start.1 = (f32[256,1024]{1,0:T(8,128)}, f32[256,1024]{1,0:T(8,128)S(1)}, u32[]{:S(2)}, u32[]{:S(2)}) collective-permute-start(f32[256,1024]{1,0:T(8,128)} %bitcast.10), channel_id=1, source_target_pairs={{0,2},{1,3},{2,0},{3,1},{4,6},{5,7},{6,4},{7,5},{8,10},{9,11},{10,... | collective-permute-start | bytes 3145736 | tf_op jit(solution)/shard_map/ppermute | solution.py:353
  2.8 25.1 %collective-permute-start.4 = (f32[256,1024]{1,0:T(8,128)}, f32[256,1024]{1,0:T(8,128)S(1)}, u32[]{:S(2)}, u32[]{:S(2)}) collective-permute-start(f32[256,1024]{1,0:T(8,128)} %bitcast.11), channel_id=1, source_target_pairs={{4,0},{5,1},{2,6},{3,7},{8,4},{9,5},{6,10},{7,11},{12,8},{13,9},{1... | collective-permute-start | bytes 3145736 | tf_op jit(solution)/shard_map/ppermute | solution.py:379
  6.1 0.7 copy-start.3
  6.1 0.7 copy-start.4
  6.8 3.0 %copy-start.2 = (f32[2,2,128,128]{3,2,1,0:T(8,128)S(1)}, f32[2,2,128,128]{3,2,1,0:T(8,128)}, u32[]{:S(2)}) copy-start(f32[2,2,128,128]{3,2,1,0:T(8,128)} %refs_1_.1) | copy-start | bytes 786436
  7.8 22.0 %collective-permute-start = (f32[520,128]{1,0:T(8,128)S(1)}, f32[520,128]{1,0:T(8,128)S(1)}, u32[]{:S(2)}, u32[]{:S(2)}) collective-permute-start(f32[520,128]{1,0:T(8,128)S(1)} %select_maximum_fusion), channel_id=1, source_target_pairs={{0,0},{1,1},{2,6},{3,7},{4,4},{5,5},{6,10},{7,11},{8,8},{9,9},{10,... | collective-permute-start | bytes 798728 | tf_op jit(solution)/shard_map/ppermute | solution.py:379
  8.5 21.3 %collective-permute-start.2 = (f32[256,1024]{1,0:T(8,128)}, f32[256,1024]{1,0:T(8,128)S(1)}, u32[]{:S(2)}, u32[]{:S(2)}) collective-permute-start(f32[256,1024]{1,0:T(8,128)} %bitcast.12), channel_id=1, source_target_pairs={{0,1},{1,0},{2,3},{3,2},{4,5},{5,4},{6,7},{7,6},{8,9},{9,8},{10,11... | collective-permute-start | bytes 3145736 | tf_op jit(solution)/shard_map/ppermute | solution.py:353
  9.8 1.2 %copy-start = (f32[4,2,32,1024]{3,2,1,0:T(8,128)S(1)}, f32[4,2,32,1024]{3,2,1,0:T(8,128)}, u32[]{:S(2)}) copy-start(f32[4,2,32,1024]{3,2,1,0:T(8,128)} %param.6) | copy-start | bytes 3145732
  11.0 1.2 %copy-start.1 = (bf16[4,2,256,256]{3,2,1,0:T(8,128)(2,1)S(1)}, bf16[4,2,256,256]{3,2,1,0:T(8,128)(2,1)}, u32[]{:S(2)}) copy-start(bf16[4,2,256,256]{3,2,1,0:T(8,128)(2,1)} %constant.22.clone.refs_2_) | copy-start | bytes 3145732
  25.9 3.9 %collective-permute-start.3 = (f32[256,1024]{1,0:T(8,128)S(1)}, f32[256,1024]{1,0:T(8,128)S(1)}, u32[]{:S(2)}, u32[]{:S(2)}) collective-permute-start(f32[256,1024]{1,0:T(8,128)S(1)} %collective-permute-done.1.refs_6_), channel_id=1, source_target_pairs={{0,1},{1,0},{2,3},{3,2},{4,5},{5,4},{6,7},{7,6},{8,9},{9,8},{10,11... | collective-permute-start | bytes 3145736 | tf_op jit(solution)/shard_map/ppermute | solution.py:353
  27.9 4.2 %collective-permute-start.5 = (f32[256,1024]{1,0:T(8,128)S(1)}, f32[256,1024]{1,0:T(8,128)S(1)}, u32[]{:S(2)}, u32[]{:S(2)}) collective-permute-start(f32[256,1024]{1,0:T(8,128)S(1)} %collective-permute-done.4.refs_8_), channel_id=1, source_target_pairs={{0,1},{1,0},{2,3},{3,2},{4,5},{5,4},{6,7},{7,6},{8,9},{9,8},{10,11... | collective-permute-start | bytes 3145736 | tf_op jit(solution)/shard_map/ppermute | solution.py:353
  42.2 7.9 %collective-permute-start.6 = (f32[512,128]{1,0:T(8,128)S(1)}, f32[512,128]{1,0:T(8,128)S(1)}, u32[]{:S(2)}, u32[]{:S(2)}) collective-permute-start(f32[512,128]{1,0:T(8,128)S(1)} %get-tuple-element.36), channel_id=1, source_target_pairs={{0,2},{1,3},{2,0},{3,1},{4,6},{5,7},{6,4},{7,5},{8,10},{9,11},{10,... | collective-permute-start | bytes 786440 | tf_op jit(solution)/shard_map/ppermute | solution.py:353
  45.0 20.0 %collective-permute-start.10 = (f32[1032,128]{1,0:T(8,128)S(1)}, f32[1032,128]{1,0:T(8,128)S(1)}, u32[]{:S(2)}, u32[]{:S(2)}) collective-permute-start(f32[1032,128]{1,0:T(8,128)S(1)} %get-tuple-element.41), channel_id=1, source_target_pairs={{0,2},{1,3},{6,4},{7,5},{4,6},{5,7},{10,8},{11,9},{8,10},{9,11},{1... | collective-permute-start | bytes 1585160 | tf_op jit(solution)/shard_map/ppermute | solution.py:379
  45.1 19.9 %collective-permute-start.9 = (f32[1032,128]{1,0:T(8,128)S(1)}, f32[1032,128]{1,0:T(8,128)S(1)}, u32[]{:S(2)}, u32[]{:S(2)}) collective-permute-start(f32[1032,128]{1,0:T(8,128)S(1)} %get-tuple-element.40), channel_id=1, source_target_pairs={{0,4},{1,5},{6,2},{7,3},{4,8},{5,9},{10,6},{11,7},{8,12},{9,13},{1... | collective-permute-start | bytes 1585160 | tf_op jit(solution)/shard_map/ppermute | solution.py:379
  50.2 5.8 %collective-permute-start.7 = (f32[256,128]{1,0:T(8,128)S(1)}, f32[256,128]{1,0:T(8,128)S(1)}, u32[]{:S(2)}, u32[]{:S(2)}) collective-permute-start(f32[256,128]{1,0:T(8,128)S(1)} %slice_select_fusion), channel_id=1, source_target_pairs={{0,1},{1,0},{2,3},{3,2},{4,5},{5,4},{6,7},{7,6},{8,9},{9,8},{10,11... | collective-permute-start | bytes 393224 | tf_op jit(solution)/shard_map/ppermute | solution.py:353
  54.2 20.7 %collective-permute-start.12 = (f32[1032,128]{1,0:T(8,128)S(1)}, f32[1032,128]{1,0:T(8,128)S(1)}, u32[]{:S(2)}, u32[]{:S(2)}) collective-permute-start(f32[1032,128]{1,0:T(8,128)S(1)} %get-tuple-element.46), channel_id=1, source_target_pairs={{0,3},{1,2},{6,5},{7,4},{4,7},{5,6},{10,9},{11,8},{8,11},{9,10},{1... | collective-permute-start | bytes 1585160 | tf_op jit(solution)/shard_map/ppermute | solution.py:379
  55.9 9.0 %collective-permute-start.8 = (f32[256,128]{1,0:T(8,128)S(1)}, f32[256,128]{1,0:T(8,128)S(1)}, u32[]{:S(2)}, u32[]{:S(2)}) collective-permute-start(f32[256,128]{1,0:T(8,128)S(1)} %select_add_fusion), channel_id=1, source_target_pairs={{0,4},{1,5},{2,6},{3,7},{4,0},{5,1},{6,2},{7,3},{8,12},{9,13},{10,... | collective-permute-start | bytes 393224 | tf_op jit(solution)/shard_map/ppermute | solution.py:353
  56.0 20.8 %collective-permute-start.13 = (f32[1032,128]{1,0:T(8,128)S(1)}, f32[1032,128]{1,0:T(8,128)S(1)}, u32[]{:S(2)}, u32[]{:S(2)}) collective-permute-start(f32[1032,128]{1,0:T(8,128)S(1)} %get-tuple-element.52), channel_id=1, source_target_pairs={{0,1},{1,4},{6,3},{7,6},{4,5},{5,8},{10,7},{11,10},{8,9},{9,12},{1... | collective-permute-start | bytes 1585160 | tf_op jit(solution)/shard_map/ppermute | solution.py:379
  65.0 9.9 %collective-permute-start.11 = (f32[256,128]{1,0:T(8,128)S(1)}, f32[256,128]{1,0:T(8,128)S(1)}, u32[]{:S(2)}, u32[]{:S(2)}) collective-permute-start(f32[256,128]{1,0:T(8,128)S(1)} %add.21), channel_id=1, source_target_pairs={{0,8},{1,9},{2,10},{3,11},{4,12},{5,13},{6,14},{7,15},{8,0},{9,1},... | collective-permute-start | bytes 393224 | tf_op jit(solution)/shard_map/ppermute | solution.py:353
  76.8 2.5 %collective-permute-start.14 = (f32[256,128]{1,0:T(8,128)S(1)}, f32[256,128]{1,0:T(8,128)S(1)}, u32[]{:S(2)}, u32[]{:S(2)}) collective-permute-start(f32[256,128]{1,0:T(8,128)S(1)} %add.22), channel_id=1, source_target_pairs={{0,1},{1,0},{2,3},{3,2},{4,5},{5,4},{6,7},{7,6},{8,9},{9,8},{10,11... | collective-permute-start | bytes 393224 | tf_op jit(solution)/shard_map/ppermute | solution.py:353

commit v6 on v5

--- a/solution.py
+++ b/solution.py
@@ -414,7 +414,8 @@
     pieces = [result[f"grad{j}"] for j in range(reach + 1)]
     total, outer = lax.optimization_barrier((total, pieces[4]))
     total = total + swap(total, 4)
-    early = [pieces[0], send(pieces[1], from_edge), send(pieces[2], return_route(2, 2))]
+    first = send(pieces[2], return_route(2, 2))
+    early = [pieces[0], send(pieces[1], from_edge), first]
     late = [send(pieces[3], return_route(3, 1))]
     total, *early = lax.optimization_barrier((total, *early))
     late.append(send(outer, return_route(1, 3)))

time: 80.3 us -> 80.3 us (level)
  no operation moved by 1% of the time
where the time goes in v6:
time: 80.3 us; the launch traced here: 80 us
  waiting for transfers between devices  38.2 us (48%)
  starting transfers between devices  21.9 us (27%)
  Pallas kernels  13.8 us (17%)
  local copies, waits for them, and re-layouts  3.13 us (4%)
  other arithmetic  2.25 us (3%)
    ppermute x9, waiting for transfers between devices, swap(): return lax.ppermute(value, 'tile', [(i, i ^ bits) for i in range(count)])  37.4 us
    ppermute x9, starting transfers between devices, swap(): return lax.ppermute(value, 'tile', [(i, i ^ bits) for i in range(count)])  14.1 us
    pallas_call x1, Pallas kernels, __call__(): pl.pallas_call(self.kernel, out_shape=shapes, in_specs=[smem] + [vmem] *...  10.2 us
    ppermute x6, starting transfers between devices, send(): return lax.ppermute(value, 'tile', pairs_there)  7.81 us
    pallas_call x2, Pallas kernels, give(): pl.pallas_call(functools.partial(give_kernel, windows, len(pieces)), out_...  3.42 us
    unnamed x10, local copies, waits for them, and re-layouts  3.12 us
  transfers between devices with their start and end apart: 15, of which 6 were waited for; matrix products, arithmetic and copies ran while one was open for 2% of the time, Pallas kernels for 5%

profile of v6, /device:TPU:1, one launch (start us, length us, event | category | flops | bytes accessed | tf_op | source)
XLA Modules:
  0.0 80.0 jit_solution(14395684893395513979)
XLA Ops:
  0.6 2.1 %collective-permute-start.1 = (f32[256,1024]{1,0:T(8,128)}, f32[256,1024]{1,0:T(8,128)S(1)}, u32[]{:S(2)}, u32[]{:S(2)}) collective-permute-start(f32[256,1024]{1,0:T(8,128)} %bitcast.10), channel_id=1, source_target_pairs={{0,2},{1,3},{2,0},{3,1},{4,6},{5,7},{6,4},{7,5},{8,10},{9,11},{10,... | collective-permute-start | bytes 3145736 | tf_op jit(solution)/shard_map/ppermute | solution.py:353
  2.8 3.3 %collective-permute-start.4 = (f32[256,1024]{1,0:T(8,128)}, f32[256,1024]{1,0:T(8,128)S(1)}, u32[]{:S(2)}, u32[]{:S(2)}) collective-permute-start(f32[256,1024]{1,0:T(8,128)} %bitcast.11), channel_id=1, source_target_pairs={{4,0},{5,1},{2,6},{3,7},{8,4},{9,5},{6,10},{7,11},{12,8},{13,9},{1... | collective-permute-start | bytes 3145736 | tf_op jit(solution)/shard_map/ppermute | solution.py:379
  6.1 0.7 copy-done.3
  6.8 1.0 %select_maximum_fusion = f32[520,128]{1,0:T(8,128)S(1)} fusion(f32[2,4]{1,0:T(2,128)S(1)} %add_convert_fusion, f32[512,128]{1,0:T(8,128)} %bitcast.17), kind=kLoop, calls=%fused_computation | loop fusion | flops 199680 | bytes 528416 | tf_op jit(solution)/shard_map/concatenate | solution.py:392
  7.8 0.7 collective-permute-start
  8.5 1.3 %collective-permute-start.2 = (f32[256,1024]{1,0:T(8,128)}, f32[256,1024]{1,0:T(8,128)S(1)}, u32[]{:S(2)}, u32[]{:S(2)}) collective-permute-start(f32[256,1024]{1,0:T(8,128)} %bitcast.12), channel_id=1, source_target_pairs={{0,1},{1,0},{2,3},{3,2},{4,5},{5,4},{6,7},{7,6},{8,9},{9,8},{10,11... | collective-permute-start | bytes 3145736 | tf_op jit(solution)/shard_map/ppermute | solution.py:353
  9.8 1.2 %copy-done = f32[4,2,32,1024]{3,2,1,0:T(8,128)S(1)} copy-done((f32[4,2,32,1024]{3,2,1,0:T(8,128)S(1)}, f32[4,2,32,1024]{3,2,1,0:T(8,128)}, u32[]{:S(2)}) %copy-start) | copy-done | bytes 1048600
  11.0 1.2 %copy-done.1 = bf16[4,2,256,256]{3,2,1,0:T(8,128)(2,1)S(1)} copy-done((bf16[4,2,256,256]{3,2,1,0:T(8,128)(2,1)S(1)}, bf16[4,2,256,256]{3,2,1,0:T(8,128)(2,1)}, u32[]{:S(2)}) %copy-start.1) | copy-done | bytes 1048600
  12.4 13.4 %collective-permute-done.1.refs_6_ = f32[256,1024]{1,0:T(8,128)S(1)} collective-permute-done((f32[256,1024]{1,0:T(8,128)}, f32[256,1024]{1,0:T(8,128)S(1)}, u32[]{:S(2)}, u32[]{:S(2)}) %collective-permute-start.1) | collective-permute-done | bytes 1048608 | tf_op jit(solution)/shard_map/ppermute | solution.py:353
  25.9 1.2 %collective-permute-start.3 = (f32[256,1024]{1,0:T(8,128)S(1)}, f32[256,1024]{1,0:T(8,128)S(1)}, u32[]{:S(2)}, u32[]{:S(2)}) collective-permute-start(f32[256,1024]{1,0:T(8,128)S(1)} %collective-permute-done.1.refs_6_), channel_id=1, source_target_pairs={{0,1},{1,0},{2,3},{3,2},{4,5},{5,4},{6,7},{7,6},{8,9},{9,8},{10,11... | collective-permute-start | bytes 3145736 | tf_op jit(solution)/shard_map/ppermute | solution.py:353
  27.1 0.8 %collective-permute-done.4.refs_8_ = f32[256,1024]{1,0:T(8,128)S(1)} collective-permute-done((f32[256,1024]{1,0:T(8,128)}, f32[256,1024]{1,0:T(8,128)S(1)}, u32[]{:S(2)}, u32[]{:S(2)}) %collective-permute-start.4) | collective-permute-done | bytes 1048608 | tf_op jit(solution)/shard_map/ppermute | solution.py:379
  27.9 1.9 %collective-permute-start.5 = (f32[256,1024]{1,0:T(8,128)S(1)}, f32[256,1024]{1,0:T(8,128)S(1)}, u32[]{:S(2)}, u32[]{:S(2)}) collective-permute-start(f32[256,1024]{1,0:T(8,128)S(1)} %collective-permute-done.4.refs_8_), channel_id=1, source_target_pairs={{0,1},{1,0},{2,3},{3,2},{4,5},{5,4},{6,7},{7,6},{8,9},{9,8},{10,11... | collective-permute-start | bytes 3145736 | tf_op jit(solution)/shard_map/ppermute | solution.py:353
  29.8 2.3 %collective-permute-done.5.refs_9_ = f32[256,1024]{1,0:T(8,128)S(1)} collective-permute-done((f32[256,1024]{1,0:T(8,128)S(1)}, f32[256,1024]{1,0:T(8,128)S(1)}, u32[]{:S(2)}, u32[]{:S(2)}) %collective-permute-start.5) | collective-permute-done | bytes 1048608 | tf_op jit(solution)/shard_map/ppermute | solution.py:353
  32.1 10.2 %shard_map.79 = (f32[1032,128]{1,0:T(8,128)}, f32[1032,128]{1,0:T(8,128)}, f32[1032,128]{1,0:T(8,128)}, f32[1032,128]{1,0:T(8,128)}, f32[1032,128]{1,0:T(8,128)}...) custom-call(s32[8,128]{1,0:T(8,128)S(1)} %shard_map.77.refs_0_, ...), custom_call_target="tpu_custom_call" | custom-call | tf_op jit(solution)/shard_map/pallas_call | solution.py:131
  42.2 2.8 %collective-permute-start.6 = (f32[512,128]{1,0:T(8,128)S(1)}, f32[512,128]{1,0:T(8,128)S(1)}, u32[]{:S(2)}, u32[]{:S(2)}) collective-permute-start(f32[512,128]{1,0:T(8,128)S(1)} %get-tuple-element.36), channel_id=1, source_target_pairs={{0,2},{1,3},{2,0},{3,1},{4,6},{5,7},{6,4},{7,5},{8,10},{9,11},{10,... | collective-permute-start | bytes 786440 | tf_op jit(solution)/shard_map/ppermute | solution.py:353
  45.1 5.0 %collective-permute-done.6 = f32[512,128]{1,0:T(8,128)S(1)} collective-permute-done((f32[512,128]{1,0:T(8,128)S(1)}, f32[512,128]{1,0:T(8,128)S(1)}, u32[]{:S(2)}, u32[]{:S(2)}) %collective-permute-start.6) | collective-permute-done | bytes 262176 | tf_op jit(solution)/shard_map/ppermute | solution.py:353
  50.1 4.1 %collective-permute-start.7 = (f32[256,128]{1,0:T(8,128)S(1)}, f32[256,128]{1,0:T(8,128)S(1)}, u32[]{:S(2)}, u32[]{:S(2)}) collective-permute-start(f32[256,128]{1,0:T(8,128)S(1)} %slice_select_fusion), channel_id=1, source_target_pairs={{0,1},{1,0},{2,3},{3,2},{4,5},{5,4},{6,7},{7,6},{8,9},{9,8},{10,11... | collective-permute-start | bytes 393224 | tf_op jit(solution)/shard_map/ppermute | solution.py:353
  54.2 1.7 %collective-permute-start.12 = (f32[1032,128]{1,0:T(8,128)S(1)}, f32[1032,128]{1,0:T(8,128)S(1)}, u32[]{:S(2)}, u32[]{:S(2)}) collective-permute-start(f32[1032,128]{1,0:T(8,128)S(1)} %get-tuple-element.46), channel_id=1, source_target_pairs={{0,3},{1,2},{6,5},{7,4},{4,7},{5,6},{10,9},{11,8},{8,11},{9,10},{1... | collective-permute-start | bytes 1585160 | tf_op jit(solution)/shard_map/ppermute | solution.py:379
  56.0 2.1 %collective-permute-start.13 = (f32[1032,128]{1,0:T(8,128)S(1)}, f32[1032,128]{1,0:T(8,128)S(1)}, u32[]{:S(2)}, u32[]{:S(2)}) collective-permute-start(f32[1032,128]{1,0:T(8,128)S(1)} %get-tuple-element.52), channel_id=1, source_target_pairs={{0,1},{1,4},{6,3},{7,6},{4,5},{5,8},{10,7},{11,10},{8,9},{9,12},{1... | collective-permute-start | bytes 1585160 | tf_op jit(solution)/shard_map/ppermute | solution.py:379
  58.1 6.9 %collective-permute-done.8 = f32[256,128]{1,0:T(8,128)S(1)} collective-permute-done((f32[256,128]{1,0:T(8,128)S(1)}, f32[256,128]{1,0:T(8,128)S(1)}, u32[]{:S(2)}, u32[]{:S(2)}) %collective-permute-start.8) | collective-permute-done | bytes 131104 | tf_op jit(solution)/shard_map/ppermute | solution.py:353
  65.1 9.8 %collective-permute-done.11 = f32[256,128]{1,0:T(8,128)S(1)} collective-permute-done((f32[256,128]{1,0:T(8,128)S(1)}, f32[256,128]{1,0:T(8,128)S(1)}, u32[]{:S(2)}, u32[]{:S(2)}) %collective-permute-start.11) | collective-permute-done | bytes 131104 | tf_op jit(solution)/shard_map/ppermute | solution.py:353
  75.2 1.6 %shard_map.80.refs_1_ = f32[8,32,1024]{2,1,0:T(8,128)S(1)} custom-call(s32[4,4]{1,0:T(4,128)S(1)} %pad_add_fusion.col_ref, f32[1032,128]{1,0:T(8,128)S(1)} %get-tuple-element.51.refs_0_, f32[1032,128]{1,0:T(8,128)S(1)} %collective-permute-done.9.refs_1_, f32[1032,128]{1,0:T(8,128)S(1)} %collective-permute-done.10.refs_2_, ...), custom_call_target="tpu_custom_call" | custom-call | tf_op jit(solution)/shard_map/pallas_call | solution.py:296
  77.5 1.8 %shard_map.81 = f32[8,32,1024]{2,1,0:T(8,128)} custom-call(s32[1,4]{1,0:T(1,128)S(1)} %bitcast.14, f32[1032,128]{1,0:T(8,128)S(1)} %collective-permute-done.13.refs_0_, f32[8,32,1024]{2,1,0:T(8,128)S(1)} %shard_map.80.refs_1_), custom_call_target="tpu_custom_call" | custom-call | tf_op jit(solution)/shard_map/pallas_call | solution.py:296
  79.3 0.7 maximum_select_fusion
  (34 shorter events, 1.5 us)
Async XLA Ops:
  0.6 25.2 %collective-permute-start.1 = (f32[256,1024]{1,0:T(8,128)}, f32[256,1024]{1,0:T(8,128)S(1)}, u32[]{:S(2)}, u32[]{:S(2)}) collective-permute-start(f32[256,1024]{1,0:T(8,128)} %bitcast.10), channel_id=1, source_target_pairs={{0,2},{1,3},{2,0},{3,1},{4,6},{5,7},{6,4},{7,5},{8,10},{9,11},{10,... | collective-permute-start | bytes 3145736 | tf_op jit(solution)/shard_map/ppermute | solution.py:353
  2.8 25.1 %collective-permute-start.4 = (f32[256,1024]{1,0:T(8,128)}, f32[256,1024]{1,0:T(8,128)S(1)}, u32[]{:S(2)}, u32[]{:S(2)}) collective-permute-start(f32[256,1024]{1,0:T(8,128)} %bitcast.11), channel_id=1, source_target_pairs={{4,0},{5,1},{2,6},{3,7},{8,4},{9,5},{6,10},{7,11},{12,8},{13,9},{1... | collective-permute-start | bytes 3145736 | tf_op jit(solution)/shard_map/ppermute | solution.py:379
  6.1 0.7 copy-start.3
  6.1 0.7 copy-start.4
  6.8 3.0 %copy-start.2 = (f32[2,2,128,128]{3,2,1,0:T(8,128)S(1)}, f32[2,2,128,128]{3,2,1,0:T(8,128)}, u32[]{:S(2)}) copy-start(f32[2,2,128,128]{3,2,1,0:T(8,128)} %refs_1_.1) | copy-start | bytes 786436
  7.8 22.0 %collective-permute-start = (f32[520,128]{1,0:T(8,128)S(1)}, f32[520,128]{1,0:T(8,128)S(1)}, u32[]{:S(2)}, u32[]{:S(2)}) collective-permute-start(f32[520,128]{1,0:T(8,128)S(1)} %select_maximum_fusion), channel_id=1, source_target_pairs={{0,0},{1,1},{2,6},{3,7},{4,4},{5,5},{6,10},{7,11},{8,8},{9,9},{10,... | collective-permute-start | bytes 798728 | tf_op jit(solution)/shard_map/ppermute | solution.py:379
  8.5 21.3 %collective-permute-start.2 = (f32[256,1024]{1,0:T(8,128)}, f32[256,1024]{1,0:T(8,128)S(1)}, u32[]{:S(2)}, u32[]{:S(2)}) collective-permute-start(f32[256,1024]{1,0:T(8,128)} %bitcast.12), channel_id=1, source_target_pairs={{0,1},{1,0},{2,3},{3,2},{4,5},{5,4},{6,7},{7,6},{8,9},{9,8},{10,11... | collective-permute-start | bytes 3145736 | tf_op jit(solution)/shard_map/ppermute | solution.py:353
  9.8 1.2 %copy-start = (f32[4,2,32,1024]{3,2,1,0:T(8,128)S(1)}, f32[4,2,32,1024]{3,2,1,0:T(8,128)}, u32[]{:S(2)}) copy-start(f32[4,2,32,1024]{3,2,1,0:T(8,128)} %param.6) | copy-start | bytes 3145732
  11.0 1.2 %copy-start.1 = (bf16[4,2,256,256]{3,2,1,0:T(8,128)(2,1)S(1)}, bf16[4,2,256,256]{3,2,1,0:T(8,128)(2,1)}, u32[]{:S(2)}) copy-start(bf16[4,2,256,256]{3,2,1,0:T(8,128)(2,1)} %constant.22.clone.refs_2_) | copy-start | bytes 3145732
  25.9 3.9 %collective-permute-start.3 = (f32[256,1024]{1,0:T(8,128)S(1)}, f32[256,1024]{1,0:T(8,128)S(1)}, u32[]{:S(2)}, u32[]{:S(2)}) collective-permute-start(f32[256,1024]{1,0:T(8,128)S(1)} %collective-permute-done.1.refs_6_), channel_id=1, source_target_pairs={{0,1},{1,0},{2,3},{3,2},{4,5},{5,4},{6,7},{7,6},{8,9},{9,8},{10,11... | collective-permute-start | bytes 3145736 | tf_op jit(solution)/shard_map/ppermute | solution.py:353
  27.9 4.2 %collective-permute-start.5 = (f32[256,1024]{1,0:T(8,128)S(1)}, f32[256,1024]{1,0:T(8,128)S(1)}, u32[]{:S(2)}, u32[]{:S(2)}) collective-permute-start(f32[256,1024]{1,0:T(8,128)S(1)} %collective-permute-done.4.refs_8_), channel_id=1, source_target_pairs={{0,1},{1,0},{2,3},{3,2},{4,5},{5,4},{6,7},{7,6},{8,9},{9,8},{10,11... | collective-permute-start | bytes 3145736 | tf_op jit(solution)/shard_map/ppermute | solution.py:353
  42.2 7.9 %collective-permute-start.6 = (f32[512,128]{1,0:T(8,128)S(1)}, f32[512,128]{1,0:T(8,128)S(1)}, u32[]{:S(2)}, u32[]{:S(2)}) collective-permute-start(f32[512,128]{1,0:T(8,128)S(1)} %get-tuple-element.36), channel_id=1, source_target_pairs={{0,2},{1,3},{2,0},{3,1},{4,6},{5,7},{6,4},{7,5},{8,10},{9,11},{10,... | collective-permute-start | bytes 786440 | tf_op jit(solution)/shard_map/ppermute | solution.py:353
  45.0 20.0 %collective-permute-start.10 = (f32[1032,128]{1,0:T(8,128)S(1)}, f32[1032,128]{1,0:T(8,128)S(1)}, u32[]{:S(2)}, u32[]{:S(2)}) collective-permute-start(f32[1032,128]{1,0:T(8,128)S(1)} %get-tuple-element.41), channel_id=1, source_target_pairs={{0,2},{1,3},{6,4},{7,5},{4,6},{5,7},{10,8},{11,9},{8,10},{9,11},{1... | collective-permute-start | bytes 1585160 | tf_op jit(solution)/shard_map/ppermute | solution.py:379
  45.1 20.0 %collective-permute-start.9 = (f32[1032,128]{1,0:T(8,128)S(1)}, f32[1032,128]{1,0:T(8,128)S(1)}, u32[]{:S(2)}, u32[]{:S(2)}) collective-permute-start(f32[1032,128]{1,0:T(8,128)S(1)} %get-tuple-element.40), channel_id=1, source_target_pairs={{0,4},{1,5},{6,2},{7,3},{4,8},{5,9},{10,6},{11,7},{8,12},{9,13},{1... | collective-permute-start | bytes 1585160 | tf_op jit(solution)/shard_map/ppermute | solution.py:379
  50.1 5.8 %collective-permute-start.7 = (f32[256,128]{1,0:T(8,128)S(1)}, f32[256,128]{1,0:T(8,128)S(1)}, u32[]{:S(2)}, u32[]{:S(2)}) collective-permute-start(f32[256,128]{1,0:T(8,128)S(1)} %slice_select_fusion), channel_id=1, source_target_pairs={{0,1},{1,0},{2,3},{3,2},{4,5},{5,4},{6,7},{7,6},{8,9},{9,8},{10,11... | collective-permute-start | bytes 393224 | tf_op jit(solution)/shard_map/ppermute | solution.py:353
  54.2 20.7 %collective-permute-start.12 = (f32[1032,128]{1,0:T(8,128)S(1)}, f32[1032,128]{1,0:T(8,128)S(1)}, u32[]{:S(2)}, u32[]{:S(2)}) collective-permute-start(f32[1032,128]{1,0:T(8,128)S(1)} %get-tuple-element.46), channel_id=1, source_target_pairs={{0,3},{1,2},{6,5},{7,4},{4,7},{5,6},{10,9},{11,8},{8,11},{9,10},{1... | collective-permute-start | bytes 1585160 | tf_op jit(solution)/shard_map/ppermute | solution.py:379
  56.0 9.0 %collective-permute-start.8 = (f32[256,128]{1,0:T(8,128)S(1)}, f32[256,128]{1,0:T(8,128)S(1)}, u32[]{:S(2)}, u32[]{:S(2)}) collective-permute-start(f32[256,128]{1,0:T(8,128)S(1)} %select_add_fusion), channel_id=1, source_target_pairs={{0,4},{1,5},{2,6},{3,7},{4,0},{5,1},{6,2},{7,3},{8,12},{9,13},{10,... | collective-permute-start | bytes 393224 | tf_op jit(solution)/shard_map/ppermute | solution.py:353
  56.0 20.8 %collective-permute-start.13 = (f32[1032,128]{1,0:T(8,128)S(1)}, f32[1032,128]{1,0:T(8,128)S(1)}, u32[]{:S(2)}, u32[]{:S(2)}) collective-permute-start(f32[1032,128]{1,0:T(8,128)S(1)} %get-tuple-element.52), channel_id=1, source_target_pairs={{0,1},{1,4},{6,3},{7,6},{4,5},{5,8},{10,7},{11,10},{8,9},{9,12},{1... | collective-permute-start | bytes 1585160 | tf_op jit(solution)/shard_map/ppermute | solution.py:379
  65.0 9.9 %collective-permute-start.11 = (f32[256,128]{1,0:T(8,128)S(1)}, f32[256,128]{1,0:T(8,128)S(1)}, u32[]{:S(2)}, u32[]{:S(2)}) collective-permute-start(f32[256,128]{1,0:T(8,128)S(1)} %add.21), channel_id=1, source_target_pairs={{0,8},{1,9},{2,10},{3,11},{4,12},{5,13},{6,14},{7,15},{8,0},{9,1},... | collective-permute-start | bytes 393224 | tf_op jit(solution)/shard_map/ppermute | solution.py:353
  76.8 2.5 %collective-permute-start.14 = (f32[256,128]{1,0:T(8,128)S(1)}, f32[256,128]{1,0:T(8,128)S(1)}, u32[]{:S(2)}, u32[]{:S(2)}) collective-permute-start(f32[256,128]{1,0:T(8,128)S(1)} %add.22), channel_id=1, source_target_pairs={{0,1},{1,0},{2,3},{3,2},{4,5},{5,4},{6,7},{7,6},{8,9},{9,8},{10,11... | collective-permute-start | bytes 393224 | tf_op jit(solution)/shard_map/ppermute | solution.py:353
